TPU v7x, 768 devices: a whole 4x8x12 slice. The times are simulated.
768 devices in a mesh: orb: 96 (over y, x, z_lo), dom: 8 (over z_hi, core).
Axes of the slice: x: 4, y: 8, z: 12 (z_hi: 4, z_lo: 3; z = z_hi * 3 + z_lo), core: 2. Of those that a mesh axis runs over, the one named last changes fastest.
Arguments:
- orbitals: float32 [2, 96, 32, 96, 128], P(None, 'orb', 'dom'), may hold values from -20 to 20
- potential: float32 [32, 96, 128], P('dom'), may hold values from -1.5 to 0.5
- laser_field: float32 [3], replicated, may hold values from -0.1 to 0.1
- box_anchor: int32 [3, 128], replicated, may hold values from 0 to 120, as said below
- domain_atoms: int32 [8, 32], replicated, may hold values from -1 to 127, as said below
- projector: float32 [4, 512], replicated, may hold values from -0.25 to 0.25
- strength: float32 [4], replicated, may hold values from 4 to 16
Outputs:
- evolved: float32 [2, 96, 32, 96, 128], P(None, 'orb', 'dom')
- density: float32 [32, 96, 128], P('dom', 'orb')
- current: float32 [3, 32, 96, 128], P(None, 'dom', 'orb')
Inputs may be any that keep to these rules, and one draw needn't show every extreme that they name: `box_anchor`: column a holds atom a's box corner relative to its domain: the first entry is 0 to 0, the second 0 to 88, the third 0 to 120; some atom has all three at their largest. `domain_atoms`: every atom stands in exactly one row; a row's atoms come first and the rest of the row is -1; a row holds at most 32 atoms and some row exactly 32.
All inputs are finite; a program needn't handle non-finite values.
Results may differ from a plain program's by a relative error of at most 0.0001.
Values sent between devices are 32-bit elements; how exact they have to be, the bound alone decides.
No kernel may reach another device: no remote copies, remote signals or barrier semaphores. Data moves between devices by JAX's collectives and lax.ppermute only.
A program may use at most 64 MiB of HBM per device.

v0:
```python
import functools

import jax
import jax.numpy as jnp
from jax import lax
from jax.experimental import pallas as pl
from jax.experimental.pallas import tpu as pltpu
from jax.sharding import PartitionSpec as P

TERMS = 4
BOX = 8
PROJ = 4

spacing = 0.5
time_step = 0.05
second_taps = (-205.0 / 72.0, 8.0 / 5.0, -1.0 / 5.0, 8.0 / 315.0, -1.0 / 560.0)
first_taps = (0.0, 4.0 / 5.0, -1.0 / 5.0, 4.0 / 105.0, -1.0 / 280.0)
kinetic = tuple(-0.5 * tap / (spacing * spacing) for tap in second_taps)
slope = tuple(tap / spacing for tap in first_taps)

VMEM = pl.BlockSpec(memory_space=pltpu.VMEM)
SMEM = pl.BlockSpec(memory_space=pltpu.SMEM)


def f32(*shape):
    return jax.ShapeDtypeStruct(shape, jnp.float32)


def shifted(value, offset):
    cells = value.shape[-1]
    lane = lax.broadcasted_iota(jnp.int32, value.shape, value.ndim - 1)
    inside = (lane < cells - offset) if offset > 0 else (lane >= -offset)
    return jnp.where(inside, pltpu.roll(value, (-offset) % cells, value.ndim - 1), 0.0)


def fill_padded(padded, planes, rows, read):
    cells = padded.shape[-1]
    for b in range(planes):
        padded[b, 0:8, :] = jnp.zeros((8, cells), jnp.float32)
        padded[b, 8 + rows : 16 + rows, :] = jnp.zeros((8, cells), jnp.float32)
        padded[b, 8 : 8 + rows, :] = read(b)


def atom_of(atoms, anchor, row, slot):
    atom = jnp.maximum(atoms[row, slot], 0)
    return anchor[1, atom], anchor[2, atom]


def fold(vectors):
    row = lax.broadcasted_iota(jnp.int32, vectors[0].shape, 0)
    for step in (4, 2, 1):
        lower = (row & step) == 0
        merged = []
        for a, b in zip(vectors[:step], vectors[step:]):
            crossed = jnp.where(lower, b, a)
            if step == 4:
                partner = pltpu.roll(crossed, 4, 0)
            else:
                partner = jnp.where(lower, pltpu.roll(crossed, 8 - step, 0), pltpu.roll(crossed, step, 0))
            merged.append(jnp.where(lower, a, b) + partner)
        vectors = merged
    return vectors[0]


def partial_sums(planes, rows, slots, me, atoms, anchor, u, proj, sums):
    cells = u.shape[-1]
    behind = jnp.maximum(me - 1, 0)

    def two_slots(pair, carry):
        for side, row in ((0, me), (1, behind)):
            products = []
            for slot in (2 * pair, 2 * pair + 1):
                y0, z0 = atom_of(atoms, anchor, row, slot)
                shift = jnp.where(z0 == 0, 0, cells - z0)
                boxes = [pltpu.roll(u[pl.ds(i * rows + y0, BOX), :], shift, 1) for i in range(planes)]
                for p in range(PROJ):
                    first = p * BOX + side * planes
                    total = proj[first] * boxes[0]
                    for i in range(1, planes):
                        total = total + proj[first + i] * boxes[i]
                    products.append(total)
            at = pl.multiple_of(side * slots * PROJ + pair * 8, 8)
            sums[pl.ds(at, 8), :] = fold(products)
        return carry

    lax.fori_loop(0, slots // 2, two_slots, 0)
    size = slots * PROJ
    lines = [jnp.sum(sums[side * size : (side + 1) * size, :].T, axis=0, keepdims=True) for side in (0, 1)]
    return jnp.concatenate(lines + [jnp.zeros((6, size), jnp.float32)], axis=0)


def prepare_kernel(
    planes, rows, slots, domains, where, atoms, anchor, laser, strength, potential, projector, u,
    v, proj, weight, partial, sums,
):
    cells = v.shape[-1]
    me = where[0]
    behind = jnp.maximum(me - 1, 0)
    lane = lax.broadcasted_iota(jnp.int32, (8, cells), 1)
    for chunk in range(BOX**3 // cells):
        block = projector[:, chunk * cells : (chunk + 1) * cells]
        for part in range(cells // BOX):
            i, j = chunk * 2 + part // BOX, part % BOX
            moved = block if part == 0 else pltpu.roll(block, cells - part * BOX, 1)
            moved = jnp.where(lane[:PROJ] < BOX, moved, 0.0)
            for p in range(PROJ):
                proj[p * BOX + i, j : j + 1, :] = moved[p : p + 1]

    line = lax.broadcasted_iota(jnp.int32, (8, cells), 0)
    listed = jnp.zeros((8, cells), jnp.float32)
    for slot in range(slots):
        own = jnp.where(atoms[me, slot] >= 0, 1.0, 0.0)
        before = jnp.where((atoms[behind, slot] >= 0) & (me > 0), 1.0, 0.0)
        here = (lane // PROJ) == slot
        listed = jnp.where(here & (line == 0), own, jnp.where(here & (line == 1), before, listed))
    strengths = jnp.zeros((8, cells), jnp.float32)
    for p in range(PROJ):
        strengths = jnp.where((lane % PROJ) == p, strength[p], strengths)
    weight[...] = listed * strengths

    y = lax.broadcasted_iota(jnp.int32, (rows, cells), 0).astype(jnp.float32)
    z = lax.broadcasted_iota(jnp.int32, (rows, cells), 1).astype(jnp.float32)
    along = laser[1] * ((y - (rows - 1) / 2.0) * spacing) + laser[2] * ((z - (cells - 1) / 2.0) * spacing)
    for i in range(planes):
        x = ((me * planes + i).astype(jnp.float32) - (domains * planes - 1) / 2.0) * spacing
        v[i] = potential[i] + laser[0] * x + along + 3.0 * kinetic[0]

    for ch in range(2):
        partial[8 * ch : 8 * ch + 8, :] = partial_sums(
            planes, rows, slots, me, atoms, anchor, u.at[ch], proj, sums
        )


def step_kernel(planes, rows, slots, factor, first, last, scale, *refs):
    refs = list(refs)
    where, atoms, anchor, u, before, after = refs[:6]
    refs = refs[6:]
    size = planes * rows
    if first is not None:
        partials = [ref.at[8 * first : 8 * first + 8] for ref in refs[:3]]
        refs = refs[3:]
    else:
        partials = [ref.at[size : size + 8] for ref in (u, before, after)]
    v, weight, proj, evolved = refs[:4]
    refs = refs[4:]
    if last == "both":
        other, result, density, acc, padded, spread, sums = refs
    elif last:
        result, acc, padded, spread, sums = refs
    else:
        message, result, acc, padded, spread, sums = refs
    cells = v.shape[-1]
    me = where[0]
    behind = jnp.maximum(me - 1, 0)

    def plane_of(ref, i):
        return ref[i * rows : (i + 1) * rows, :]

    fill_padded(padded, planes, rows, lambda i: plane_of(u, i))
    for i in range(planes):
        centre = plane_of(u, i)
        total = v[i] * centre
        for m in (1, 2, 3, 4):
            near = padded[i, 8 + m : 8 + m + rows, :] + padded[i, 8 - m : 8 - m + rows, :]
            near = near + shifted(centre, m) + shifted(centre, -m)
            near = near + (plane_of(u, i + m) if i + m < planes else plane_of(after, i + m - planes))
            near = near + (plane_of(u, i - m) if i >= m else plane_of(before, i - m + planes))
            total = total + kinetic[m] * near
        acc[i * rows : (i + 1) * rows, :] = total

    mine, ahead, back = [ref[...] for ref in partials[:1] + partials[2:] + partials[1:2]]
    for side, got in ((0, ahead[1:2]), (1, back[0:1])):
        line = (mine[side : side + 1] + got) * weight[side : side + 1, :]
        spread[side * cells : (side + 1) * cells, :] = jnp.broadcast_to(line, (cells, cells)).T

    def two_slots(pair, carry):
        for slot in (2 * pair, 2 * pair + 1):
            for side, row in ((0, me), (1, behind)):
                y0, z0 = atom_of(atoms, anchor, row, slot)
                at = side * slots * PROJ + slot * PROJ
                lines = [
                    jnp.broadcast_to(spread[pl.ds(at + p, 1), :], (BOX, cells)) for p in range(PROJ)
                ]
                for i in range(planes):
                    delta = lines[0] * proj[side * planes + i]
                    for p in range(1, PROJ):
                        delta = delta + lines[p] * proj[p * BOX + side * planes + i]
                    at_row = pl.ds(i * rows + y0, BOX)
                    acc[at_row, :] = acc[at_row, :] + pltpu.roll(delta, z0, 1)
        return carry

    lax.fori_loop(0, slots // 2, two_slots, 0)
    for i in range(planes):
        span = slice(i * rows, (i + 1) * rows)
        new = factor * acc[span, :]
        total = evolved[span, :] + new
        if last == "both":
            held = other[span, :]
            result[0, span, :] = held
            result[1, span, :] = total
            density[i] = scale * (held * held + total * total)
        else:
            result[span, :] = total
        if not last:
            message[span, :] = new
    if not last:
        message[size : size + 8, :] = partial_sums(planes, rows, slots, me, atoms, anchor, message, proj, sums)


def current_kernel(planes, rows, scale, u, real_before, real_after, imag_before, imag_after, flow, padded):
    cells = u.shape[-1]
    halos = ((real_before, real_after), (imag_before, imag_after))
    for ch in range(2):
        fill_padded(padded.at[ch], planes, rows, lambda i, ch=ch: u[ch, i * rows : (i + 1) * rows, :])

    def plane_of(ref, i):
        return ref[i * rows : (i + 1) * rows, :]

    for i in range(planes):
        gradients = []
        for ch in range(2):
            own, (before, after) = u.at[ch], halos[ch]
            centre = plane_of(own, i)
            along_x = along_y = along_z = 0.0
            for m in (1, 2, 3, 4):
                upper = plane_of(own, i + m) if i + m < planes else plane_of(after, i + m - planes)
                lower = plane_of(own, i - m) if i >= m else plane_of(before, i - m + planes)
                along_x = along_x + slope[m] * (upper - lower)
                along_y = along_y + slope[m] * (
                    padded[ch, i, 8 + m : 8 + m + rows, :] - padded[ch, i, 8 - m : 8 - m + rows, :]
                )
                along_z = along_z + slope[m] * (shifted(centre, m) - shifted(centre, -m))
            gradients.append((along_x, along_y, along_z))
        for c in range(3):
            flow[c * planes + i] = scale * (
                plane_of(u.at[0], i) * gradients[1][c] - plane_of(u.at[1], i) * gradients[0][c]
            )


def body(orbitals, potential, laser_field, box_anchor, domain_atoms, projector, strength):
    planes, rows, cells = orbitals.shape[2:]
    size = planes * rows
    domains = lax.axis_size("dom")
    orbs = lax.axis_size("orb")
    slots = domain_atoms.shape[1]
    me = lax.axis_index("dom")
    where = me.reshape(1).astype(jnp.int32)
    places = (where, domain_atoms, box_anchor)
    scale = 2.0 / orbs
    params = pltpu.CompilerParams(vmem_limit_bytes=32 * 1024 * 1024)

    up = [(i, i + 1) for i in range(domains - 1)]
    down = [(j, i) for i, j in up]

    def exchange(value):
        return lax.ppermute(value, "dom", up), lax.ppermute(value, "dom", down)

    u = orbitals.reshape(2, size, cells)
    start = [u[0], u[1]]
    halos = [exchange(start[0])]
    sums = pltpu.VMEM((2 * slots * PROJ, cells), jnp.float32)
    v, proj, weight, partial = pl.pallas_call(
        functools.partial(prepare_kernel, planes, rows, slots, domains),
        out_shape=(f32(planes, rows, cells), f32(PROJ * BOX, BOX, cells), f32(8, cells), f32(16, cells)),
        in_specs=[SMEM] * 5 + [VMEM] * 3,
        out_specs=(VMEM,) * 4,
        scratch_shapes=[sums],
        compiler_params=params,
        cost_estimate=pl.CostEstimate(flops=8_000_000, bytes_accessed=10_000_000, transcendentals=0),
        name="prepare_part",
    )(*places, laser_field, strength, potential, projector, u)
    partial_halos = exchange(partial)
    later, partial = lax.optimization_barrier((start[1], partial))
    halos.append(exchange(later))

    def step(order, channel, operands, evolved, other=None):
        factor = time_step / order * (1.0 if (channel + order) % 2 == 0 else -1.0)
        last = False if order < TERMS else ("both" if other is not None else True)
        out = (f32(size, cells),)
        if not last:
            out = (f32(size + 8, cells),) + out
        if last == "both":
            out = (f32(2, size, cells), f32(planes, rows, cells))
        extra = () if other is None else (other,)
        count = len(operands) + 4 + len(extra)
        return pl.pallas_call(
            functools.partial(
                step_kernel, planes, rows, slots, factor, channel if order == 1 else None, last, scale
            ),
            out_shape=out,
            in_specs=[SMEM] * 3 + [VMEM] * count,
            out_specs=(VMEM,) * len(out),
            scratch_shapes=[
                pltpu.VMEM((size, cells), jnp.float32),
                pltpu.VMEM((planes, rows + 16, cells), jnp.float32),
                pltpu.VMEM((2 * slots * PROJ, cells), jnp.float32),
                sums,
            ],
            compiler_params=params,
            cost_estimate=pl.CostEstimate(flops=8_000_000, bytes_accessed=10_000_000, transcendentals=0),
            name="taylor_step",
        )(*places, *operands, v, weight, proj, evolved, *extra)

    totals = [start[0], start[1]]
    held = list(start)
    for order in range(1, TERMS + 1):
        for channel in (0, 1):
            to = (channel + order) % 2
            operands = (held[channel], *halos[channel])
            if order == 1:
                operands += (partial, *partial_halos)
            if order < TERMS:
                held[channel], totals[to] = step(order, channel, operands, totals[to])
            elif channel == 0:
                (totals[to],) = step(order, channel, operands, totals[to])
            else:
                evolved, density = step(order, channel, operands, totals[to], totals[1 - to])
        if order == 1:
            flow = pl.pallas_call(
                functools.partial(current_kernel, planes, rows, scale),
                out_shape=f32(3 * planes, rows, cells),
                in_specs=[VMEM] * 5,
                out_specs=VMEM,
                scratch_shapes=[pltpu.VMEM((2, planes, rows + 16, cells), jnp.float32)],
                compiler_params=params,
                cost_estimate=pl.CostEstimate(flops=8_000_000, bytes_accessed=5_000_000, transcendentals=0),
                name="current_part",
            )(u, *halos[0], *halos[1])
        if order < TERMS:
            halos = [exchange(held[channel]) for channel in (0, 1)]

    fields = jnp.concatenate([density, flow], axis=0)
    fields = jnp.moveaxis(fields, 1, 0)
    fields = lax.all_to_all(fields, "orb", 0, 0, tiled=True)
    fields = jnp.sum(fields, axis=0).reshape(4, planes, 1, cells)
    return evolved.reshape(orbitals.shape), fields[0], fields[1:]


def solution(mesh):
    in_specs = (P(None, "orb", "dom", None, None), P("dom", None, None), P(), P(), P(), P(), P())
    out_specs = (
        P(None, "orb", "dom", None, None),
        P("dom", "orb", None),
        P(None, "dom", "orb", None),
    )
    return jax.shard_map(body, mesh=mesh, in_specs=in_specs, out_specs=out_specs, check_vma=False)
```

profile of v0, /device:TPU:1, one launch (start us, length us, event | category | flops | bytes accessed | tf_op | source)
XLA Modules:
  0.0 163.7 jit_solution(13328986526959952537)
XLA Ops:
  0.6 0.0 copy-start
  0.6 0.0 copy-start.2
  0.7 0.0 copy-start.4
  0.7 1.1 fusion
  1.8 12.4 %collective-permute-start.7 = (f32[384,128]{1,0:T(8,128)S(1)}, f32[384,128]{1,0:T(8,128)S(1)}, u32[]{:S(2)}, u32[]{:S(2)}) collective-permute-start(f32[384,128]{1,0:T(8,128)S(1)} %bitcast.12), channel_id=1, source_target_pairs={{1,0},{2,1},{3,2},{4,3},{5,4},{6,5},{7,6},{9,8},{10,9},{11,10},{12... | collective-permute-start | bytes 589832 | tf_op jit(solution)/shard_map/ppermute | solution.py:256
  14.2 1.9 %collective-permute-start.6 = (f32[384,128]{1,0:T(8,128)S(1)}, f32[384,128]{1,0:T(8,128)S(1)}, u32[]{:S(2)}, u32[]{:S(2)}) collective-permute-start(f32[384,128]{1,0:T(8,128)S(1)} %bitcast.13), channel_id=1, source_target_pairs={{0,1},{1,2},{2,3},{3,4},{4,5},{5,6},{6,7},{8,9},{9,10},{10,11},{11... | collective-permute-start | bytes 589832 | tf_op jit(solution)/shard_map/ppermute | solution.py:256
  16.1 0.0 copy-start.1
  16.1 0.0 copy-start.3
  16.2 0.0 copy-start.5
  16.2 0.0 copy-start.6
  16.2 0.0 copy-done
  16.2 0.6 copy-done.1
  16.8 0.0 copy-done.3
  16.8 0.0 copy-done.6
  16.8 4.8 %prepare_part.1 = (f32[4,96,128]{2,1,0:T(8,128)S(1)}, f32[32,8,128]{2,1,0:T(8,128)S(1)}, f32[8,128]{1,0:T(8,128)S(1)}, f32[16,128]{1,0:T(8,128)S(1)}) custom-call(s32[1]{0:T(128)} %bitcast.where.refs_0_, s32[8,32]{1,0:T(8,128)S(1)} %copy-done.1, s32[3,128]{1,0:T(4,128)S(1)} %copy-done.3, f32[3]{0:T(128)S(1)} %copy-done.5, f32[4]{0:T(128)S(1)} %copy-done.6, ...), custom_call_target="tpu_custom_call" | custom-call | flops 8000000 | bytes 10000000 | tf_op jit(solution)/shard_map/prepare_part/pallas_call | solution.py:262
  21.6 2.4 %collective-permute-start.1 = (f32[384,128]{1,0:T(8,128)S(1)}, f32[384,128]{1,0:T(8,128)S(1)}, u32[]{:S(2)}, u32[]{:S(2)}) collective-permute-start(f32[384,128]{1,0:T(8,128)S(1)} %bitcast.16), channel_id=1, source_target_pairs={{1,0},{2,1},{3,2},{4,3},{5,4},{6,5},{7,6},{9,8},{10,9},{11,10},{12... | collective-permute-start | bytes 589832 | tf_op jit(solution)/shard_map/ppermute | solution.py:256
  24.0 4.9 %collective-permute-start = (f32[384,128]{1,0:T(8,128)S(1)}, f32[384,128]{1,0:T(8,128)S(1)}, u32[]{:S(2)}, u32[]{:S(2)}) collective-permute-start(f32[384,128]{1,0:T(8,128)S(1)} %bitcast.17), channel_id=1, source_target_pairs={{0,1},{1,2},{2,3},{3,4},{4,5},{5,6},{6,7},{8,9},{9,10},{10,11},{11... | collective-permute-start | bytes 589832 | tf_op jit(solution)/shard_map/ppermute | solution.py:256
  29.0 1.9 %collective-permute-start.3 = (f32[16,128]{1,0:T(8,128)S(1)}, f32[16,128]{1,0:T(8,128)S(1)}, u32[]{:S(2)}, u32[]{:S(2)}) collective-permute-start(f32[16,128]{1,0:T(8,128)S(1)} %get-tuple-element.25.refs_6_), channel_id=1, source_target_pairs={{1,0},{2,1},{3,2},{4,3},{5,4},{6,5},{7,6},{9,8},{10,9},{11,10},{12... | collective-permute-start | bytes 24584 | tf_op jit(solution)/shard_map/ppermute | solution.py:256
  30.9 4.9 %collective-permute-done.3.refs_8_ = f32[16,128]{1,0:T(8,128)S(1)} collective-permute-done((f32[16,128]{1,0:T(8,128)S(1)}, f32[16,128]{1,0:T(8,128)S(1)}, u32[]{:S(2)}, u32[]{:S(2)}) %collective-permute-start.3) | collective-permute-done | bytes 8224 | tf_op jit(solution)/shard_map/ppermute | solution.py:256
  35.8 2.8 %collective-permute-start.2 = (f32[16,128]{1,0:T(8,128)S(1)}, f32[16,128]{1,0:T(8,128)S(1)}, u32[]{:S(2)}, u32[]{:S(2)}) collective-permute-start(f32[16,128]{1,0:T(8,128)S(1)} %get-tuple-element.25.refs_6_), channel_id=1, source_target_pairs={{0,1},{1,2},{2,3},{3,4},{4,5},{5,6},{6,7},{8,9},{9,10},{10,11},{11... | collective-permute-start | bytes 24584 | tf_op jit(solution)/shard_map/ppermute | solution.py:256
  38.6 0.8 collective-permute-done.2.refs_7_
  39.3 0.0 collective-permute-done.7.refs_5_.real_after
  39.3 0.0 collective-permute-done.6.refs_4_.real_before
  39.3 4.8 %taylor_step.9 = (f32[392,128]{1,0:T(8,128)S(1)}, f32[384,128]{1,0:T(8,128)S(1)}) custom-call(s32[1]{0:T(128)} %bitcast.where.refs_0_, s32[8,32]{1,0:T(8,128)S(1)} %copy-done.1, s32[3,128]{1,0:T(4,128)S(1)} %copy-done.3, f32[384,128]{1,0:T(8,128)S(1)} %bitcast.14, f32[384,128]{1,0:T(8,128)S(1)} %collective-permute-done.6.refs_4_.real_before, ...), custom_call_target="tpu_custom_call" | custom-call | flops 8000000 | bytes 10000000 | tf_op jit(solution)/shard_map/taylor_step/pallas_call | solution.py:286
  44.1 1.9 %collective-permute-start.11 = (f32[392,128]{1,0:T(8,128)S(1)}, f32[392,128]{1,0:T(8,128)S(1)}, u32[]{:S(2)}, u32[]{:S(2)}) collective-permute-start(f32[392,128]{1,0:T(8,128)S(1)} %get-tuple-element.32.refs_3_), channel_id=1, source_target_pairs={{1,0},{2,1},{3,2},{4,3},{5,4},{6,5},{7,6},{9,8},{10,9},{11,10},{12... | collective-permute-start | bytes 602120 | tf_op jit(solution)/shard_map/ppermute | solution.py:256
  46.0 7.4 %collective-permute-start.10 = (f32[392,128]{1,0:T(8,128)S(1)}, f32[392,128]{1,0:T(8,128)S(1)}, u32[]{:S(2)}, u32[]{:S(2)}) collective-permute-start(f32[392,128]{1,0:T(8,128)S(1)} %get-tuple-element.32.refs_3_), channel_id=1, source_target_pairs={{0,1},{1,2},{2,3},{3,4},{4,5},{5,6},{6,7},{8,9},{9,10},{10,11},{11... | collective-permute-start | bytes 602120 | tf_op jit(solution)/shard_map/ppermute | solution.py:256
  53.4 0.0 collective-permute-done.1.refs_5_.imag_after
  53.4 0.0 collective-permute-done.refs_4_.imag_before
  53.4 4.8 %taylor_step.8 = (f32[392,128]{1,0:T(8,128)S(1)}, f32[384,128]{1,0:T(8,128)S(1)}) custom-call(s32[1]{0:T(128)} %bitcast.where.refs_0_, s32[8,32]{1,0:T(8,128)S(1)} %copy-done.1, s32[3,128]{1,0:T(4,128)S(1)} %copy-done.3, f32[384,128]{1,0:T(8,128)S(1)} %bitcast.19, f32[384,128]{1,0:T(8,128)S(1)} %collective-permute-done.refs_4_.imag_before, ...), custom_call_target="tpu_custom_call" | custom-call | flops 8000000 | bytes 10000000 | tf_op jit(solution)/shard_map/taylor_step/pallas_call | solution.py:286
  58.3 1.9 %collective-permute-start.5 = (f32[392,128]{1,0:T(8,128)S(1)}, f32[392,128]{1,0:T(8,128)S(1)}, u32[]{:S(2)}, u32[]{:S(2)}) collective-permute-start(f32[392,128]{1,0:T(8,128)S(1)} %get-tuple-element.29.refs_3_), channel_id=1, source_target_pairs={{1,0},{2,1},{3,2},{4,3},{5,4},{6,5},{7,6},{9,8},{10,9},{11,10},{12... | collective-permute-start | bytes 602120 | tf_op jit(solution)/shard_map/ppermute | solution.py:256
  60.2 5.4 %collective-permute-start.4 = (f32[392,128]{1,0:T(8,128)S(1)}, f32[392,128]{1,0:T(8,128)S(1)}, u32[]{:S(2)}, u32[]{:S(2)}) collective-permute-start(f32[392,128]{1,0:T(8,128)S(1)} %get-tuple-element.29.refs_3_), channel_id=1, source_target_pairs={{0,1},{1,2},{2,3},{3,4},{4,5},{5,6},{6,7},{8,9},{9,10},{10,11},{11... | collective-permute-start | bytes 602120 | tf_op jit(solution)/shard_map/ppermute | solution.py:256
  65.6 0.0 collective-permute-done.11.refs_5_
  65.6 0.0 collective-permute-done.10.refs_4_
  65.6 4.8 %taylor_step.11 = (f32[392,128]{1,0:T(8,128)S(1)}, f32[384,128]{1,0:T(8,128)S(1)}) custom-call(s32[1]{0:T(128)} %bitcast.where.refs_0_, s32[8,32]{1,0:T(8,128)S(1)} %copy-done.1, s32[3,128]{1,0:T(4,128)S(1)} %copy-done.3, f32[392,128]{1,0:T(8,128)S(1)} %get-tuple-element.32.refs_3_, f32[392,128]{1,0:T(8,128)S(1)} %collective-permute-done.10.refs_4_, ...), custom_call_target="tpu_custom_call" | custom-call | flops 8000000 | bytes 10000000 | tf_op jit(solution)/shard_map/taylor_step/pallas_call | solution.py:286
  70.5 1.9 %collective-permute-start.15 = (f32[392,128]{1,0:T(8,128)S(1)}, f32[392,128]{1,0:T(8,128)S(1)}, u32[]{:S(2)}, u32[]{:S(2)}) collective-permute-start(f32[392,128]{1,0:T(8,128)S(1)} %get-tuple-element.36.refs_3_), channel_id=1, source_target_pairs={{1,0},{2,1},{3,2},{4,3},{5,4},{6,5},{7,6},{9,8},{10,9},{11,10},{12... | collective-permute-start | bytes 602120 | tf_op jit(solution)/shard_map/ppermute | solution.py:256
  72.4 5.4 %collective-permute-start.14 = (f32[392,128]{1,0:T(8,128)S(1)}, f32[392,128]{1,0:T(8,128)S(1)}, u32[]{:S(2)}, u32[]{:S(2)}) collective-permute-start(f32[392,128]{1,0:T(8,128)S(1)} %get-tuple-element.36.refs_3_), channel_id=1, source_target_pairs={{0,1},{1,2},{2,3},{3,4},{4,5},{5,6},{6,7},{8,9},{9,10},{10,11},{11... | collective-permute-start | bytes 602120 | tf_op jit(solution)/shard_map/ppermute | solution.py:256
  77.8 0.0 collective-permute-done.5.refs_5_
  77.9 0.0 collective-permute-done.4.refs_4_
  77.9 4.8 %taylor_step.10 = (f32[392,128]{1,0:T(8,128)S(1)}, f32[384,128]{1,0:T(8,128)S(1)}) custom-call(s32[1]{0:T(128)} %bitcast.where.refs_0_, s32[8,32]{1,0:T(8,128)S(1)} %copy-done.1, s32[3,128]{1,0:T(4,128)S(1)} %copy-done.3, f32[392,128]{1,0:T(8,128)S(1)} %get-tuple-element.29.refs_3_, f32[392,128]{1,0:T(8,128)S(1)} %collective-permute-done.4.refs_4_, ...), custom_call_target="tpu_custom_call" | custom-call | flops 8000000 | bytes 10000000 | tf_op jit(solution)/shard_map/taylor_step/pallas_call | solution.py:286
  82.7 1.9 %collective-permute-start.9 = (f32[392,128]{1,0:T(8,128)S(1)}, f32[392,128]{1,0:T(8,128)S(1)}, u32[]{:S(2)}, u32[]{:S(2)}) collective-permute-start(f32[392,128]{1,0:T(8,128)S(1)} %get-tuple-element.31.refs_3_), channel_id=1, source_target_pairs={{1,0},{2,1},{3,2},{4,3},{5,4},{6,5},{7,6},{9,8},{10,9},{11,10},{12... | collective-permute-start | bytes 602120 | tf_op jit(solution)/shard_map/ppermute | solution.py:256
  84.6 5.4 %collective-permute-start.8 = (f32[392,128]{1,0:T(8,128)S(1)}, f32[392,128]{1,0:T(8,128)S(1)}, u32[]{:S(2)}, u32[]{:S(2)}) collective-permute-start(f32[392,128]{1,0:T(8,128)S(1)} %get-tuple-element.31.refs_3_), channel_id=1, source_target_pairs={{0,1},{1,2},{2,3},{3,4},{4,5},{5,6},{6,7},{8,9},{9,10},{10,11},{11... | collective-permute-start | bytes 602120 | tf_op jit(solution)/shard_map/ppermute | solution.py:256
  90.1 0.0 collective-permute-done.15.refs_5_
  90.1 0.0 collective-permute-done.14.refs_4_
  90.1 4.8 %taylor_step.13 = (f32[392,128]{1,0:T(8,128)S(1)}, f32[384,128]{1,0:T(8,128)S(1)}) custom-call(s32[1]{0:T(128)} %bitcast.where.refs_0_, s32[8,32]{1,0:T(8,128)S(1)} %copy-done.1, s32[3,128]{1,0:T(4,128)S(1)} %copy-done.3, f32[392,128]{1,0:T(8,128)S(1)} %get-tuple-element.36.refs_3_, f32[392,128]{1,0:T(8,128)S(1)} %collective-permute-done.14.refs_4_, ...), custom_call_target="tpu_custom_call" | custom-call | flops 8000000 | bytes 10000000 | tf_op jit(solution)/shard_map/taylor_step/pallas_call | solution.py:286
  94.9 1.9 %collective-permute-start.17 = (f32[392,128]{1,0:T(8,128)S(1)}, f32[392,128]{1,0:T(8,128)S(1)}, u32[]{:S(2)}, u32[]{:S(2)}) collective-permute-start(f32[392,128]{1,0:T(8,128)S(1)} %get-tuple-element.39.refs_3_), channel_id=1, source_target_pairs={{1,0},{2,1},{3,2},{4,3},{5,4},{6,5},{7,6},{9,8},{10,9},{11,10},{12... | collective-permute-start | bytes 602120 | tf_op jit(solution)/shard_map/ppermute | solution.py:256
  96.8 6.2 %collective-permute-start.16 = (f32[392,128]{1,0:T(8,128)S(1)}, f32[392,128]{1,0:T(8,128)S(1)}, u32[]{:S(2)}, u32[]{:S(2)}) collective-permute-start(f32[392,128]{1,0:T(8,128)S(1)} %get-tuple-element.39.refs_3_), channel_id=1, source_target_pairs={{0,1},{1,2},{2,3},{3,4},{4,5},{5,6},{6,7},{8,9},{9,10},{10,11},{11... | collective-permute-start | bytes 602120 | tf_op jit(solution)/shard_map/ppermute | solution.py:256
  103.0 0.0 collective-permute-done.9.refs_5_
  103.0 0.0 collective-permute-done.8.refs_4_
  103.0 4.8 %taylor_step.12 = (f32[392,128]{1,0:T(8,128)S(1)}, f32[384,128]{1,0:T(8,128)S(1)}) custom-call(s32[1]{0:T(128)} %bitcast.where.refs_0_, s32[8,32]{1,0:T(8,128)S(1)} %copy-done.1, s32[3,128]{1,0:T(4,128)S(1)} %copy-done.3, f32[392,128]{1,0:T(8,128)S(1)} %get-tuple-element.31.refs_3_, f32[392,128]{1,0:T(8,128)S(1)} %collective-permute-done.8.refs_4_, ...), custom_call_target="tpu_custom_call" | custom-call | flops 8000000 | bytes 10000000 | tf_op jit(solution)/shard_map/taylor_step/pallas_call | solution.py:286
  107.9 1.9 %collective-permute-start.13 = (f32[392,128]{1,0:T(8,128)S(1)}, f32[392,128]{1,0:T(8,128)S(1)}, u32[]{:S(2)}, u32[]{:S(2)}) collective-permute-start(f32[392,128]{1,0:T(8,128)S(1)} %get-tuple-element.35.refs_3_), channel_id=1, source_target_pairs={{1,0},{2,1},{3,2},{4,3},{5,4},{6,5},{7,6},{9,8},{10,9},{11,10},{12... | collective-permute-start | bytes 602120 | tf_op jit(solution)/shard_map/ppermute | solution.py:256
  109.8 6.7 %collective-permute-start.12 = (f32[392,128]{1,0:T(8,128)S(1)}, f32[392,128]{1,0:T(8,128)S(1)}, u32[]{:S(2)}, u32[]{:S(2)}) collective-permute-start(f32[392,128]{1,0:T(8,128)S(1)} %get-tuple-element.35.refs_3_), channel_id=1, source_target_pairs={{0,1},{1,2},{2,3},{3,4},{4,5},{5,6},{6,7},{8,9},{9,10},{10,11},{11... | collective-permute-start | bytes 602120 | tf_op jit(solution)/shard_map/ppermute | solution.py:256
  116.5 1.1 current_part.1
  117.6 0.0 collective-permute-done.17.refs_5_
  117.6 0.0 collective-permute-done.16.refs_4_
  117.6 2.8 %taylor_step.14.refs_10_ = f32[384,128]{1,0:T(8,128)S(1)} custom-call(s32[1]{0:T(128)} %bitcast.where.refs_0_, s32[8,32]{1,0:T(8,128)S(1)} %copy-done.1, s32[3,128]{1,0:T(4,128)S(1)} %copy-done.3, f32[392,128]{1,0:T(8,128)S(1)} %get-tuple-element.39.refs_3_, f32[392,128]{1,0:T(8,128)S(1)} %collective-permute-done.16.refs_4_, ...), custom_call_target="tpu_custom_call" | custom-call | flops 8000000 | bytes 10000000 | tf_op jit(solution)/shard_map/taylor_step/pallas_call | solution.py:286
  120.4 0.0 collective-permute-done.13.refs_5_
  120.5 0.0 collective-permute-done.12.refs_4_
  120.5 3.6 %taylor_step.15 = (f32[2,384,128]{2,1,0:T(8,128)}, f32[4,96,128]{2,1,0:T(8,128)S(1)}) custom-call(s32[1]{0:T(128)} %bitcast.where.refs_0_, s32[8,32]{1,0:T(8,128)S(1)} %copy-done.1, s32[3,128]{1,0:T(4,128)S(1)} %copy-done.3, f32[392,128]{1,0:T(8,128)S(1)} %get-tuple-element.35.refs_3_, f32[392,128]{1,0:T(8,128)S(1)} %collective-permute-done.12.refs_4_, ...), custom_call_target="tpu_custom_call" | custom-call | flops 8000000 | bytes 10000000 | tf_op jit(solution)/shard_map/taylor_step/pallas_call | solution.py:286
  124.1 0.1 maximum_bitcast_fusion
  124.1 0.5 copy.11
  124.6 37.8 %all_to_all.5 = f32[96,16,128]{2,1,0:T(8,128)S(1)} all-to-all(f32[96,16,128]{2,1,0:T(8,128)S(1)} %copy.11), channel_id=1, replica_groups=mesh['orb'=96,'dom'=8] {'orb'}, dimensions={0} | all-to-all | bytes 1572864 | tf_op jit(solution)/shard_map/all_to_all | solution.py:334
  162.4 0.1 reduce_sum.9
  162.5 0.6 slice.23
  163.1 0.6 slice.22
  (4 shorter events, 0.0 us)
Async XLA Ops:
  0.6 15.6 %copy-start = (f32[2,1,4,96,128]{4,3,2,1,0:T(8,128)S(1)}, f32[2,1,4,96,128]{4,3,2,1,0:T(8,128)}, u32[]{:S(2)}) copy-start(f32[2,1,4,96,128]{4,3,2,1,0:T(8,128)} %param.7) | copy-start | bytes 1179652
  0.6 15.6 %copy-start.2 = (f32[4,96,128]{2,1,0:T(8,128)S(1)}, f32[4,96,128]{2,1,0:T(8,128)}, u32[]{:S(2)}) copy-start(f32[4,96,128]{2,1,0:T(8,128)} %potential.1) | copy-start | bytes 589828
  0.7 15.6 %copy-start.4 = (f32[4,512]{1,0:T(4,128)S(1)}, f32[4,512]{1,0:T(4,128)}, u32[]{:S(2)}) copy-start(f32[4,512]{1,0:T(4,128)} %projector.1) | copy-start | bytes 24580
  1.8 37.6 %collective-permute-start.7 = (f32[384,128]{1,0:T(8,128)S(1)}, f32[384,128]{1,0:T(8,128)S(1)}, u32[]{:S(2)}, u32[]{:S(2)}) collective-permute-start(f32[384,128]{1,0:T(8,128)S(1)} %bitcast.12), channel_id=1, source_target_pairs={{1,0},{2,1},{3,2},{4,3},{5,4},{6,5},{7,6},{9,8},{10,9},{11,10},{12... | collective-permute-start | bytes 589832 | tf_op jit(solution)/shard_map/ppermute | solution.py:256
  14.2 25.1 %collective-permute-start.6 = (f32[384,128]{1,0:T(8,128)S(1)}, f32[384,128]{1,0:T(8,128)S(1)}, u32[]{:S(2)}, u32[]{:S(2)}) collective-permute-start(f32[384,128]{1,0:T(8,128)S(1)} %bitcast.13), channel_id=1, source_target_pairs={{0,1},{1,2},{2,3},{3,4},{4,5},{5,6},{6,7},{8,9},{9,10},{10,11},{11... | collective-permute-start | bytes 589832 | tf_op jit(solution)/shard_map/ppermute | solution.py:256
  16.1 0.7 copy-start.1
  16.1 0.7 copy-start.3
  16.2 0.7 copy-start.5
  16.2 0.7 copy-start.6
  21.6 31.8 %collective-permute-start.1 = (f32[384,128]{1,0:T(8,128)S(1)}, f32[384,128]{1,0:T(8,128)S(1)}, u32[]{:S(2)}, u32[]{:S(2)}) collective-permute-start(f32[384,128]{1,0:T(8,128)S(1)} %bitcast.16), channel_id=1, source_target_pairs={{1,0},{2,1},{3,2},{4,3},{5,4},{6,5},{7,6},{9,8},{10,9},{11,10},{12... | collective-permute-start | bytes 589832 | tf_op jit(solution)/shard_map/ppermute | solution.py:256
  24.0 29.4 %collective-permute-start = (f32[384,128]{1,0:T(8,128)S(1)}, f32[384,128]{1,0:T(8,128)S(1)}, u32[]{:S(2)}, u32[]{:S(2)}) collective-permute-start(f32[384,128]{1,0:T(8,128)S(1)} %bitcast.17), channel_id=1, source_target_pairs={{0,1},{1,2},{2,3},{3,4},{4,5},{5,6},{6,7},{8,9},{9,10},{10,11},{11... | collective-permute-start | bytes 589832 | tf_op jit(solution)/shard_map/ppermute | solution.py:256
  29.0 6.8 %collective-permute-start.3 = (f32[16,128]{1,0:T(8,128)S(1)}, f32[16,128]{1,0:T(8,128)S(1)}, u32[]{:S(2)}, u32[]{:S(2)}) collective-permute-start(f32[16,128]{1,0:T(8,128)S(1)} %get-tuple-element.25.refs_6_), channel_id=1, source_target_pairs={{1,0},{2,1},{3,2},{4,3},{5,4},{6,5},{7,6},{9,8},{10,9},{11,10},{12... | collective-permute-start | bytes 24584 | tf_op jit(solution)/shard_map/ppermute | solution.py:256
  35.8 3.6 %collective-permute-start.2 = (f32[16,128]{1,0:T(8,128)S(1)}, f32[16,128]{1,0:T(8,128)S(1)}, u32[]{:S(2)}, u32[]{:S(2)}) collective-permute-start(f32[16,128]{1,0:T(8,128)S(1)} %get-tuple-element.25.refs_6_), channel_id=1, source_target_pairs={{0,1},{1,2},{2,3},{3,4},{4,5},{5,6},{6,7},{8,9},{9,10},{10,11},{11... | collective-permute-start | bytes 24584 | tf_op jit(solution)/shard_map/ppermute | solution.py:256
  44.1 21.5 %collective-permute-start.11 = (f32[392,128]{1,0:T(8,128)S(1)}, f32[392,128]{1,0:T(8,128)S(1)}, u32[]{:S(2)}, u32[]{:S(2)}) collective-permute-start(f32[392,128]{1,0:T(8,128)S(1)} %get-tuple-element.32.refs_3_), channel_id=1, source_target_pairs={{1,0},{2,1},{3,2},{4,3},{5,4},{6,5},{7,6},{9,8},{10,9},{11,10},{12... | collective-permute-start | bytes 602120 | tf_op jit(solution)/shard_map/ppermute | solution.py:256
  46.0 19.6 %collective-permute-start.10 = (f32[392,128]{1,0:T(8,128)S(1)}, f32[392,128]{1,0:T(8,128)S(1)}, u32[]{:S(2)}, u32[]{:S(2)}) collective-permute-start(f32[392,128]{1,0:T(8,128)S(1)} %get-tuple-element.32.refs_3_), channel_id=1, source_target_pairs={{0,1},{1,2},{2,3},{3,4},{4,5},{5,6},{6,7},{8,9},{9,10},{10,11},{11... | collective-permute-start | bytes 602120 | tf_op jit(solution)/shard_map/ppermute | solution.py:256
  58.3 19.6 %collective-permute-start.5 = (f32[392,128]{1,0:T(8,128)S(1)}, f32[392,128]{1,0:T(8,128)S(1)}, u32[]{:S(2)}, u32[]{:S(2)}) collective-permute-start(f32[392,128]{1,0:T(8,128)S(1)} %get-tuple-element.29.refs_3_), channel_id=1, source_target_pairs={{1,0},{2,1},{3,2},{4,3},{5,4},{6,5},{7,6},{9,8},{10,9},{11,10},{12... | collective-permute-start | bytes 602120 | tf_op jit(solution)/shard_map/ppermute | solution.py:256
  60.2 17.7 %collective-permute-start.4 = (f32[392,128]{1,0:T(8,128)S(1)}, f32[392,128]{1,0:T(8,128)S(1)}, u32[]{:S(2)}, u32[]{:S(2)}) collective-permute-start(f32[392,128]{1,0:T(8,128)S(1)} %get-tuple-element.29.refs_3_), channel_id=1, source_target_pairs={{0,1},{1,2},{2,3},{3,4},{4,5},{5,6},{6,7},{8,9},{9,10},{10,11},{11... | collective-permute-start | bytes 602120 | tf_op jit(solution)/shard_map/ppermute | solution.py:256
  70.5 19.6 %collective-permute-start.15 = (f32[392,128]{1,0:T(8,128)S(1)}, f32[392,128]{1,0:T(8,128)S(1)}, u32[]{:S(2)}, u32[]{:S(2)}) collective-permute-start(f32[392,128]{1,0:T(8,128)S(1)} %get-tuple-element.36.refs_3_), channel_id=1, source_target_pairs={{1,0},{2,1},{3,2},{4,3},{5,4},{6,5},{7,6},{9,8},{10,9},{11,10},{12... | collective-permute-start | bytes 602120 | tf_op jit(solution)/shard_map/ppermute | solution.py:256
  72.4 17.7 %collective-permute-start.14 = (f32[392,128]{1,0:T(8,128)S(1)}, f32[392,128]{1,0:T(8,128)S(1)}, u32[]{:S(2)}, u32[]{:S(2)}) collective-permute-start(f32[392,128]{1,0:T(8,128)S(1)} %get-tuple-element.36.refs_3_), channel_id=1, source_target_pairs={{0,1},{1,2},{2,3},{3,4},{4,5},{5,6},{6,7},{8,9},{9,10},{10,11},{11... | collective-permute-start | bytes 602120 | tf_op jit(solution)/shard_map/ppermute | solution.py:256
  82.7 20.3 %collective-permute-start.9 = (f32[392,128]{1,0:T(8,128)S(1)}, f32[392,128]{1,0:T(8,128)S(1)}, u32[]{:S(2)}, u32[]{:S(2)}) collective-permute-start(f32[392,128]{1,0:T(8,128)S(1)} %get-tuple-element.31.refs_3_), channel_id=1, source_target_pairs={{1,0},{2,1},{3,2},{4,3},{5,4},{6,5},{7,6},{9,8},{10,9},{11,10},{12... | collective-permute-start | bytes 602120 | tf_op jit(solution)/shard_map/ppermute | solution.py:256
  84.6 18.4 %collective-permute-start.8 = (f32[392,128]{1,0:T(8,128)S(1)}, f32[392,128]{1,0:T(8,128)S(1)}, u32[]{:S(2)}, u32[]{:S(2)}) collective-permute-start(f32[392,128]{1,0:T(8,128)S(1)} %get-tuple-element.31.refs_3_), channel_id=1, source_target_pairs={{0,1},{1,2},{2,3},{3,4},{4,5},{5,6},{6,7},{8,9},{9,10},{10,11},{11... | collective-permute-start | bytes 602120 | tf_op jit(solution)/shard_map/ppermute | solution.py:256
  94.9 22.7 %collective-permute-start.17 = (f32[392,128]{1,0:T(8,128)S(1)}, f32[392,128]{1,0:T(8,128)S(1)}, u32[]{:S(2)}, u32[]{:S(2)}) collective-permute-start(f32[392,128]{1,0:T(8,128)S(1)} %get-tuple-element.39.refs_3_), channel_id=1, source_target_pairs={{1,0},{2,1},{3,2},{4,3},{5,4},{6,5},{7,6},{9,8},{10,9},{11,10},{12... | collective-permute-start | bytes 602120 | tf_op jit(solution)/shard_map/ppermute | solution.py:256
  96.8 20.7 %collective-permute-start.16 = (f32[392,128]{1,0:T(8,128)S(1)}, f32[392,128]{1,0:T(8,128)S(1)}, u32[]{:S(2)}, u32[]{:S(2)}) collective-permute-start(f32[392,128]{1,0:T(8,128)S(1)} %get-tuple-element.39.refs_3_), channel_id=1, source_target_pairs={{0,1},{1,2},{2,3},{3,4},{4,5},{5,6},{6,7},{8,9},{9,10},{10,11},{11... | collective-permute-start | bytes 602120 | tf_op jit(solution)/shard_map/ppermute | solution.py:256
  107.9 12.6 %collective-permute-start.13 = (f32[392,128]{1,0:T(8,128)S(1)}, f32[392,128]{1,0:T(8,128)S(1)}, u32[]{:S(2)}, u32[]{:S(2)}) collective-permute-start(f32[392,128]{1,0:T(8,128)S(1)} %get-tuple-element.35.refs_3_), channel_id=1, source_target_pairs={{1,0},{2,1},{3,2},{4,3},{5,4},{6,5},{7,6},{9,8},{10,9},{11,10},{12... | collective-permute-start | bytes 602120 | tf_op jit(solution)/shard_map/ppermute | solution.py:256
  109.8 10.7 %collective-permute-start.12 = (f32[392,128]{1,0:T(8,128)S(1)}, f32[392,128]{1,0:T(8,128)S(1)}, u32[]{:S(2)}, u32[]{:S(2)}) collective-permute-start(f32[392,128]{1,0:T(8,128)S(1)} %get-tuple-element.35.refs_3_), channel_id=1, source_target_pairs={{0,1},{1,2},{2,3},{3,4},{4,5},{5,6},{6,7},{8,9},{9,10},{10,11},{11... | collective-permute-start | bytes 602120 | tf_op jit(solution)/shard_map/ppermute | solution.py:256
where the time goes:
time: 167 us; the launch traced here: 164 us
  starting transfers between devices  74.5 us (45%)
  Pallas kernels  41.1 us (25%)
  blocking collectives  37.8 us (23%)
  waiting for transfers between devices  5.68 us (3%)
  local copies, waits for them, and re-layouts  3.41 us (2%)
    ppermute x18, starting transfers between devices, exchange(): return (lax.ppermute(value, 'dom', up), lax.ppermute(value, 'dom', down))  74.5 us
    all_to_all x1, blocking collectives, body(): fields = lax.all_to_all(fields, 'orb', 0, 0, tiled=True)  37.8 us
    pallas_call x8, Pallas kernels, step(): pl.pallas_call(functools.partial(step_kernel, planes, rows, slots, factor...  35.3 us
    ppermute x18, waiting for transfers between devices, exchange(): return (lax.ppermute(value, 'dom', up), lax.ppermute(value, 'dom', down))  5.68 us
    pallas_call x1, Pallas kernels, body(): pl.pallas_call(functools.partial(prepare_kernel, planes, rows, slots, dom...  4.76 us
  transfers between devices with their start and end apart: 18, of which 2 were waited for; matrix products, arithmetic and copies ran while one was open for 0% of the time, Pallas kernels for 23%

commit v1 on v0

v1 whole, which is shorter than its diff:
```python
import functools

import jax
import jax.numpy as jnp
from jax import lax
from jax.experimental import pallas as pl
from jax.experimental.pallas import tpu as pltpu
from jax.sharding import PartitionSpec as P

TERMS = 4
BOX = 8
PROJ = 4
GROUP = 4

spacing = 0.5
time_step = 0.05
second_taps = (-205.0 / 72.0, 8.0 / 5.0, -1.0 / 5.0, 8.0 / 315.0, -1.0 / 560.0)
first_taps = (0.0, 4.0 / 5.0, -1.0 / 5.0, 4.0 / 105.0, -1.0 / 280.0)
kinetic = tuple(-0.5 * tap / (spacing * spacing) for tap in second_taps)
slope = tuple(tap / spacing for tap in first_taps)

VMEM = pl.BlockSpec(memory_space=pltpu.VMEM)
SMEM = pl.BlockSpec(memory_space=pltpu.SMEM)


def f32(*shape):
    return jax.ShapeDtypeStruct(shape, jnp.float32)


def shifted(value, offset):
    cells = value.shape[-1]
    lane = lax.broadcasted_iota(jnp.int32, value.shape, value.ndim - 1)
    inside = (lane < cells - offset) if offset > 0 else (lane >= -offset)
    return jnp.where(inside, pltpu.roll(value, (-offset) % cells, value.ndim - 1), 0.0)


def fill_padded(padded, planes, rows, read):
    cells = padded.shape[-1]
    for b in range(planes):
        padded[b, 0:8, :] = jnp.zeros((8, cells), jnp.float32)
        padded[b, 8 + rows : 16 + rows, :] = jnp.zeros((8, cells), jnp.float32)
        padded[b, 8 : 8 + rows, :] = read(b)


def atom_of(atoms, anchor, row, slot):
    atom = jnp.maximum(atoms[row, slot], 0)
    return anchor[1, atom], anchor[2, atom]


def fold(vectors):
    row = lax.broadcasted_iota(jnp.int32, vectors[0].shape, 0)
    for step in (4, 2, 1):
        lower = (row & step) == 0
        merged = []
        for a, b in zip(vectors[:step], vectors[step:]):
            crossed = jnp.where(lower, b, a)
            if step == 4:
                partner = pltpu.roll(crossed, 4, 0)
            else:
                partner = jnp.where(lower, pltpu.roll(crossed, 8 - step, 0), pltpu.roll(crossed, step, 0))
            merged.append(jnp.where(lower, a, b) + partner)
        vectors = merged
    return vectors[0]


def partial_sums(planes, rows, slots, me, atoms, anchor, u, proj, sums):
    cells = u.shape[-1]
    behind = jnp.maximum(me - 1, 0)

    def group(index, carry):
        stored = []
        for side, row in ((0, me), (1, behind)):
            for pair in range(GROUP // 2):
                products = []
                for slot in (index * GROUP + 2 * pair, index * GROUP + 2 * pair + 1):
                    y0, z0 = atom_of(atoms, anchor, row, slot)
                    shift = jnp.where(z0 == 0, 0, cells - z0)
                    boxes = [pltpu.roll(u[pl.ds(i * rows + y0, BOX), :], shift, 1) for i in range(planes)]
                    for p in range(PROJ):
                        first = p * BOX + side * planes
                        total = proj[first] * boxes[0]
                        for i in range(1, planes):
                            total = total + proj[first + i] * boxes[i]
                        products.append(total)
                at = side * slots * PROJ + index * GROUP * PROJ + 8 * pair
                stored.append((pl.multiple_of(at, 8), fold(products)))
        for at, value in stored:
            sums[pl.ds(at, 8), :] = value
        return carry

    lax.fori_loop(0, slots // GROUP, group, 0)
    size = slots * PROJ
    lines = [jnp.sum(sums[side * size : (side + 1) * size, :].T, axis=0, keepdims=True) for side in (0, 1)]
    return jnp.concatenate(lines + [jnp.zeros((6, size), jnp.float32)], axis=0)


def halo_weights(even, planes, taps, mirror):
    pair, other = {}, {}
    for i in range(planes):
        for j in range(planes):
            above = taps[planes + j - i] if j <= i else 0.0
            below = mirror * taps[planes + i - j] if i <= j else 0.0
            pair[i, j] = jnp.where(even, above, below)
            other[i, j] = jnp.where(even, below, above)
    return pair, other


def prepare_kernel(
    planes, rows, slots, where, atoms, anchor, strength, projector, u,
    proj, weight, message, sums,
):
    cells = u.shape[-1]
    size = planes * rows
    me = where[0]
    behind = jnp.maximum(me - 1, 0)
    lane = lax.broadcasted_iota(jnp.int32, (8, cells), 1)
    for chunk in range(BOX**3 // cells):
        block = projector[:, chunk * cells : (chunk + 1) * cells]
        for part in range(cells // BOX):
            i, j = chunk * (cells // BOX**2) + part // BOX, part % BOX
            moved = block if part == 0 else pltpu.roll(block, cells - part * BOX, 1)
            moved = jnp.where(lane[:PROJ] < BOX, moved, 0.0)
            for p in range(PROJ):
                proj[p * BOX + i, j : j + 1, :] = moved[p : p + 1]

    line = lax.broadcasted_iota(jnp.int32, (8, cells), 0)
    listed = jnp.zeros((8, cells), jnp.float32)
    for slot in range(slots):
        own = jnp.where(atoms[me, slot] >= 0, 1.0, 0.0)
        before = jnp.where((atoms[behind, slot] >= 0) & (me > 0), 1.0, 0.0)
        here = (lane // PROJ) == slot
        listed = jnp.where(here & (line == 0), own, jnp.where(here & (line == 1), before, listed))
    strengths = jnp.zeros((8, cells), jnp.float32)
    for p in range(PROJ):
        strengths = jnp.where((lane % PROJ) == p, strength[p], strengths)
    weight[...] = listed * strengths

    message[0:size, :] = u[0]
    message[size : size + 8, :] = partial_sums(planes, rows, slots, me, atoms, anchor, u.at[0], proj, sums)


def second_kernel(
    planes, rows, slots, domains, where, atoms, anchor, laser, potential, proj, u, v, message, sums
):
    cells = u.shape[-1]
    size = planes * rows
    me = where[0]
    message[0:size, :] = u[1]
    message[size : size + 8, :] = partial_sums(planes, rows, slots, me, atoms, anchor, u.at[1], proj, sums)
    y = lax.broadcasted_iota(jnp.int32, (rows, cells), 0).astype(jnp.float32)
    z = lax.broadcasted_iota(jnp.int32, (rows, cells), 1).astype(jnp.float32)
    along = laser[1] * ((y - (rows - 1) / 2.0) * spacing) + laser[2] * ((z - (cells - 1) / 2.0) * spacing)
    for i in range(planes):
        x = ((me * planes + i).astype(jnp.float32) - (domains * planes - 1) / 2.0) * spacing
        v[i] = potential[i] + laser[0] * x + along + 3.0 * kinetic[0]


def step_kernel(planes, rows, slots, factor, last, scale, *refs):
    where, atoms, anchor, u, pair_u, other_u, v, weight, proj, evolved, *refs = refs
    size = planes * rows
    if last == "both":
        held, result, density, acc, padded, spread, sums = refs
    elif last:
        result, acc, padded, spread, sums = refs
    else:
        message, result, acc, padded, spread, sums = refs
    cells = v.shape[-1]
    me = where[0]
    behind = jnp.maximum(me - 1, 0)
    even = lax.rem(me, 2) == 0
    pair_w, other_w = halo_weights(even, planes, kinetic, 1.0)

    def plane_of(ref, i):
        return ref[i * rows : (i + 1) * rows, :]

    fill_padded(padded, planes, rows, lambda i: plane_of(u, i))
    for i in range(planes):
        centre = plane_of(u, i)
        total = v[i] * centre
        for m in (1, 2, 3, 4):
            near = padded[i, 8 + m : 8 + m + rows, :] + padded[i, 8 - m : 8 - m + rows, :]
            near = near + shifted(centre, m) + shifted(centre, -m)
            if i + m < planes:
                near = near + plane_of(u, i + m)
            if i >= m:
                near = near + plane_of(u, i - m)
            total = total + kinetic[m] * near
        for j in range(planes):
            total = total + pair_w[i, j] * plane_of(pair_u, j) + other_w[i, j] * plane_of(other_u, j)
        acc[i * rows : (i + 1) * rows, :] = total

    mine, of_pair, of_other = (ref[size : size + 8, :] for ref in (u, pair_u, other_u))
    ahead = jnp.where(even, of_pair, of_other)
    back = jnp.where(even, of_other, of_pair)
    for side, got in ((0, ahead[1:2]), (1, back[0:1])):
        line = (mine[side : side + 1] + got) * weight[side : side + 1, :]
        spread[side * cells : (side + 1) * cells, :] = jnp.broadcast_to(line, (cells, cells)).T

    def group(index, carry):
        added = []
        for slot in [index * GROUP + k for k in range(GROUP)]:
            for side, row in ((0, me), (1, behind)):
                y0, z0 = atom_of(atoms, anchor, row, slot)
                at = side * slots * PROJ + slot * PROJ
                lines = [jnp.broadcast_to(spread[pl.ds(at + p, 1), :], (BOX, cells)) for p in range(PROJ)]
                for i in range(planes):
                    delta = lines[0] * proj[side * planes + i]
                    for p in range(1, PROJ):
                        delta = delta + lines[p] * proj[p * BOX + side * planes + i]
                    added.append((pl.ds(i * rows + y0, BOX), pltpu.roll(delta, z0, 1)))
        for at_rows, delta in added:
            acc[at_rows, :] = acc[at_rows, :] + delta
        return carry

    lax.fori_loop(0, slots // GROUP, group, 0)
    for i in range(planes):
        span = slice(i * rows, (i + 1) * rows)
        new = factor * acc[span, :]
        total = evolved[span, :] + new
        if last == "both":
            real = held[span, :]
            result[0, span, :] = real
            result[1, span, :] = total
            density[i] = scale * (real * real + total * total)
        else:
            result[span, :] = total
        if not last:
            message[span, :] = new
    if not last:
        message[size : size + 8, :] = partial_sums(planes, rows, slots, me, atoms, anchor, message, proj, sums)


def current_kernel(planes, rows, scale, where, u, real_pair, real_other, imag_pair, imag_other, flow, padded):
    halos = ((real_pair, real_other), (imag_pair, imag_other))
    pair_w, other_w = halo_weights(lax.rem(where[0], 2) == 0, planes, slope, -1.0)

    def plane_of(ref, i):
        return ref[i * rows : (i + 1) * rows, :]

    for ch in range(2):
        fill_padded(padded.at[ch], planes, rows, lambda i, ch=ch: plane_of(u.at[ch], i))
    for i in range(planes):
        gradients = []
        for ch in range(2):
            own, (pair, other) = u.at[ch], halos[ch]
            centre = plane_of(own, i)
            along_x = along_y = along_z = 0.0
            for m in (1, 2, 3, 4):
                if i + m < planes:
                    along_x = along_x + slope[m] * plane_of(own, i + m)
                if i >= m:
                    along_x = along_x - slope[m] * plane_of(own, i - m)
                along_y = along_y + slope[m] * (
                    padded[ch, i, 8 + m : 8 + m + rows, :] - padded[ch, i, 8 - m : 8 - m + rows, :]
                )
                along_z = along_z + slope[m] * (shifted(centre, m) - shifted(centre, -m))
            for j in range(planes):
                along_x = along_x + pair_w[i, j] * plane_of(pair, j) + other_w[i, j] * plane_of(other, j)
            gradients.append((along_x, along_y, along_z))
        for c in range(3):
            flow[c * planes + i] = scale * (
                plane_of(u.at[0], i) * gradients[1][c] - plane_of(u.at[1], i) * gradients[0][c]
            )


def gather_kernel(planes, got, density, current):
    total = got[0]
    for source in range(1, got.shape[0]):
        total = total + got[source]
    for i in range(planes):
        density[i] = total[i : i + 1]
        for c in range(3):
            current[c, i] = total[planes * (c + 1) + i : planes * (c + 1) + i + 1]


def body(orbitals, potential, laser_field, box_anchor, domain_atoms, projector, strength):
    planes, rows, cells = orbitals.shape[2:]
    size = planes * rows
    domains = lax.axis_size("dom")
    orbs = lax.axis_size("orb")
    slots = domain_atoms.shape[1]
    me = lax.axis_index("dom")
    where = me.reshape(1).astype(jnp.int32)
    places = (where, domain_atoms, box_anchor)
    scale = 2.0 / orbs

    pairs = [(i, i ^ 1) for i in range(domains)]
    others = [(i, i + 1) for i in range(1, domains - 1, 2)] + [(i + 1, i) for i in range(1, domains - 1, 2)]

    def exchange(value):
        other = lax.ppermute(value, "dom", others)
        return lax.ppermute(value, "dom", pairs), other

    def kernel(function, name, out, scalars, arrays, scratch):
        return pl.pallas_call(
            function,
            out_shape=out,
            in_specs=[SMEM] * scalars + [VMEM] * arrays,
            out_specs=jax.tree.map(lambda _: VMEM, out),
            scratch_shapes=scratch,
            compiler_params=pltpu.CompilerParams(vmem_limit_bytes=32 * 1024 * 1024),
            cost_estimate=pl.CostEstimate(flops=8_000_000, bytes_accessed=10_000_000, transcendentals=0),
            name=name,
        )

    sums = pltpu.VMEM((2 * slots * PROJ, cells), jnp.float32)
    u = orbitals.reshape(2, size, cells)
    proj, weight, first = kernel(
        functools.partial(prepare_kernel, planes, rows, slots),
        "prepare_real",
        (f32(PROJ * BOX, BOX, cells), f32(8, cells), f32(size + 8, cells)),
        4, 2, [sums],
    )(*places, strength, projector, u)
    v, second = kernel(
        functools.partial(second_kernel, planes, rows, slots, domains),
        "prepare_imag",
        (f32(planes, rows, cells), f32(size + 8, cells)),
        4, 3, [sums],
    )(*places, laser_field, potential, proj, u)

    def step(order, channel, halos, evolved, held=None):
        sign = 1.0 if (channel + order) % 2 == 0 else -1.0
        last = False if order < TERMS else ("both" if held is not None else True)
        out = (f32(size, cells),)
        if not last:
            out = (f32(size + 8, cells),) + out
        if last == "both":
            out = (f32(2, size, cells), f32(planes, rows, cells))
        extra = () if held is None else (held,)
        return kernel(
            functools.partial(step_kernel, planes, rows, slots, sign * time_step / order, last, scale),
            "taylor_step", out, 3, 7 + len(extra),
            [
                pltpu.VMEM((size, cells), jnp.float32),
                pltpu.VMEM((planes, rows + 16, cells), jnp.float32),
                pltpu.VMEM((2 * slots * PROJ, cells), jnp.float32),
                sums,
            ],
        )(*places, *halos, v, weight, proj, evolved, *extra)

    terms = [first, second]
    totals = [first, second]
    for order in range(1, TERMS + 1):
        halos = [(term, *exchange(term)) for term in terms]
        for channel in (0, 1):
            to = (channel + order) % 2
            if order < TERMS:
                terms[channel], totals[to] = step(order, channel, halos[channel], totals[to])
            elif channel == 0:
                (totals[to],) = step(order, channel, halos[channel], totals[to])
            else:
                evolved, density = step(order, channel, halos[channel], totals[to], totals[1 - to])
        if order == 1:
            flow = kernel(
                functools.partial(current_kernel, planes, rows, scale),
                "current_part", f32(3 * planes, rows, cells), 1, 5,
                [pltpu.VMEM((2, planes, rows + 16, cells), jnp.float32)],
            )(where, u, *halos[0][1:], *halos[1][1:])

    fields = jnp.concatenate([density, flow], axis=0)
    fields = jnp.moveaxis(fields, 1, 0)
    fields = lax.all_to_all(fields, "orb", 0, 0, tiled=True)
    density, current = kernel(
        functools.partial(gather_kernel, planes),
        "sum_over_orb", (f32(planes, 1, cells), f32(3, planes, 1, cells)), 0, 1, [],
    )(fields)
    return evolved.reshape(orbitals.shape), density, current


def solution(mesh):
    in_specs = (P(None, "orb", "dom", None, None), P("dom", None, None), P(), P(), P(), P(), P())
    out_specs = (
        P(None, "orb", "dom", None, None),
        P("dom", "orb", None),
        P(None, "dom", "orb", None),
    )
    return jax.shard_map(body, mesh=mesh, in_specs=in_specs, out_specs=out_specs, check_vma=False)
```

time: 167 us -> 136 us (0.81); the launches traced: 164 us -> 136 us
  starting transfers between devices: 74.5 us -> 59.6 us
  Pallas kernels: 41.1 us -> 33.9 us
  waiting for transfers between devices: 5.68 us -> 2.58 us
  blocking collectives: 37.8 us -> 35.5 us
    ppermute x18 -> x16, starting transfers between devices: 74.5 us -> 59.6 us  [the longest x8 42.1 us: exchange(): other = lax.ppermute(value, 'dom', others)]
    pallas_call x10 -> x12, Pallas kernels: 41.1 us -> 33.9 us  [the longest x8 27.8 us: step(): kernel(functools.partial(step_kernel, planes, rows, slots, sign * time_st...]
    ppermute x18 -> x16, waiting for transfers between devices: 5.68 us -> 2.58 us  [the longest x8 2.56 us: exchange(): other = lax.ppermute(value, 'dom', others)]
    slice x4 -> x0, local copies, waits for them, and re-layouts: 2.3 us -> none  [the longest x3 1.19 us: body(): return (evolved.reshape(orbitals.shape), fields[0], fields[1:])]
    all_to_all x1, blocking collectives: 37.8 us -> 35.5 us  [body(): fields = lax.all_to_all(fields, 'orb', 0, 0, tiled=True)]
    unnamed x14 -> x16, local copies, waits for them, and re-layouts: 0.65 us -> 2.38 us
  transfers between devices with their start and end apart: 18 -> 16, of which waited for: 2 -> 1; matrix products, arithmetic and copies ran while one was open for 0% -> 0% of each run, Pallas kernels for 23% -> 21%
where the time goes in v1:
time: 136 us
  starting transfers between devices  59.6 us (44%)
  blocking collectives  35.5 us (26%)
  Pallas kernels  33.9 us (25%)
  local copies, waits for them, and re-layouts  2.87 us (2%)
  waiting for transfers between devices  2.58 us (2%)
    ppermute x8, starting transfers between devices, exchange(): other = lax.ppermute(value, 'dom', others)  42.1 us
    all_to_all x1, blocking collectives, body(): fields = lax.all_to_all(fields, 'orb', 0, 0, tiled=True)  35.5 us
    pallas_call x8, Pallas kernels, step(): kernel(functools.partial(step_kernel, planes, rows, slots, sign * time_st...  27.8 us
    ppermute x8, starting transfers between devices, exchange(): return (lax.ppermute(value, 'dom', pairs), other)  17.5 us
  transfers between devices with their start and end apart: 16, of which 1 were waited for; matrix products, arithmetic and copies ran while one was open for 0% of the time, Pallas kernels for 21%

profile of v1, /device:TPU:1, one launch (start us, length us, event | category | flops | bytes accessed | tf_op | source)
XLA Modules:
  0.0 135.6 jit_solution(9625915555786114888)
XLA Ops:
  0.6 0.0 copy-start.2
  0.6 0.0 copy-start.3
  0.7 0.0 copy-start.6
  0.7 0.7 copy-done.2
  1.3 0.0 copy-done.3
  1.3 0.0 copy-done.6
  1.3 0.0 copy-start
  1.3 1.0 copy-done
  2.3 0.0 copy-start.5
  2.3 0.7 copy-done.5
  3.0 0.0 copy-start.4
  3.0 2.1 %prepare_real.1 = (f32[32,8,128]{2,1,0:T(8,128)S(1)}, f32[8,128]{1,0:T(8,128)S(1)}, f32[392,128]{1,0:T(8,128)S(1)}) custom-call(s32[1]{0:T(128)} %bitcast.where.refs_0_, s32[8,32]{1,0:T(8,128)S(1)} %copy-done.2, s32[3,128]{1,0:T(4,128)S(1)} %copy-done.3, f32[4]{0:T(128)S(1)} %copy-done.6, f32[4,512]{1,0:T(4,128)S(1)} %copy-done.5, f32[2,384,128]{2,1,0:T(8,128)S(1)} %bitcast.7), custom_call_target="tpu_custom_call" | custom-call | flops 8000000 | bytes 10000000 | tf_op jit(solution)/shard_map/prepare_real/pallas_call | solution.py:308
  5.2 0.0 copy-start.7
  5.2 9.0 %collective-permute-start.5 = (f32[392,128]{1,0:T(8,128)S(1)}, f32[392,128]{1,0:T(8,128)S(1)}, u32[]{:S(2)}, u32[]{:S(2)}) collective-permute-start(f32[392,128]{1,0:T(8,128)S(1)} %get-tuple-element.28.refs_9_.refs_3_), channel_id=1, source_target_pairs={{1,2},{3,4},{5,6},{2,1},{4,3},{6,5},{9,10},{11,12},{13,14},{10,9},... | collective-permute-start | bytes 602120 | tf_op jit(solution)/shard_map/ppermute | solution.py:291
  14.2 4.1 %collective-permute-start.4 = (f32[392,128]{1,0:T(8,128)S(1)}, f32[392,128]{1,0:T(8,128)S(1)}, u32[]{:S(2)}, u32[]{:S(2)}) collective-permute-start(f32[392,128]{1,0:T(8,128)S(1)} %get-tuple-element.28.refs_9_.refs_3_), channel_id=1, source_target_pairs={{0,1},{1,0},{2,3},{3,2},{4,5},{5,4},{6,7},{7,6},{8,9},{9,8},{10,11... | collective-permute-start | bytes 602120 | tf_op jit(solution)/shard_map/ppermute | solution.py:292
  18.3 0.0 copy-done.4
  18.3 0.0 copy-done.7
  18.3 2.0 %prepare_imag.1 = (f32[4,96,128]{2,1,0:T(8,128)S(1)}, f32[392,128]{1,0:T(8,128)S(1)}) custom-call(s32[1]{0:T(128)} %bitcast.where.refs_0_, s32[8,32]{1,0:T(8,128)S(1)} %copy-done.2, s32[3,128]{1,0:T(4,128)S(1)} %copy-done.3, f32[3]{0:T(128)S(1)} %copy-done.7, f32[4,96,128]{2,1,0:T(8,128)S(1)} %copy-done.4, f32[32,8,128]{2,1,0:T(8,128)S(1)} %get-tuple-element.24.proj.refs_8_, ...), custom_call_target="tpu_custom_call" | custom-call | flops 8000000 | bytes 10000000 | tf_op jit(solution)/shard_map/prepare_imag/pallas_call | solution.py:314
  20.4 7.0 %collective-permute-start.1 = (f32[392,128]{1,0:T(8,128)S(1)}, f32[392,128]{1,0:T(8,128)S(1)}, u32[]{:S(2)}, u32[]{:S(2)}) collective-permute-start(f32[392,128]{1,0:T(8,128)S(1)} %get-tuple-element.25.refs_3_.refs_9_), channel_id=1, source_target_pairs={{1,2},{3,4},{5,6},{2,1},{4,3},{6,5},{9,10},{11,12},{13,14},{10,9},... | collective-permute-start | bytes 602120 | tf_op jit(solution)/shard_map/ppermute | solution.py:291
  27.4 1.9 %collective-permute-start = (f32[392,128]{1,0:T(8,128)S(1)}, f32[392,128]{1,0:T(8,128)S(1)}, u32[]{:S(2)}, u32[]{:S(2)}) collective-permute-start(f32[392,128]{1,0:T(8,128)S(1)} %get-tuple-element.25.refs_3_.refs_9_), channel_id=1, source_target_pairs={{0,1},{1,0},{2,3},{3,2},{4,5},{5,4},{6,7},{7,6},{8,9},{9,8},{10,11... | collective-permute-start | bytes 602120 | tf_op jit(solution)/shard_map/ppermute | solution.py:292
  29.3 0.0 collective-permute-done.5.refs_5_.real_other
  29.3 0.0 collective-permute-done.4.refs_4_.real_pair
  29.4 3.7 %taylor_step.9 = (f32[392,128]{1,0:T(8,128)S(1)}, f32[384,128]{1,0:T(8,128)S(1)}) custom-call(s32[1]{0:T(128)} %bitcast.where.refs_0_, s32[8,32]{1,0:T(8,128)S(1)} %copy-done.2, s32[3,128]{1,0:T(4,128)S(1)} %copy-done.3, f32[392,128]{1,0:T(8,128)S(1)} %get-tuple-element.28.refs_9_.refs_3_, f32[392,128]{1,0:T(8,128)S(1)} %collective-permute-done.4.refs_4_.real_pair, ...), custom_call_target="tpu_custom_call" | custom-call | flops 8000000 | bytes 10000000 | tf_op jit(solution)/shard_map/taylor_step/pallas_call | solution.py:330
  33.1 5.9 %collective-permute-start.9 = (f32[392,128]{1,0:T(8,128)S(1)}, f32[392,128]{1,0:T(8,128)S(1)}, u32[]{:S(2)}, u32[]{:S(2)}) collective-permute-start(f32[392,128]{1,0:T(8,128)S(1)} %get-tuple-element.32.refs_3_), channel_id=1, source_target_pairs={{1,2},{3,4},{5,6},{2,1},{4,3},{6,5},{9,10},{11,12},{13,14},{10,9},... | collective-permute-start | bytes 602120 | tf_op jit(solution)/shard_map/ppermute | solution.py:291
  39.0 1.9 %collective-permute-start.8 = (f32[392,128]{1,0:T(8,128)S(1)}, f32[392,128]{1,0:T(8,128)S(1)}, u32[]{:S(2)}, u32[]{:S(2)}) collective-permute-start(f32[392,128]{1,0:T(8,128)S(1)} %get-tuple-element.32.refs_3_), channel_id=1, source_target_pairs={{0,1},{1,0},{2,3},{3,2},{4,5},{5,4},{6,7},{7,6},{8,9},{9,8},{10,11... | collective-permute-start | bytes 602120 | tf_op jit(solution)/shard_map/ppermute | solution.py:292
  41.0 0.0 collective-permute-done.1.refs_5_.imag_other
  41.0 0.0 collective-permute-done.refs_4_.imag_pair
  41.0 3.7 %taylor_step.8 = (f32[392,128]{1,0:T(8,128)S(1)}, f32[384,128]{1,0:T(8,128)S(1)}) custom-call(s32[1]{0:T(128)} %bitcast.where.refs_0_, s32[8,32]{1,0:T(8,128)S(1)} %copy-done.2, s32[3,128]{1,0:T(4,128)S(1)} %copy-done.3, f32[392,128]{1,0:T(8,128)S(1)} %get-tuple-element.25.refs_3_.refs_9_, f32[392,128]{1,0:T(8,128)S(1)} %collective-permute-done.refs_4_.imag_pair, ...), custom_call_target="tpu_custom_call" | custom-call | flops 8000000 | bytes 10000000 | tf_op jit(solution)/shard_map/taylor_step/pallas_call | solution.py:330
  44.7 2.6 %collective-permute-start.3 = (f32[392,128]{1,0:T(8,128)S(1)}, f32[392,128]{1,0:T(8,128)S(1)}, u32[]{:S(2)}, u32[]{:S(2)}) collective-permute-start(f32[392,128]{1,0:T(8,128)S(1)} %get-tuple-element.29.refs_3_), channel_id=1, source_target_pairs={{1,2},{3,4},{5,6},{2,1},{4,3},{6,5},{9,10},{11,12},{13,14},{10,9},... | collective-permute-start | bytes 602120 | tf_op jit(solution)/shard_map/ppermute | solution.py:291
  47.4 1.9 %collective-permute-start.2 = (f32[392,128]{1,0:T(8,128)S(1)}, f32[392,128]{1,0:T(8,128)S(1)}, u32[]{:S(2)}, u32[]{:S(2)}) collective-permute-start(f32[392,128]{1,0:T(8,128)S(1)} %get-tuple-element.29.refs_3_), channel_id=1, source_target_pairs={{0,1},{1,0},{2,3},{3,2},{4,5},{5,4},{6,7},{7,6},{8,9},{9,8},{10,11... | collective-permute-start | bytes 602120 | tf_op jit(solution)/shard_map/ppermute | solution.py:292
  49.3 0.0 collective-permute-done.9.refs_5_
  49.3 0.0 collective-permute-done.8.refs_4_
  49.3 3.7 %taylor_step.11 = (f32[392,128]{1,0:T(8,128)S(1)}, f32[384,128]{1,0:T(8,128)S(1)}) custom-call(s32[1]{0:T(128)} %bitcast.where.refs_0_, s32[8,32]{1,0:T(8,128)S(1)} %copy-done.2, s32[3,128]{1,0:T(4,128)S(1)} %copy-done.3, f32[392,128]{1,0:T(8,128)S(1)} %get-tuple-element.32.refs_3_, f32[392,128]{1,0:T(8,128)S(1)} %collective-permute-done.8.refs_4_, ...), custom_call_target="tpu_custom_call" | custom-call | flops 8000000 | bytes 10000000 | tf_op jit(solution)/shard_map/taylor_step/pallas_call | solution.py:330
  53.0 5.9 %collective-permute-start.13 = (f32[392,128]{1,0:T(8,128)S(1)}, f32[392,128]{1,0:T(8,128)S(1)}, u32[]{:S(2)}, u32[]{:S(2)}) collective-permute-start(f32[392,128]{1,0:T(8,128)S(1)} %get-tuple-element.36.refs_3_), channel_id=1, source_target_pairs={{1,2},{3,4},{5,6},{2,1},{4,3},{6,5},{9,10},{11,12},{13,14},{10,9},... | collective-permute-start | bytes 602120 | tf_op jit(solution)/shard_map/ppermute | solution.py:291
  58.9 1.9 %collective-permute-start.12 = (f32[392,128]{1,0:T(8,128)S(1)}, f32[392,128]{1,0:T(8,128)S(1)}, u32[]{:S(2)}, u32[]{:S(2)}) collective-permute-start(f32[392,128]{1,0:T(8,128)S(1)} %get-tuple-element.36.refs_3_), channel_id=1, source_target_pairs={{0,1},{1,0},{2,3},{3,2},{4,5},{5,4},{6,7},{7,6},{8,9},{9,8},{10,11... | collective-permute-start | bytes 602120 | tf_op jit(solution)/shard_map/ppermute | solution.py:292
  60.8 0.0 collective-permute-done.3.refs_5_
  60.9 0.0 collective-permute-done.2.refs_4_
  60.9 3.7 %taylor_step.10 = (f32[392,128]{1,0:T(8,128)S(1)}, f32[384,128]{1,0:T(8,128)S(1)}) custom-call(s32[1]{0:T(128)} %bitcast.where.refs_0_, s32[8,32]{1,0:T(8,128)S(1)} %copy-done.2, s32[3,128]{1,0:T(4,128)S(1)} %copy-done.3, f32[392,128]{1,0:T(8,128)S(1)} %get-tuple-element.29.refs_3_, f32[392,128]{1,0:T(8,128)S(1)} %collective-permute-done.2.refs_4_, ...), custom_call_target="tpu_custom_call" | custom-call | flops 8000000 | bytes 10000000 | tf_op jit(solution)/shard_map/taylor_step/pallas_call | solution.py:330
  64.6 3.1 %collective-permute-start.7 = (f32[392,128]{1,0:T(8,128)S(1)}, f32[392,128]{1,0:T(8,128)S(1)}, u32[]{:S(2)}, u32[]{:S(2)}) collective-permute-start(f32[392,128]{1,0:T(8,128)S(1)} %get-tuple-element.31.refs_3_), channel_id=1, source_target_pairs={{1,2},{3,4},{5,6},{2,1},{4,3},{6,5},{9,10},{11,12},{13,14},{10,9},... | collective-permute-start | bytes 602120 | tf_op jit(solution)/shard_map/ppermute | solution.py:291
  67.7 1.9 %collective-permute-start.6 = (f32[392,128]{1,0:T(8,128)S(1)}, f32[392,128]{1,0:T(8,128)S(1)}, u32[]{:S(2)}, u32[]{:S(2)}) collective-permute-start(f32[392,128]{1,0:T(8,128)S(1)} %get-tuple-element.31.refs_3_), channel_id=1, source_target_pairs={{0,1},{1,0},{2,3},{3,2},{4,5},{5,4},{6,7},{7,6},{8,9},{9,8},{10,11... | collective-permute-start | bytes 602120 | tf_op jit(solution)/shard_map/ppermute | solution.py:292
  69.6 0.0 collective-permute-done.13.refs_5_
  69.6 0.0 collective-permute-done.12.refs_4_
  69.7 3.7 %taylor_step.13 = (f32[392,128]{1,0:T(8,128)S(1)}, f32[384,128]{1,0:T(8,128)S(1)}) custom-call(s32[1]{0:T(128)} %bitcast.where.refs_0_, s32[8,32]{1,0:T(8,128)S(1)} %copy-done.2, s32[3,128]{1,0:T(4,128)S(1)} %copy-done.3, f32[392,128]{1,0:T(8,128)S(1)} %get-tuple-element.36.refs_3_, f32[392,128]{1,0:T(8,128)S(1)} %collective-permute-done.12.refs_4_, ...), custom_call_target="tpu_custom_call" | custom-call | flops 8000000 | bytes 10000000 | tf_op jit(solution)/shard_map/taylor_step/pallas_call | solution.py:330
  73.3 5.9 %collective-permute-start.15 = (f32[392,128]{1,0:T(8,128)S(1)}, f32[392,128]{1,0:T(8,128)S(1)}, u32[]{:S(2)}, u32[]{:S(2)}) collective-permute-start(f32[392,128]{1,0:T(8,128)S(1)} %get-tuple-element.39.refs_3_), channel_id=1, source_target_pairs={{1,2},{3,4},{5,6},{2,1},{4,3},{6,5},{9,10},{11,12},{13,14},{10,9},... | collective-permute-start | bytes 602120 | tf_op jit(solution)/shard_map/ppermute | solution.py:291
  79.2 1.9 %collective-permute-start.14 = (f32[392,128]{1,0:T(8,128)S(1)}, f32[392,128]{1,0:T(8,128)S(1)}, u32[]{:S(2)}, u32[]{:S(2)}) collective-permute-start(f32[392,128]{1,0:T(8,128)S(1)} %get-tuple-element.39.refs_3_), channel_id=1, source_target_pairs={{0,1},{1,0},{2,3},{3,2},{4,5},{5,4},{6,7},{7,6},{8,9},{9,8},{10,11... | collective-permute-start | bytes 602120 | tf_op jit(solution)/shard_map/ppermute | solution.py:292
  81.2 0.0 collective-permute-done.7.refs_5_
  81.2 0.0 collective-permute-done.6.refs_4_
  81.2 0.0 copy-start.1
  81.2 3.7 %taylor_step.12 = (f32[392,128]{1,0:T(8,128)S(1)}, f32[384,128]{1,0:T(8,128)S(1)}) custom-call(s32[1]{0:T(128)} %bitcast.where.refs_0_, s32[8,32]{1,0:T(8,128)S(1)} %copy-done.2, s32[3,128]{1,0:T(4,128)S(1)} %copy-done.3, f32[392,128]{1,0:T(8,128)S(1)} %get-tuple-element.31.refs_3_, f32[392,128]{1,0:T(8,128)S(1)} %collective-permute-done.6.refs_4_, ...), custom_call_target="tpu_custom_call" | custom-call | flops 8000000 | bytes 10000000 | tf_op jit(solution)/shard_map/taylor_step/pallas_call | solution.py:330
  84.9 2.6 %collective-permute-start.11 = (f32[392,128]{1,0:T(8,128)S(1)}, f32[392,128]{1,0:T(8,128)S(1)}, u32[]{:S(2)}, u32[]{:S(2)}) collective-permute-start(f32[392,128]{1,0:T(8,128)S(1)} %get-tuple-element.35.refs_3_), channel_id=1, source_target_pairs={{1,2},{3,4},{5,6},{2,1},{4,3},{6,5},{9,10},{11,12},{13,14},{10,9},... | collective-permute-start | bytes 602120 | tf_op jit(solution)/shard_map/ppermute | solution.py:291
  87.6 1.9 %collective-permute-start.10 = (f32[392,128]{1,0:T(8,128)S(1)}, f32[392,128]{1,0:T(8,128)S(1)}, u32[]{:S(2)}, u32[]{:S(2)}) collective-permute-start(f32[392,128]{1,0:T(8,128)S(1)} %get-tuple-element.35.refs_3_), channel_id=1, source_target_pairs={{0,1},{1,0},{2,3},{3,2},{4,5},{5,4},{6,7},{7,6},{8,9},{9,8},{10,11... | collective-permute-start | bytes 602120 | tf_op jit(solution)/shard_map/ppermute | solution.py:292
  89.5 0.0 copy-done.1
  89.5 1.2 current_part.1
  90.7 0.4 copy.11
  91.1 0.0 collective-permute-done.15.refs_5_
  91.1 0.0 collective-permute-done.14.refs_4_
  91.1 2.4 %taylor_step.14.refs_10_ = f32[384,128]{1,0:T(8,128)S(1)} custom-call(s32[1]{0:T(128)} %bitcast.where.refs_0_, s32[8,32]{1,0:T(8,128)S(1)} %copy-done.2, s32[3,128]{1,0:T(4,128)S(1)} %copy-done.3, f32[392,128]{1,0:T(8,128)S(1)} %get-tuple-element.39.refs_3_, f32[392,128]{1,0:T(8,128)S(1)} %collective-permute-done.14.refs_4_, ...), custom_call_target="tpu_custom_call" | custom-call | flops 8000000 | bytes 10000000 | tf_op jit(solution)/shard_map/taylor_step/pallas_call | solution.py:330
  93.4 2.5 %collective-permute-done.11.refs_5_ = f32[392,128]{1,0:T(8,128)S(1)} collective-permute-done((f32[392,128]{1,0:T(8,128)S(1)}, f32[392,128]{1,0:T(8,128)S(1)}, u32[]{:S(2)}, u32[]{:S(2)}) %collective-permute-start.11) | collective-permute-done | bytes 200736 | tf_op jit(solution)/shard_map/ppermute | solution.py:291
  96.0 0.0 collective-permute-done.10.refs_4_
  96.0 3.1 %taylor_step.15 = (f32[2,384,128]{2,1,0:T(8,128)}, f32[4,96,128]{2,1,0:T(8,128)S(1)}) custom-call(s32[1]{0:T(128)} %bitcast.where.refs_0_, s32[8,32]{1,0:T(8,128)S(1)} %copy-done.2, s32[3,128]{1,0:T(4,128)S(1)} %copy-done.3, f32[392,128]{1,0:T(8,128)S(1)} %get-tuple-element.35.refs_3_, f32[392,128]{1,0:T(8,128)S(1)} %collective-permute-done.10.refs_4_, ...), custom_call_target="tpu_custom_call" | custom-call | flops 8000000 | bytes 10000000 | tf_op jit(solution)/shard_map/taylor_step/pallas_call | solution.py:330
  99.1 0.1 copy.10
  99.3 0.1 maximum_bitcast_fusion
  99.4 35.5 %all_to_all.5.got = f32[96,16,128]{2,1,0:T(8,128)S(1)} all-to-all(f32[96,16,128]{2,1,0:T(8,128)S(1)} %maximum_bitcast_fusion), channel_id=1, replica_groups=mesh['orb'=96,'dom'=8] {'orb'}, dimensions={0} | all-to-all | bytes 1572864 | tf_op jit(solution)/shard_map/all_to_all | solution.py:362
  134.8 0.7 sum_over_orb.1
Async XLA Ops:
  0.6 0.7 copy-start.2
  0.6 0.7 copy-start.3
  0.7 0.7 copy-start.6
  1.3 1.0 copy-start
  2.3 0.7 copy-start.5
  3.0 15.3 %copy-start.4 = (f32[4,96,128]{2,1,0:T(8,128)S(1)}, f32[4,96,128]{2,1,0:T(8,128)}, u32[]{:S(2)}) copy-start(f32[4,96,128]{2,1,0:T(8,128)} %potential.1) | copy-start | bytes 589828
  5.2 13.1 %copy-start.7 = (f32[3]{0:T(128)S(1)}, f32[3]{0:T(128)}, u32[]{:S(2)}) copy-start(f32[3]{0:T(128)} %laser.1) | copy-start | bytes 40
  5.2 24.1 %collective-permute-start.5 = (f32[392,128]{1,0:T(8,128)S(1)}, f32[392,128]{1,0:T(8,128)S(1)}, u32[]{:S(2)}, u32[]{:S(2)}) collective-permute-start(f32[392,128]{1,0:T(8,128)S(1)} %get-tuple-element.28.refs_9_.refs_3_), channel_id=1, source_target_pairs={{1,2},{3,4},{5,6},{2,1},{4,3},{6,5},{9,10},{11,12},{13,14},{10,9},... | collective-permute-start | bytes 602120 | tf_op jit(solution)/shard_map/ppermute | solution.py:291
  14.2 15.1 %collective-permute-start.4 = (f32[392,128]{1,0:T(8,128)S(1)}, f32[392,128]{1,0:T(8,128)S(1)}, u32[]{:S(2)}, u32[]{:S(2)}) collective-permute-start(f32[392,128]{1,0:T(8,128)S(1)} %get-tuple-element.28.refs_9_.refs_3_), channel_id=1, source_target_pairs={{0,1},{1,0},{2,3},{3,2},{4,5},{5,4},{6,7},{7,6},{8,9},{9,8},{10,11... | collective-permute-start | bytes 602120 | tf_op jit(solution)/shard_map/ppermute | solution.py:292
  20.4 20.6 %collective-permute-start.1 = (f32[392,128]{1,0:T(8,128)S(1)}, f32[392,128]{1,0:T(8,128)S(1)}, u32[]{:S(2)}, u32[]{:S(2)}) collective-permute-start(f32[392,128]{1,0:T(8,128)S(1)} %get-tuple-element.25.refs_3_.refs_9_), channel_id=1, source_target_pairs={{1,2},{3,4},{5,6},{2,1},{4,3},{6,5},{9,10},{11,12},{13,14},{10,9},... | collective-permute-start | bytes 602120 | tf_op jit(solution)/shard_map/ppermute | solution.py:291
  27.4 13.6 %collective-permute-start = (f32[392,128]{1,0:T(8,128)S(1)}, f32[392,128]{1,0:T(8,128)S(1)}, u32[]{:S(2)}, u32[]{:S(2)}) collective-permute-start(f32[392,128]{1,0:T(8,128)S(1)} %get-tuple-element.25.refs_3_.refs_9_), channel_id=1, source_target_pairs={{0,1},{1,0},{2,3},{3,2},{4,5},{5,4},{6,7},{7,6},{8,9},{9,8},{10,11... | collective-permute-start | bytes 602120 | tf_op jit(solution)/shard_map/ppermute | solution.py:292
  33.1 16.2 %collective-permute-start.9 = (f32[392,128]{1,0:T(8,128)S(1)}, f32[392,128]{1,0:T(8,128)S(1)}, u32[]{:S(2)}, u32[]{:S(2)}) collective-permute-start(f32[392,128]{1,0:T(8,128)S(1)} %get-tuple-element.32.refs_3_), channel_id=1, source_target_pairs={{1,2},{3,4},{5,6},{2,1},{4,3},{6,5},{9,10},{11,12},{13,14},{10,9},... | collective-permute-start | bytes 602120 | tf_op jit(solution)/shard_map/ppermute | solution.py:291
  39.0 10.3 %collective-permute-start.8 = (f32[392,128]{1,0:T(8,128)S(1)}, f32[392,128]{1,0:T(8,128)S(1)}, u32[]{:S(2)}, u32[]{:S(2)}) collective-permute-start(f32[392,128]{1,0:T(8,128)S(1)} %get-tuple-element.32.refs_3_), channel_id=1, source_target_pairs={{0,1},{1,0},{2,3},{3,2},{4,5},{5,4},{6,7},{7,6},{8,9},{9,8},{10,11... | collective-permute-start | bytes 602120 | tf_op jit(solution)/shard_map/ppermute | solution.py:292
  44.7 16.1 %collective-permute-start.3 = (f32[392,128]{1,0:T(8,128)S(1)}, f32[392,128]{1,0:T(8,128)S(1)}, u32[]{:S(2)}, u32[]{:S(2)}) collective-permute-start(f32[392,128]{1,0:T(8,128)S(1)} %get-tuple-element.29.refs_3_), channel_id=1, source_target_pairs={{1,2},{3,4},{5,6},{2,1},{4,3},{6,5},{9,10},{11,12},{13,14},{10,9},... | collective-permute-start | bytes 602120 | tf_op jit(solution)/shard_map/ppermute | solution.py:291
  47.4 13.5 %collective-permute-start.2 = (f32[392,128]{1,0:T(8,128)S(1)}, f32[392,128]{1,0:T(8,128)S(1)}, u32[]{:S(2)}, u32[]{:S(2)}) collective-permute-start(f32[392,128]{1,0:T(8,128)S(1)} %get-tuple-element.29.refs_3_), channel_id=1, source_target_pairs={{0,1},{1,0},{2,3},{3,2},{4,5},{5,4},{6,7},{7,6},{8,9},{9,8},{10,11... | collective-permute-start | bytes 602120 | tf_op jit(solution)/shard_map/ppermute | solution.py:292
  53.0 16.6 %collective-permute-start.13 = (f32[392,128]{1,0:T(8,128)S(1)}, f32[392,128]{1,0:T(8,128)S(1)}, u32[]{:S(2)}, u32[]{:S(2)}) collective-permute-start(f32[392,128]{1,0:T(8,128)S(1)} %get-tuple-element.36.refs_3_), channel_id=1, source_target_pairs={{1,2},{3,4},{5,6},{2,1},{4,3},{6,5},{9,10},{11,12},{13,14},{10,9},... | collective-permute-start | bytes 602120 | tf_op jit(solution)/shard_map/ppermute | solution.py:291
  58.9 10.7 %collective-permute-start.12 = (f32[392,128]{1,0:T(8,128)S(1)}, f32[392,128]{1,0:T(8,128)S(1)}, u32[]{:S(2)}, u32[]{:S(2)}) collective-permute-start(f32[392,128]{1,0:T(8,128)S(1)} %get-tuple-element.36.refs_3_), channel_id=1, source_target_pairs={{0,1},{1,0},{2,3},{3,2},{4,5},{5,4},{6,7},{7,6},{8,9},{9,8},{10,11... | collective-permute-start | bytes 602120 | tf_op jit(solution)/shard_map/ppermute | solution.py:292
  64.6 16.5 %collective-permute-start.7 = (f32[392,128]{1,0:T(8,128)S(1)}, f32[392,128]{1,0:T(8,128)S(1)}, u32[]{:S(2)}, u32[]{:S(2)}) collective-permute-start(f32[392,128]{1,0:T(8,128)S(1)} %get-tuple-element.31.refs_3_), channel_id=1, source_target_pairs={{1,2},{3,4},{5,6},{2,1},{4,3},{6,5},{9,10},{11,12},{13,14},{10,9},... | collective-permute-start | bytes 602120 | tf_op jit(solution)/shard_map/ppermute | solution.py:291
  67.7 13.5 %collective-permute-start.6 = (f32[392,128]{1,0:T(8,128)S(1)}, f32[392,128]{1,0:T(8,128)S(1)}, u32[]{:S(2)}, u32[]{:S(2)}) collective-permute-start(f32[392,128]{1,0:T(8,128)S(1)} %get-tuple-element.31.refs_3_), channel_id=1, source_target_pairs={{0,1},{1,0},{2,3},{3,2},{4,5},{5,4},{6,7},{7,6},{8,9},{9,8},{10,11... | collective-permute-start | bytes 602120 | tf_op jit(solution)/shard_map/ppermute | solution.py:292
  73.3 17.7 %collective-permute-start.15 = (f32[392,128]{1,0:T(8,128)S(1)}, f32[392,128]{1,0:T(8,128)S(1)}, u32[]{:S(2)}, u32[]{:S(2)}) collective-permute-start(f32[392,128]{1,0:T(8,128)S(1)} %get-tuple-element.39.refs_3_), channel_id=1, source_target_pairs={{1,2},{3,4},{5,6},{2,1},{4,3},{6,5},{9,10},{11,12},{13,14},{10,9},... | collective-permute-start | bytes 602120 | tf_op jit(solution)/shard_map/ppermute | solution.py:291
  79.2 11.8 %collective-permute-start.14 = (f32[392,128]{1,0:T(8,128)S(1)}, f32[392,128]{1,0:T(8,128)S(1)}, u32[]{:S(2)}, u32[]{:S(2)}) collective-permute-start(f32[392,128]{1,0:T(8,128)S(1)} %get-tuple-element.39.refs_3_), channel_id=1, source_target_pairs={{0,1},{1,0},{2,3},{3,2},{4,5},{5,4},{6,7},{7,6},{8,9},{9,8},{10,11... | collective-permute-start | bytes 602120 | tf_op jit(solution)/shard_map/ppermute | solution.py:292
  81.2 8.3 %copy-start.1 = (f32[2,1,4,96,128]{4,3,2,1,0:T(8,128)S(1)}, f32[2,1,4,96,128]{4,3,2,1,0:T(8,128)}, u32[]{:S(2)}) copy-start(f32[2,1,4,96,128]{4,3,2,1,0:T(8,128)} %param.7) | copy-start | bytes 1179652
  84.9 11.1 %collective-permute-start.11 = (f32[392,128]{1,0:T(8,128)S(1)}, f32[392,128]{1,0:T(8,128)S(1)}, u32[]{:S(2)}, u32[]{:S(2)}) collective-permute-start(f32[392,128]{1,0:T(8,128)S(1)} %get-tuple-element.35.refs_3_), channel_id=1, source_target_pairs={{1,2},{3,4},{5,6},{2,1},{4,3},{6,5},{9,10},{11,12},{13,14},{10,9},... | collective-permute-start | bytes 602120 | tf_op jit(solution)/shard_map/ppermute | solution.py:291
  87.6 8.4 %collective-permute-start.10 = (f32[392,128]{1,0:T(8,128)S(1)}, f32[392,128]{1,0:T(8,128)S(1)}, u32[]{:S(2)}, u32[]{:S(2)}) collective-permute-start(f32[392,128]{1,0:T(8,128)S(1)} %get-tuple-element.35.refs_3_), channel_id=1, source_target_pairs={{0,1},{1,0},{2,3},{3,2},{4,5},{5,4},{6,7},{7,6},{8,9},{9,8},{10,11... | collective-permute-start | bytes 602120 | tf_op jit(solution)/shard_map/ppermute | solution.py:292

commit v2 on v1

--- a/solution.py
+++ b/solution.py
@@ -10,7 +10,7 @@
 TERMS = 4
 BOX = 8
 PROJ = 4
-GROUP = 4
+GROUP = 32
 
 spacing = 0.5
 time_step = 0.05

time: 136 us -> 127 us (0.934)
  Pallas kernels: 33.9 us -> 23.5 us
  blocking collectives: 35.5 us -> 37.7 us
  waiting for transfers between devices: 2.58 us -> 0.79 us
    pallas_call x8, Pallas kernels: 27.8 us -> 19.1 us  [step(): kernel(functools.partial(step_kernel, planes, rows, slots, sign * time_st...]
    all_to_all x1, blocking collectives: 35.5 us -> 37.7 us  [body(): fields = lax.all_to_all(fields, 'orb', 0, 0, tiled=True)]
    ppermute x8, waiting for transfers between devices: 2.56 us -> 0.77 us  [exchange(): other = lax.ppermute(value, 'dom', others)]
  transfers between devices with their start and end apart: 16 -> 16, of which waited for: 1 -> 1; matrix products, arithmetic and copies ran while one was open for 0% -> 0% of each run, Pallas kernels for 21% -> 15%
where the time goes in v2:
time: 127 us; the launch traced here: 126 us
  starting transfers between devices  60 us (47%)
  blocking collectives  37.7 us (30%)
  Pallas kernels  23.5 us (19%)
  local copies, waits for them, and re-layouts  2.87 us (2%)
    ppermute x8, starting transfers between devices, exchange(): other = lax.ppermute(value, 'dom', others)  42.3 us
    all_to_all x1, blocking collectives, body(): fields = lax.all_to_all(fields, 'orb', 0, 0, tiled=True)  37.7 us
    pallas_call x8, Pallas kernels, step(): kernel(functools.partial(step_kernel, planes, rows, slots, sign * time_st...  19.1 us
    ppermute x8, starting transfers between devices, exchange(): return (lax.ppermute(value, 'dom', pairs), other)  17.7 us
  transfers between devices with their start and end apart: 16, of which 1 were waited for; matrix products, arithmetic and copies ran while one was open for 0% of the time, Pallas kernels for 15%

profile of v2, /device:TPU:1, one launch (start us, length us, event | category | flops | bytes accessed | tf_op | source)
XLA Modules:
  0.0 126.0 jit_solution(17747077469307907712)
XLA Ops:
  0.6 0.0 copy-start.2
  0.6 0.0 copy-start.3
  0.7 0.0 copy-start.6
  0.7 0.7 copy-done.2
  1.3 0.0 copy-done.3
  1.3 0.0 copy-done.6
  1.3 0.0 copy-start
  1.3 1.0 copy-done
  2.3 0.0 copy-start.5
  2.3 0.7 copy-done.5
  3.0 0.0 copy-start.4
  3.0 1.3 %prepare_real.1 = (f32[32,8,128]{2,1,0:T(8,128)S(1)}, f32[8,128]{1,0:T(8,128)S(1)}, f32[392,128]{1,0:T(8,128)S(1)}) custom-call(s32[1]{0:T(128)} %bitcast.where.refs_0_, s32[8,32]{1,0:T(8,128)S(1)} %copy-done.2, s32[3,128]{1,0:T(4,128)S(1)} %copy-done.3, f32[4]{0:T(128)S(1)} %copy-done.6, f32[4,512]{1,0:T(4,128)S(1)} %copy-done.5, f32[2,384,128]{2,1,0:T(8,128)S(1)} %bitcast.7), custom_call_target="tpu_custom_call" | custom-call | flops 8000000 | bytes 10000000 | tf_op jit(solution)/shard_map/prepare_real/pallas_call | solution.py:308
  4.3 0.0 copy-start.7
  4.3 9.0 %collective-permute-start.5 = (f32[392,128]{1,0:T(8,128)S(1)}, f32[392,128]{1,0:T(8,128)S(1)}, u32[]{:S(2)}, u32[]{:S(2)}) collective-permute-start(f32[392,128]{1,0:T(8,128)S(1)} %get-tuple-element.28.refs_9_.refs_3_), channel_id=1, source_target_pairs={{1,2},{3,4},{5,6},{2,1},{4,3},{6,5},{9,10},{11,12},{13,14},{10,9},... | collective-permute-start | bytes 602120 | tf_op jit(solution)/shard_map/ppermute | solution.py:291
  13.4 4.1 %collective-permute-start.4 = (f32[392,128]{1,0:T(8,128)S(1)}, f32[392,128]{1,0:T(8,128)S(1)}, u32[]{:S(2)}, u32[]{:S(2)}) collective-permute-start(f32[392,128]{1,0:T(8,128)S(1)} %get-tuple-element.28.refs_9_.refs_3_), channel_id=1, source_target_pairs={{0,1},{1,0},{2,3},{3,2},{4,5},{5,4},{6,7},{7,6},{8,9},{9,8},{10,11... | collective-permute-start | bytes 602120 | tf_op jit(solution)/shard_map/ppermute | solution.py:292
  17.5 0.0 copy-done.4
  17.5 0.0 copy-done.7
  17.5 1.2 prepare_imag.1
  18.7 7.0 %collective-permute-start.1 = (f32[392,128]{1,0:T(8,128)S(1)}, f32[392,128]{1,0:T(8,128)S(1)}, u32[]{:S(2)}, u32[]{:S(2)}) collective-permute-start(f32[392,128]{1,0:T(8,128)S(1)} %get-tuple-element.25.refs_3_.refs_9_), channel_id=1, source_target_pairs={{1,2},{3,4},{5,6},{2,1},{4,3},{6,5},{9,10},{11,12},{13,14},{10,9},... | collective-permute-start | bytes 602120 | tf_op jit(solution)/shard_map/ppermute | solution.py:291
  25.8 1.9 %collective-permute-start = (f32[392,128]{1,0:T(8,128)S(1)}, f32[392,128]{1,0:T(8,128)S(1)}, u32[]{:S(2)}, u32[]{:S(2)}) collective-permute-start(f32[392,128]{1,0:T(8,128)S(1)} %get-tuple-element.25.refs_3_.refs_9_), channel_id=1, source_target_pairs={{0,1},{1,0},{2,3},{3,2},{4,5},{5,4},{6,7},{7,6},{8,9},{9,8},{10,11... | collective-permute-start | bytes 602120 | tf_op jit(solution)/shard_map/ppermute | solution.py:292
  27.7 0.0 collective-permute-done.5.refs_5_.real_other
  27.7 0.0 collective-permute-done.4.refs_4_.real_pair
  27.7 2.4 %taylor_step.9 = (f32[392,128]{1,0:T(8,128)S(1)}, f32[384,128]{1,0:T(8,128)S(1)}) custom-call(s32[1]{0:T(128)} %bitcast.where.refs_0_, s32[8,32]{1,0:T(8,128)S(1)} %copy-done.2, s32[3,128]{1,0:T(4,128)S(1)} %copy-done.3, f32[392,128]{1,0:T(8,128)S(1)} %get-tuple-element.28.refs_9_.refs_3_, f32[392,128]{1,0:T(8,128)S(1)} %collective-permute-done.4.refs_4_.real_pair, ...), custom_call_target="tpu_custom_call" | custom-call | flops 8000000 | bytes 10000000 | tf_op jit(solution)/shard_map/taylor_step/pallas_call | solution.py:330
  30.2 5.9 %collective-permute-start.9 = (f32[392,128]{1,0:T(8,128)S(1)}, f32[392,128]{1,0:T(8,128)S(1)}, u32[]{:S(2)}, u32[]{:S(2)}) collective-permute-start(f32[392,128]{1,0:T(8,128)S(1)} %get-tuple-element.32.refs_3_), channel_id=1, source_target_pairs={{1,2},{3,4},{5,6},{2,1},{4,3},{6,5},{9,10},{11,12},{13,14},{10,9},... | collective-permute-start | bytes 602120 | tf_op jit(solution)/shard_map/ppermute | solution.py:291
  36.1 1.9 %collective-permute-start.8 = (f32[392,128]{1,0:T(8,128)S(1)}, f32[392,128]{1,0:T(8,128)S(1)}, u32[]{:S(2)}, u32[]{:S(2)}) collective-permute-start(f32[392,128]{1,0:T(8,128)S(1)} %get-tuple-element.32.refs_3_), channel_id=1, source_target_pairs={{0,1},{1,0},{2,3},{3,2},{4,5},{5,4},{6,7},{7,6},{8,9},{9,8},{10,11... | collective-permute-start | bytes 602120 | tf_op jit(solution)/shard_map/ppermute | solution.py:292
  38.0 0.0 collective-permute-done.1.refs_5_.imag_other
  38.0 0.0 collective-permute-done.refs_4_.imag_pair
  38.0 2.4 %taylor_step.8 = (f32[392,128]{1,0:T(8,128)S(1)}, f32[384,128]{1,0:T(8,128)S(1)}) custom-call(s32[1]{0:T(128)} %bitcast.where.refs_0_, s32[8,32]{1,0:T(8,128)S(1)} %copy-done.2, s32[3,128]{1,0:T(4,128)S(1)} %copy-done.3, f32[392,128]{1,0:T(8,128)S(1)} %get-tuple-element.25.refs_3_.refs_9_, f32[392,128]{1,0:T(8,128)S(1)} %collective-permute-done.refs_4_.imag_pair, ...), custom_call_target="tpu_custom_call" | custom-call | flops 8000000 | bytes 10000000 | tf_op jit(solution)/shard_map/taylor_step/pallas_call | solution.py:330
  40.5 2.7 %collective-permute-start.3 = (f32[392,128]{1,0:T(8,128)S(1)}, f32[392,128]{1,0:T(8,128)S(1)}, u32[]{:S(2)}, u32[]{:S(2)}) collective-permute-start(f32[392,128]{1,0:T(8,128)S(1)} %get-tuple-element.29.refs_3_), channel_id=1, source_target_pairs={{1,2},{3,4},{5,6},{2,1},{4,3},{6,5},{9,10},{11,12},{13,14},{10,9},... | collective-permute-start | bytes 602120 | tf_op jit(solution)/shard_map/ppermute | solution.py:291
  43.1 1.9 %collective-permute-start.2 = (f32[392,128]{1,0:T(8,128)S(1)}, f32[392,128]{1,0:T(8,128)S(1)}, u32[]{:S(2)}, u32[]{:S(2)}) collective-permute-start(f32[392,128]{1,0:T(8,128)S(1)} %get-tuple-element.29.refs_3_), channel_id=1, source_target_pairs={{0,1},{1,0},{2,3},{3,2},{4,5},{5,4},{6,7},{7,6},{8,9},{9,8},{10,11... | collective-permute-start | bytes 602120 | tf_op jit(solution)/shard_map/ppermute | solution.py:292
  45.1 0.0 collective-permute-done.9.refs_5_
  45.1 0.0 collective-permute-done.8.refs_4_
  45.1 2.4 %taylor_step.11 = (f32[392,128]{1,0:T(8,128)S(1)}, f32[384,128]{1,0:T(8,128)S(1)}) custom-call(s32[1]{0:T(128)} %bitcast.where.refs_0_, s32[8,32]{1,0:T(8,128)S(1)} %copy-done.2, s32[3,128]{1,0:T(4,128)S(1)} %copy-done.3, f32[392,128]{1,0:T(8,128)S(1)} %get-tuple-element.32.refs_3_, f32[392,128]{1,0:T(8,128)S(1)} %collective-permute-done.8.refs_4_, ...), custom_call_target="tpu_custom_call" | custom-call | flops 8000000 | bytes 10000000 | tf_op jit(solution)/shard_map/taylor_step/pallas_call | solution.py:330
  47.5 5.9 %collective-permute-start.13 = (f32[392,128]{1,0:T(8,128)S(1)}, f32[392,128]{1,0:T(8,128)S(1)}, u32[]{:S(2)}, u32[]{:S(2)}) collective-permute-start(f32[392,128]{1,0:T(8,128)S(1)} %get-tuple-element.36.refs_3_), channel_id=1, source_target_pairs={{1,2},{3,4},{5,6},{2,1},{4,3},{6,5},{9,10},{11,12},{13,14},{10,9},... | collective-permute-start | bytes 602120 | tf_op jit(solution)/shard_map/ppermute | solution.py:291
  53.4 1.9 %collective-permute-start.12 = (f32[392,128]{1,0:T(8,128)S(1)}, f32[392,128]{1,0:T(8,128)S(1)}, u32[]{:S(2)}, u32[]{:S(2)}) collective-permute-start(f32[392,128]{1,0:T(8,128)S(1)} %get-tuple-element.36.refs_3_), channel_id=1, source_target_pairs={{0,1},{1,0},{2,3},{3,2},{4,5},{5,4},{6,7},{7,6},{8,9},{9,8},{10,11... | collective-permute-start | bytes 602120 | tf_op jit(solution)/shard_map/ppermute | solution.py:292
  55.4 0.0 collective-permute-done.3.refs_5_
  55.4 0.0 collective-permute-done.2.refs_4_
  55.4 2.5 %taylor_step.10 = (f32[392,128]{1,0:T(8,128)S(1)}, f32[384,128]{1,0:T(8,128)S(1)}) custom-call(s32[1]{0:T(128)} %bitcast.where.refs_0_, s32[8,32]{1,0:T(8,128)S(1)} %copy-done.2, s32[3,128]{1,0:T(4,128)S(1)} %copy-done.3, f32[392,128]{1,0:T(8,128)S(1)} %get-tuple-element.29.refs_3_, f32[392,128]{1,0:T(8,128)S(1)} %collective-permute-done.2.refs_4_, ...), custom_call_target="tpu_custom_call" | custom-call | flops 8000000 | bytes 10000000 | tf_op jit(solution)/shard_map/taylor_step/pallas_call | solution.py:330
  57.8 3.2 %collective-permute-start.7 = (f32[392,128]{1,0:T(8,128)S(1)}, f32[392,128]{1,0:T(8,128)S(1)}, u32[]{:S(2)}, u32[]{:S(2)}) collective-permute-start(f32[392,128]{1,0:T(8,128)S(1)} %get-tuple-element.31.refs_3_), channel_id=1, source_target_pairs={{1,2},{3,4},{5,6},{2,1},{4,3},{6,5},{9,10},{11,12},{13,14},{10,9},... | collective-permute-start | bytes 602120 | tf_op jit(solution)/shard_map/ppermute | solution.py:291
  61.0 1.9 %collective-permute-start.6 = (f32[392,128]{1,0:T(8,128)S(1)}, f32[392,128]{1,0:T(8,128)S(1)}, u32[]{:S(2)}, u32[]{:S(2)}) collective-permute-start(f32[392,128]{1,0:T(8,128)S(1)} %get-tuple-element.31.refs_3_), channel_id=1, source_target_pairs={{0,1},{1,0},{2,3},{3,2},{4,5},{5,4},{6,7},{7,6},{8,9},{9,8},{10,11... | collective-permute-start | bytes 602120 | tf_op jit(solution)/shard_map/ppermute | solution.py:292
  63.0 0.0 collective-permute-done.13.refs_5_
  63.0 0.0 collective-permute-done.12.refs_4_
  63.0 2.4 %taylor_step.13 = (f32[392,128]{1,0:T(8,128)S(1)}, f32[384,128]{1,0:T(8,128)S(1)}) custom-call(s32[1]{0:T(128)} %bitcast.where.refs_0_, s32[8,32]{1,0:T(8,128)S(1)} %copy-done.2, s32[3,128]{1,0:T(4,128)S(1)} %copy-done.3, f32[392,128]{1,0:T(8,128)S(1)} %get-tuple-element.36.refs_3_, f32[392,128]{1,0:T(8,128)S(1)} %collective-permute-done.12.refs_4_, ...), custom_call_target="tpu_custom_call" | custom-call | flops 8000000 | bytes 10000000 | tf_op jit(solution)/shard_map/taylor_step/pallas_call | solution.py:330
  65.4 5.9 %collective-permute-start.15 = (f32[392,128]{1,0:T(8,128)S(1)}, f32[392,128]{1,0:T(8,128)S(1)}, u32[]{:S(2)}, u32[]{:S(2)}) collective-permute-start(f32[392,128]{1,0:T(8,128)S(1)} %get-tuple-element.39.refs_3_), channel_id=1, source_target_pairs={{1,2},{3,4},{5,6},{2,1},{4,3},{6,5},{9,10},{11,12},{13,14},{10,9},... | collective-permute-start | bytes 602120 | tf_op jit(solution)/shard_map/ppermute | solution.py:291
  71.3 2.1 %collective-permute-start.14 = (f32[392,128]{1,0:T(8,128)S(1)}, f32[392,128]{1,0:T(8,128)S(1)}, u32[]{:S(2)}, u32[]{:S(2)}) collective-permute-start(f32[392,128]{1,0:T(8,128)S(1)} %get-tuple-element.39.refs_3_), channel_id=1, source_target_pairs={{0,1},{1,0},{2,3},{3,2},{4,5},{5,4},{6,7},{7,6},{8,9},{9,8},{10,11... | collective-permute-start | bytes 602120 | tf_op jit(solution)/shard_map/ppermute | solution.py:292
  73.4 0.0 collective-permute-done.7.refs_5_
  73.4 0.0 collective-permute-done.6.refs_4_
  73.4 0.0 copy-start.1
  73.4 2.4 %taylor_step.12 = (f32[392,128]{1,0:T(8,128)S(1)}, f32[384,128]{1,0:T(8,128)S(1)}) custom-call(s32[1]{0:T(128)} %bitcast.where.refs_0_, s32[8,32]{1,0:T(8,128)S(1)} %copy-done.2, s32[3,128]{1,0:T(4,128)S(1)} %copy-done.3, f32[392,128]{1,0:T(8,128)S(1)} %get-tuple-element.31.refs_3_, f32[392,128]{1,0:T(8,128)S(1)} %collective-permute-done.6.refs_4_, ...), custom_call_target="tpu_custom_call" | custom-call | flops 8000000 | bytes 10000000 | tf_op jit(solution)/shard_map/taylor_step/pallas_call | solution.py:330
  75.8 2.7 %collective-permute-start.11 = (f32[392,128]{1,0:T(8,128)S(1)}, f32[392,128]{1,0:T(8,128)S(1)}, u32[]{:S(2)}, u32[]{:S(2)}) collective-permute-start(f32[392,128]{1,0:T(8,128)S(1)} %get-tuple-element.35.refs_3_), channel_id=1, source_target_pairs={{1,2},{3,4},{5,6},{2,1},{4,3},{6,5},{9,10},{11,12},{13,14},{10,9},... | collective-permute-start | bytes 602120 | tf_op jit(solution)/shard_map/ppermute | solution.py:291
  78.5 1.9 %collective-permute-start.10 = (f32[392,128]{1,0:T(8,128)S(1)}, f32[392,128]{1,0:T(8,128)S(1)}, u32[]{:S(2)}, u32[]{:S(2)}) collective-permute-start(f32[392,128]{1,0:T(8,128)S(1)} %get-tuple-element.35.refs_3_), channel_id=1, source_target_pairs={{0,1},{1,0},{2,3},{3,2},{4,5},{5,4},{6,7},{7,6},{8,9},{9,8},{10,11... | collective-permute-start | bytes 602120 | tf_op jit(solution)/shard_map/ppermute | solution.py:292
  80.5 0.0 copy-done.1
  80.5 1.2 current_part.1
  81.7 0.4 copy.11
  82.0 0.0 collective-permute-done.15.refs_5_
  82.0 0.0 collective-permute-done.14.refs_4_
  82.1 1.9 %taylor_step.14.refs_10_ = f32[384,128]{1,0:T(8,128)S(1)} custom-call(s32[1]{0:T(128)} %bitcast.where.refs_0_, s32[8,32]{1,0:T(8,128)S(1)} %copy-done.2, s32[3,128]{1,0:T(4,128)S(1)} %copy-done.3, f32[392,128]{1,0:T(8,128)S(1)} %get-tuple-element.39.refs_3_, f32[392,128]{1,0:T(8,128)S(1)} %collective-permute-done.14.refs_4_, ...), custom_call_target="tpu_custom_call" | custom-call | flops 8000000 | bytes 10000000 | tf_op jit(solution)/shard_map/taylor_step/pallas_call | solution.py:330
  83.9 0.7 collective-permute-done.11.refs_5_
  84.7 0.0 collective-permute-done.10.refs_4_
  84.7 2.6 %taylor_step.15 = (f32[2,384,128]{2,1,0:T(8,128)}, f32[4,96,128]{2,1,0:T(8,128)S(1)}) custom-call(s32[1]{0:T(128)} %bitcast.where.refs_0_, s32[8,32]{1,0:T(8,128)S(1)} %copy-done.2, s32[3,128]{1,0:T(4,128)S(1)} %copy-done.3, f32[392,128]{1,0:T(8,128)S(1)} %get-tuple-element.35.refs_3_, f32[392,128]{1,0:T(8,128)S(1)} %collective-permute-done.10.refs_4_, ...), custom_call_target="tpu_custom_call" | custom-call | flops 8000000 | bytes 10000000 | tf_op jit(solution)/shard_map/taylor_step/pallas_call | solution.py:330
  87.3 0.1 copy.10
  87.4 0.1 maximum_bitcast_fusion
  87.5 37.7 %all_to_all.5.got = f32[96,16,128]{2,1,0:T(8,128)S(1)} all-to-all(f32[96,16,128]{2,1,0:T(8,128)S(1)} %maximum_bitcast_fusion), channel_id=1, replica_groups=mesh['orb'=96,'dom'=8] {'orb'}, dimensions={0} | all-to-all | bytes 1572864 | tf_op jit(solution)/shard_map/all_to_all | solution.py:362
  125.3 0.7 sum_over_orb.1
Async XLA Ops:
  0.6 0.7 copy-start.2
  0.6 0.7 copy-start.3
  0.7 0.7 copy-start.6
  1.3 1.0 copy-start
  2.3 0.7 copy-start.5
  3.0 14.4 %copy-start.4 = (f32[4,96,128]{2,1,0:T(8,128)S(1)}, f32[4,96,128]{2,1,0:T(8,128)}, u32[]{:S(2)}) copy-start(f32[4,96,128]{2,1,0:T(8,128)} %potential.1) | copy-start | bytes 589828
  4.3 13.1 %copy-start.7 = (f32[3]{0:T(128)S(1)}, f32[3]{0:T(128)}, u32[]{:S(2)}) copy-start(f32[3]{0:T(128)} %laser.1) | copy-start | bytes 40
  4.3 23.4 %collective-permute-start.5 = (f32[392,128]{1,0:T(8,128)S(1)}, f32[392,128]{1,0:T(8,128)S(1)}, u32[]{:S(2)}, u32[]{:S(2)}) collective-permute-start(f32[392,128]{1,0:T(8,128)S(1)} %get-tuple-element.28.refs_9_.refs_3_), channel_id=1, source_target_pairs={{1,2},{3,4},{5,6},{2,1},{4,3},{6,5},{9,10},{11,12},{13,14},{10,9},... | collective-permute-start | bytes 602120 | tf_op jit(solution)/shard_map/ppermute | solution.py:291
  13.4 14.4 %collective-permute-start.4 = (f32[392,128]{1,0:T(8,128)S(1)}, f32[392,128]{1,0:T(8,128)S(1)}, u32[]{:S(2)}, u32[]{:S(2)}) collective-permute-start(f32[392,128]{1,0:T(8,128)S(1)} %get-tuple-element.28.refs_9_.refs_3_), channel_id=1, source_target_pairs={{0,1},{1,0},{2,3},{3,2},{4,5},{5,4},{6,7},{7,6},{8,9},{9,8},{10,11... | collective-permute-start | bytes 602120 | tf_op jit(solution)/shard_map/ppermute | solution.py:292
  18.7 19.3 %collective-permute-start.1 = (f32[392,128]{1,0:T(8,128)S(1)}, f32[392,128]{1,0:T(8,128)S(1)}, u32[]{:S(2)}, u32[]{:S(2)}) collective-permute-start(f32[392,128]{1,0:T(8,128)S(1)} %get-tuple-element.25.refs_3_.refs_9_), channel_id=1, source_target_pairs={{1,2},{3,4},{5,6},{2,1},{4,3},{6,5},{9,10},{11,12},{13,14},{10,9},... | collective-permute-start | bytes 602120 | tf_op jit(solution)/shard_map/ppermute | solution.py:291
  25.8 12.2 %collective-permute-start = (f32[392,128]{1,0:T(8,128)S(1)}, f32[392,128]{1,0:T(8,128)S(1)}, u32[]{:S(2)}, u32[]{:S(2)}) collective-permute-start(f32[392,128]{1,0:T(8,128)S(1)} %get-tuple-element.25.refs_3_.refs_9_), channel_id=1, source_target_pairs={{0,1},{1,0},{2,3},{3,2},{4,5},{5,4},{6,7},{7,6},{8,9},{9,8},{10,11... | collective-permute-start | bytes 602120 | tf_op jit(solution)/shard_map/ppermute | solution.py:292
  30.2 14.9 %collective-permute-start.9 = (f32[392,128]{1,0:T(8,128)S(1)}, f32[392,128]{1,0:T(8,128)S(1)}, u32[]{:S(2)}, u32[]{:S(2)}) collective-permute-start(f32[392,128]{1,0:T(8,128)S(1)} %get-tuple-element.32.refs_3_), channel_id=1, source_target_pairs={{1,2},{3,4},{5,6},{2,1},{4,3},{6,5},{9,10},{11,12},{13,14},{10,9},... | collective-permute-start | bytes 602120 | tf_op jit(solution)/shard_map/ppermute | solution.py:291
  36.1 9.0 %collective-permute-start.8 = (f32[392,128]{1,0:T(8,128)S(1)}, f32[392,128]{1,0:T(8,128)S(1)}, u32[]{:S(2)}, u32[]{:S(2)}) collective-permute-start(f32[392,128]{1,0:T(8,128)S(1)} %get-tuple-element.32.refs_3_), channel_id=1, source_target_pairs={{0,1},{1,0},{2,3},{3,2},{4,5},{5,4},{6,7},{7,6},{8,9},{9,8},{10,11... | collective-permute-start | bytes 602120 | tf_op jit(solution)/shard_map/ppermute | solution.py:292
  40.5 14.9 %collective-permute-start.3 = (f32[392,128]{1,0:T(8,128)S(1)}, f32[392,128]{1,0:T(8,128)S(1)}, u32[]{:S(2)}, u32[]{:S(2)}) collective-permute-start(f32[392,128]{1,0:T(8,128)S(1)} %get-tuple-element.29.refs_3_), channel_id=1, source_target_pairs={{1,2},{3,4},{5,6},{2,1},{4,3},{6,5},{9,10},{11,12},{13,14},{10,9},... | collective-permute-start | bytes 602120 | tf_op jit(solution)/shard_map/ppermute | solution.py:291
  43.1 12.2 %collective-permute-start.2 = (f32[392,128]{1,0:T(8,128)S(1)}, f32[392,128]{1,0:T(8,128)S(1)}, u32[]{:S(2)}, u32[]{:S(2)}) collective-permute-start(f32[392,128]{1,0:T(8,128)S(1)} %get-tuple-element.29.refs_3_), channel_id=1, source_target_pairs={{0,1},{1,0},{2,3},{3,2},{4,5},{5,4},{6,7},{7,6},{8,9},{9,8},{10,11... | collective-permute-start | bytes 602120 | tf_op jit(solution)/shard_map/ppermute | solution.py:292
  47.5 15.4 %collective-permute-start.13 = (f32[392,128]{1,0:T(8,128)S(1)}, f32[392,128]{1,0:T(8,128)S(1)}, u32[]{:S(2)}, u32[]{:S(2)}) collective-permute-start(f32[392,128]{1,0:T(8,128)S(1)} %get-tuple-element.36.refs_3_), channel_id=1, source_target_pairs={{1,2},{3,4},{5,6},{2,1},{4,3},{6,5},{9,10},{11,12},{13,14},{10,9},... | collective-permute-start | bytes 602120 | tf_op jit(solution)/shard_map/ppermute | solution.py:291
  53.4 9.5 %collective-permute-start.12 = (f32[392,128]{1,0:T(8,128)S(1)}, f32[392,128]{1,0:T(8,128)S(1)}, u32[]{:S(2)}, u32[]{:S(2)}) collective-permute-start(f32[392,128]{1,0:T(8,128)S(1)} %get-tuple-element.36.refs_3_), channel_id=1, source_target_pairs={{0,1},{1,0},{2,3},{3,2},{4,5},{5,4},{6,7},{7,6},{8,9},{9,8},{10,11... | collective-permute-start | bytes 602120 | tf_op jit(solution)/shard_map/ppermute | solution.py:292
  57.8 15.5 %collective-permute-start.7 = (f32[392,128]{1,0:T(8,128)S(1)}, f32[392,128]{1,0:T(8,128)S(1)}, u32[]{:S(2)}, u32[]{:S(2)}) collective-permute-start(f32[392,128]{1,0:T(8,128)S(1)} %get-tuple-element.31.refs_3_), channel_id=1, source_target_pairs={{1,2},{3,4},{5,6},{2,1},{4,3},{6,5},{9,10},{11,12},{13,14},{10,9},... | collective-permute-start | bytes 602120 | tf_op jit(solution)/shard_map/ppermute | solution.py:291
  61.0 12.4 %collective-permute-start.6 = (f32[392,128]{1,0:T(8,128)S(1)}, f32[392,128]{1,0:T(8,128)S(1)}, u32[]{:S(2)}, u32[]{:S(2)}) collective-permute-start(f32[392,128]{1,0:T(8,128)S(1)} %get-tuple-element.31.refs_3_), channel_id=1, source_target_pairs={{0,1},{1,0},{2,3},{3,2},{4,5},{5,4},{6,7},{7,6},{8,9},{9,8},{10,11... | collective-permute-start | bytes 602120 | tf_op jit(solution)/shard_map/ppermute | solution.py:292
  65.4 16.7 %collective-permute-start.15 = (f32[392,128]{1,0:T(8,128)S(1)}, f32[392,128]{1,0:T(8,128)S(1)}, u32[]{:S(2)}, u32[]{:S(2)}) collective-permute-start(f32[392,128]{1,0:T(8,128)S(1)} %get-tuple-element.39.refs_3_), channel_id=1, source_target_pairs={{1,2},{3,4},{5,6},{2,1},{4,3},{6,5},{9,10},{11,12},{13,14},{10,9},... | collective-permute-start | bytes 602120 | tf_op jit(solution)/shard_map/ppermute | solution.py:291
  71.3 10.8 %collective-permute-start.14 = (f32[392,128]{1,0:T(8,128)S(1)}, f32[392,128]{1,0:T(8,128)S(1)}, u32[]{:S(2)}, u32[]{:S(2)}) collective-permute-start(f32[392,128]{1,0:T(8,128)S(1)} %get-tuple-element.39.refs_3_), channel_id=1, source_target_pairs={{0,1},{1,0},{2,3},{3,2},{4,5},{5,4},{6,7},{7,6},{8,9},{9,8},{10,11... | collective-permute-start | bytes 602120 | tf_op jit(solution)/shard_map/ppermute | solution.py:292
  73.4 7.1 %copy-start.1 = (f32[2,1,4,96,128]{4,3,2,1,0:T(8,128)S(1)}, f32[2,1,4,96,128]{4,3,2,1,0:T(8,128)}, u32[]{:S(2)}) copy-start(f32[2,1,4,96,128]{4,3,2,1,0:T(8,128)} %param.7) | copy-start | bytes 1179652
  75.8 8.8 %collective-permute-start.11 = (f32[392,128]{1,0:T(8,128)S(1)}, f32[392,128]{1,0:T(8,128)S(1)}, u32[]{:S(2)}, u32[]{:S(2)}) collective-permute-start(f32[392,128]{1,0:T(8,128)S(1)} %get-tuple-element.35.refs_3_), channel_id=1, source_target_pairs={{1,2},{3,4},{5,6},{2,1},{4,3},{6,5},{9,10},{11,12},{13,14},{10,9},... | collective-permute-start | bytes 602120 | tf_op jit(solution)/shard_map/ppermute | solution.py:291
  78.5 6.1 %collective-permute-start.10 = (f32[392,128]{1,0:T(8,128)S(1)}, f32[392,128]{1,0:T(8,128)S(1)}, u32[]{:S(2)}, u32[]{:S(2)}) collective-permute-start(f32[392,128]{1,0:T(8,128)S(1)} %get-tuple-element.35.refs_3_), channel_id=1, source_target_pairs={{0,1},{1,0},{2,3},{3,2},{4,5},{5,4},{6,7},{7,6},{8,9},{9,8},{10,11... | collective-permute-start | bytes 602120 | tf_op jit(solution)/shard_map/ppermute | solution.py:292

commit v3 on v2

--- a/solution.py
+++ b/solution.py
@@ -11,6 +11,7 @@
 BOX = 8
 PROJ = 4
 GROUP = 32
+RUN = 3
 
 spacing = 0.5
 time_step = 0.05
@@ -21,6 +22,7 @@
 
 VMEM = pl.BlockSpec(memory_space=pltpu.VMEM)
 SMEM = pl.BlockSpec(memory_space=pltpu.SMEM)
+ANY = pl.BlockSpec(memory_space=pl.ANY)
 
 
 def f32(*shape):
@@ -106,23 +108,18 @@
 
 
 def prepare_kernel(
-    planes, rows, slots, where, atoms, anchor, strength, projector, u,
-    proj, weight, message, sums,
+    planes, rows, slots, where, atoms, anchor, strength, projector_far, u,
+    proj, weight, message, sums, projector, sems,
 ):
     cells = u.shape[-1]
     size = planes * rows
+    fetch = pltpu.make_async_copy(u.at[0], message.at[0:size], sems.at[0])
+    fetch_projector = pltpu.make_async_copy(projector_far, projector, sems.at[1])
+    fetch.start()
+    fetch_projector.start()
     me = where[0]
     behind = jnp.maximum(me - 1, 0)
     lane = lax.broadcasted_iota(jnp.int32, (8, cells), 1)
-    for chunk in range(BOX**3 // cells):
-        block = projector[:, chunk * cells : (chunk + 1) * cells]
-        for part in range(cells // BOX):
-            i, j = chunk * (cells // BOX**2) + part // BOX, part % BOX
-            moved = block if part == 0 else pltpu.roll(block, cells - part * BOX, 1)
-            moved = jnp.where(lane[:PROJ] < BOX, moved, 0.0)
-            for p in range(PROJ):
-                proj[p * BOX + i, j : j + 1, :] = moved[p : p + 1]
-
     line = lax.broadcasted_iota(jnp.int32, (8, cells), 0)
     listed = jnp.zeros((8, cells), jnp.float32)
     for slot in range(slots):
@@ -135,24 +132,36 @@
         strengths = jnp.where((lane % PROJ) == p, strength[p], strengths)
     weight[...] = listed * strengths
 
-    message[0:size, :] = u[0]
-    message[size : size + 8, :] = partial_sums(planes, rows, slots, me, atoms, anchor, u.at[0], proj, sums)
+    fetch_projector.wait()
+    for chunk in range(BOX**3 // cells):
+        block = projector[:, chunk * cells : (chunk + 1) * cells]
+        for part in range(cells // BOX):
+            i, j = chunk * (cells // BOX**2) + part // BOX, part % BOX
+            moved = block if part == 0 else pltpu.roll(block, cells - part * BOX, 1)
+            moved = jnp.where(lane[:PROJ] < BOX, moved, 0.0)
+            for p in range(PROJ):
+                proj[p * BOX + i, j : j + 1, :] = moved[p : p + 1]
+
+    fetch.wait()
+    message[size : size + 8, :] = partial_sums(planes, rows, slots, me, atoms, anchor, message, proj, sums)
 
 
 def second_kernel(
-    planes, rows, slots, domains, where, atoms, anchor, laser, potential, proj, u, v, message, sums
+    planes, rows, slots, domains, where, atoms, anchor, laser, potential, proj, u, v, message, sums, sem
 ):
     cells = u.shape[-1]
     size = planes * rows
     me = where[0]
-    message[0:size, :] = u[1]
-    message[size : size + 8, :] = partial_sums(planes, rows, slots, me, atoms, anchor, u.at[1], proj, sums)
+    fetch = pltpu.make_async_copy(u.at[1], message.at[0:size], sem)
+    fetch.start()
     y = lax.broadcasted_iota(jnp.int32, (rows, cells), 0).astype(jnp.float32)
     z = lax.broadcasted_iota(jnp.int32, (rows, cells), 1).astype(jnp.float32)
     along = laser[1] * ((y - (rows - 1) / 2.0) * spacing) + laser[2] * ((z - (cells - 1) / 2.0) * spacing)
     for i in range(planes):
         x = ((me * planes + i).astype(jnp.float32) - (domains * planes - 1) / 2.0) * spacing
         v[i] = potential[i] + laser[0] * x + along + 3.0 * kinetic[0]
+    fetch.wait()
+    message[size : size + 8, :] = partial_sums(planes, rows, slots, me, atoms, anchor, message, proj, sums)
 
 
 def step_kernel(planes, rows, slots, factor, last, scale, *refs):
@@ -230,19 +239,23 @@
         message[size : size + 8, :] = partial_sums(planes, rows, slots, me, atoms, anchor, message, proj, sums)
 
 
-def current_kernel(planes, rows, scale, where, u, real_pair, real_other, imag_pair, imag_other, flow, padded):
-    halos = ((real_pair, real_other), (imag_pair, imag_other))
+def current_kernel(
+    planes, rows, scale, where, spot, real, imag, real_pair, real_other, imag_pair, imag_other, keep, send, padded
+):
+    halos = ((real, real_pair, real_other), (imag, imag_pair, imag_other))
     pair_w, other_w = halo_weights(lax.rem(where[0], 2) == 0, planes, slope, -1.0)
+    lower = lax.rem(spot[0], 2) == 0
 
     def plane_of(ref, i):
         return ref[i * rows : (i + 1) * rows, :]
 
     for ch in range(2):
-        fill_padded(padded.at[ch], planes, rows, lambda i, ch=ch: plane_of(u.at[ch], i))
+        fill_padded(padded.at[ch], planes, rows, lambda i, ch=ch: plane_of(halos[ch][0], i))
+    flows = {}
     for i in range(planes):
         gradients = []
         for ch in range(2):
-            own, (pair, other) = u.at[ch], halos[ch]
+            own, pair, other = halos[ch]
             centre = plane_of(own, i)
             along_x = along_y = along_z = 0.0
             for m in (1, 2, 3, 4):
@@ -257,20 +270,42 @@
             for j in range(planes):
                 along_x = along_x + pair_w[i, j] * plane_of(pair, j) + other_w[i, j] * plane_of(other, j)
             gradients.append((along_x, along_y, along_z))
+        half = planes // 2
         for c in range(3):
-            flow[c * planes + i] = scale * (
-                plane_of(u.at[0], i) * gradients[1][c] - plane_of(u.at[1], i) * gradients[0][c]
-            )
+            flow = scale * (plane_of(real, i) * gradients[1][c] - plane_of(imag, i) * gradients[0][c])
+            at = c * half + i % half
+            if i < half:
+                keep[at] = flow
+            else:
+                first = keep[at]
+                keep[at] = jnp.where(lower, first, flow)
+                send[at] = jnp.where(lower, flow, first)
+
+
+def merge_kernel(spot, held, got, keep, send):
+    lower = lax.rem(spot[0] // 2, 2) == 0
+    for c in range(3):
+        first = held[2 * c] + got[2 * c]
+        second = held[2 * c + 1] + got[2 * c + 1]
+        keep[c] = jnp.where(lower, first, second)
+        send[c] = jnp.where(lower, second, first)
+
+
+def plane_kept(source):
+    x = source // RUN
+    return 2 * (x % 2) + x // 2 % 2
 
 
 def gather_kernel(planes, got, density, current):
-    total = got[0]
-    for source in range(1, got.shape[0]):
-        total = total + got[source]
-    for i in range(planes):
-        density[i] = total[i : i + 1]
+    totals = [None] * planes
+    for source in range(got.shape[0]):
+        p = plane_kept(source)
+        totals[p] = got[source] if totals[p] is None else totals[p] + got[source]
+    everywhere = totals[0] + totals[1] + totals[2] + totals[3]
+    for i in range(planes):
+        density[i] = everywhere[i : i + 1]
         for c in range(3):
-            current[c, i] = total[planes * (c + 1) + i : planes * (c + 1) + i + 1]
+            current[c, i] = totals[i][planes + c : planes + c + 1]
 
 
 def body(orbitals, potential, laser_field, box_anchor, domain_atoms, projector, strength):
@@ -282,6 +317,7 @@
     me = lax.axis_index("dom")
     where = me.reshape(1).astype(jnp.int32)
     places = (where, domain_atoms, box_anchor)
+    spot = (lax.axis_index("orb") // RUN).reshape(1).astype(jnp.int32)
     scale = 2.0 / orbs
 
     pairs = [(i, i ^ 1) for i in range(domains)]
@@ -291,11 +327,11 @@
         other = lax.ppermute(value, "dom", others)
         return lax.ppermute(value, "dom", pairs), other
 
-    def kernel(function, name, out, scalars, arrays, scratch):
+    def kernel(function, name, out, scalars, arrays, scratch, far=0):
         return pl.pallas_call(
             function,
             out_shape=out,
-            in_specs=[SMEM] * scalars + [VMEM] * arrays,
+            in_specs=[SMEM] * scalars + [VMEM] * arrays + [ANY] * far,
             out_specs=jax.tree.map(lambda _: VMEM, out),
             scratch_shapes=scratch,
             compiler_params=pltpu.CompilerParams(vmem_limit_bytes=32 * 1024 * 1024),
@@ -309,13 +345,15 @@
         functools.partial(prepare_kernel, planes, rows, slots),
         "prepare_real",
         (f32(PROJ * BOX, BOX, cells), f32(8, cells), f32(size + 8, cells)),
-        4, 2, [sums],
+        4, 0,
+        [sums, pltpu.VMEM((PROJ, BOX**3), jnp.float32), pltpu.SemaphoreType.DMA((2,))],
+        2,
     )(*places, strength, projector, u)
     v, second = kernel(
         functools.partial(second_kernel, planes, rows, slots, domains),
         "prepare_imag",
         (f32(planes, rows, cells), f32(size + 8, cells)),
-        4, 3, [sums],
+        4, 2, [sums, pltpu.SemaphoreType.DMA], 1,
     )(*places, laser_field, potential, proj, u)
 
     def step(order, channel, halos, evolved, held=None):
@@ -351,13 +389,21 @@
             else:
                 evolved, density = step(order, channel, halos[channel], totals[to], totals[1 - to])
         if order == 1:
-            flow = kernel(
+            halos_in = halos
+        if order == 2:
+            _, spot = lax.optimization_barrier((terms[0], spot))
+            half = f32(3 * planes // 2, rows, cells)
+            keep, send = kernel(
                 functools.partial(current_kernel, planes, rows, scale),
-                "current_part", f32(3 * planes, rows, cells), 1, 5,
+                "current_part", (half, half), 2, 6,
                 [pltpu.VMEM((2, planes, rows + 16, cells), jnp.float32)],
-            )(where, u, *halos[0][1:], *halos[1][1:])
-
-    fields = jnp.concatenate([density, flow], axis=0)
+            )(where, spot, first, second, *halos_in[0][1:], *halos_in[1][1:])
+            got = lax.ppermute(send, "orb", [(i, (i // RUN ^ 1) * RUN + i % RUN) for i in range(orbs)])
+            quarter = f32(3 * planes // 4, rows, cells)
+            keep, send = kernel(merge_kernel, "merge_current", (quarter, quarter), 1, 2, [])(spot, keep, got)
+            got = lax.ppermute(send, "orb", [(i, (i // RUN ^ 2) * RUN + i % RUN) for i in range(orbs)])
+
+    fields = jnp.concatenate([density, keep + got], axis=0)
     fields = jnp.moveaxis(fields, 1, 0)
     fields = lax.all_to_all(fields, "orb", 0, 0, tiled=True)
     density, current = kernel(

time: 127 us -> 127 us (level)
  starting transfers between devices: 60 us -> 72.5 us
  blocking collectives: 37.7 us -> 25.8 us
    all_to_all x1, blocking collectives: 37.7 us -> 25.8 us  [body(): fields = lax.all_to_all(fields, 'orb', 0, 0, tiled=True)]
    ppermute x8, starting transfers between devices: 17.7 us -> 25.9 us  [exchange(): return (lax.ppermute(value, 'dom', pairs), other)]
    ppermute x0 -> x2, starting transfers between devices: none -> 7.48 us  [the longest x1 4.36 us: body(): lax.ppermute(send, 'orb', [(i, (i // RUN ^ 2) * RUN + i % RUN) for i in r...]
    ppermute x8, starting transfers between devices: 42.3 us -> 39.2 us  [exchange(): other = lax.ppermute(value, 'dom', others)]
  transfers between devices with their start and end apart: 16 -> 18, of which waited for: 1 -> 0; matrix products, arithmetic and copies ran while one was open for 0% -> 0% of each run, Pallas kernels for 15% -> 17%
where the time goes in v3:
time: 127 us; the launch traced here: 126 us
  starting transfers between devices  72.5 us (57%)
  blocking collectives  25.8 us (20%)
  Pallas kernels  24 us (19%)
  local copies, waits for them, and re-layouts  2.61 us (2%)
    ppermute x8, starting transfers between devices, exchange(): other = lax.ppermute(value, 'dom', others)  39.2 us
    ppermute x8, starting transfers between devices, exchange(): return (lax.ppermute(value, 'dom', pairs), other)  25.9 us
    all_to_all x1, blocking collectives, body(): fields = lax.all_to_all(fields, 'orb', 0, 0, tiled=True)  25.8 us
    pallas_call x8, Pallas kernels, step(): kernel(functools.partial(step_kernel, planes, rows, slots, sign * time_st...  18.9 us
    ppermute x1, starting transfers between devices, body(): lax.ppermute(send, 'orb', [(i, (i // RUN ^ 2) * RUN + i % RUN) for i in r...  4.36 us
    ppermute x1, starting transfers between devices, body(): lax.ppermute(send, 'orb', [(i, (i // RUN ^ 1) * RUN + i % RUN) for i in r...  3.12 us
  transfers between devices with their start and end apart: 18, of which 0 were waited for; matrix products, arithmetic and copies ran while one was open for 0% of the time, Pallas kernels for 17%

profile of v3, /device:TPU:1, one launch (start us, length us, event | category | flops | bytes accessed | tf_op | source)
XLA Modules:
  0.0 126.2 jit_solution(13674833762549645425)
XLA Ops:
  0.6 0.0 copy-start.1
  0.6 0.0 copy-start.2
  0.7 0.0 copy-start.5
  0.7 0.7 copy-done.1
  1.3 0.0 copy-done.2
  1.3 0.0 copy-done.5
  1.3 1.0 copy-done
  2.3 0.7 copy-done.4
  3.0 1.7 %prepare_real.1 = (f32[32,8,128]{2,1,0:T(8,128)S(1)}, f32[8,128]{1,0:T(8,128)S(1)}, f32[392,128]{1,0:T(8,128)S(1)}) custom-call(s32[1]{0:T(128)} %bitcast.where.refs_0_, s32[8,32]{1,0:T(8,128)S(1)} %copy-done.1, s32[3,128]{1,0:T(4,128)S(1)} %copy-done.2, f32[4]{0:T(128)S(1)} %copy-done.5, f32[4,512]{1,0:T(4,128)S(1)} %copy-done.4, f32[2,384,128]{2,1,0:T(8,128)S(1)} %bitcast.8), custom_call_target="tpu_custom_call" | custom-call | flops 8000000 | bytes 10000000 | tf_op jit(solution)/shard_map/prepare_real/pallas_call | solution.py:344
  4.7 0.0 copy-start.6
  4.8 12.4 %collective-permute-start.4 = (f32[392,128]{1,0:T(8,128)S(1)}, f32[392,128]{1,0:T(8,128)S(1)}, u32[]{:S(2)}, u32[]{:S(2)}) collective-permute-start(f32[392,128]{1,0:T(8,128)S(1)} %get-tuple-element.33.refs_9_.refs_3_.real), channel_id=1, source_target_pairs={{0,1},{1,0},{2,3},{3,2},{4,5},{5,4},{6,7},{7,6},{8,9},{9,8},{10,11... | collective-permute-start | bytes 602120 | tf_op jit(solution)/shard_map/ppermute | solution.py:328
  17.2 1.9 %collective-permute-start.5 = (f32[392,128]{1,0:T(8,128)S(1)}, f32[392,128]{1,0:T(8,128)S(1)}, u32[]{:S(2)}, u32[]{:S(2)}) collective-permute-start(f32[392,128]{1,0:T(8,128)S(1)} %get-tuple-element.33.refs_9_.refs_3_.real), channel_id=1, source_target_pairs={{1,2},{3,4},{5,6},{2,1},{4,3},{6,5},{9,10},{11,12},{13,14},{10,9},... | collective-permute-start | bytes 602120 | tf_op jit(solution)/shard_map/ppermute | solution.py:327
  19.1 0.0 copy-done.3
  19.1 0.0 copy-done.6
  19.1 1.5 %prepare_imag.1 = (f32[4,96,128]{2,1,0:T(8,128)S(1)}, f32[392,128]{1,0:T(8,128)S(1)}) custom-call(s32[1]{0:T(128)} %bitcast.where.refs_0_, s32[8,32]{1,0:T(8,128)S(1)} %copy-done.1, s32[3,128]{1,0:T(4,128)S(1)} %copy-done.2, f32[3]{0:T(128)S(1)} %copy-done.6, f32[4,96,128]{2,1,0:T(8,128)S(1)} %copy-done.3, f32[32,8,128]{2,1,0:T(8,128)S(1)} %get-tuple-element.29.proj.refs_8_, ...), custom_call_target="tpu_custom_call" | custom-call | flops 8000000 | bytes 10000000 | tf_op jit(solution)/shard_map/prepare_imag/pallas_call | solution.py:352
  20.6 1.9 %collective-permute-start = (f32[392,128]{1,0:T(8,128)S(1)}, f32[392,128]{1,0:T(8,128)S(1)}, u32[]{:S(2)}, u32[]{:S(2)}) collective-permute-start(f32[392,128]{1,0:T(8,128)S(1)} %get-tuple-element.30.refs_3_.refs_9_.imag), channel_id=1, source_target_pairs={{0,1},{1,0},{2,3},{3,2},{4,5},{5,4},{6,7},{7,6},{8,9},{9,8},{10,11... | collective-permute-start | bytes 602120 | tf_op jit(solution)/shard_map/ppermute | solution.py:328
  22.6 5.8 %collective-permute-start.1 = (f32[392,128]{1,0:T(8,128)S(1)}, f32[392,128]{1,0:T(8,128)S(1)}, u32[]{:S(2)}, u32[]{:S(2)}) collective-permute-start(f32[392,128]{1,0:T(8,128)S(1)} %get-tuple-element.30.refs_3_.refs_9_.imag), channel_id=1, source_target_pairs={{1,2},{3,4},{5,6},{2,1},{4,3},{6,5},{9,10},{11,12},{13,14},{10,9},... | collective-permute-start | bytes 602120 | tf_op jit(solution)/shard_map/ppermute | solution.py:327
  28.4 0.0 collective-permute-done.4.refs_4_.real_pair
  28.4 0.0 collective-permute-done.5.refs_5_.real_other
  28.4 2.4 %taylor_step.9 = (f32[392,128]{1,0:T(8,128)S(1)}, f32[384,128]{1,0:T(8,128)S(1)}) custom-call(s32[1]{0:T(128)} %bitcast.where.refs_0_, s32[8,32]{1,0:T(8,128)S(1)} %copy-done.1, s32[3,128]{1,0:T(4,128)S(1)} %copy-done.2, f32[392,128]{1,0:T(8,128)S(1)} %get-tuple-element.33.refs_9_.refs_3_.real, f32[392,128]{1,0:T(8,128)S(1)} %collective-permute-done.4.refs_4_.real_pair, ...), custom_call_target="tpu_custom_call" | custom-call | flops 8000000 | bytes 10000000 | tf_op jit(solution)/shard_map/taylor_step/pallas_call | solution.py:368
  30.8 1.9 %collective-permute-start.8 = (f32[392,128]{1,0:T(8,128)S(1)}, f32[392,128]{1,0:T(8,128)S(1)}, u32[]{:S(2)}, u32[]{:S(2)}) collective-permute-start(f32[392,128]{1,0:T(8,128)S(1)} %get-tuple-element.37.refs_3_), channel_id=1, source_target_pairs={{0,1},{1,0},{2,3},{3,2},{4,5},{5,4},{6,7},{7,6},{8,9},{9,8},{10,11... | collective-permute-start | bytes 602120 | tf_op jit(solution)/shard_map/ppermute | solution.py:328
  32.7 5.9 %collective-permute-start.9 = (f32[392,128]{1,0:T(8,128)S(1)}, f32[392,128]{1,0:T(8,128)S(1)}, u32[]{:S(2)}, u32[]{:S(2)}) collective-permute-start(f32[392,128]{1,0:T(8,128)S(1)} %get-tuple-element.37.refs_3_), channel_id=1, source_target_pairs={{1,2},{3,4},{5,6},{2,1},{4,3},{6,5},{9,10},{11,12},{13,14},{10,9},... | collective-permute-start | bytes 602120 | tf_op jit(solution)/shard_map/ppermute | solution.py:327
  38.6 0.0 collective-permute-done.refs_4_.imag_pair
  38.6 0.0 collective-permute-done.1.refs_5_.imag_other
  38.6 2.4 %taylor_step.8 = (f32[392,128]{1,0:T(8,128)S(1)}, f32[384,128]{1,0:T(8,128)S(1)}) custom-call(s32[1]{0:T(128)} %bitcast.where.refs_0_, s32[8,32]{1,0:T(8,128)S(1)} %copy-done.1, s32[3,128]{1,0:T(4,128)S(1)} %copy-done.2, f32[392,128]{1,0:T(8,128)S(1)} %get-tuple-element.30.refs_3_.refs_9_.imag, f32[392,128]{1,0:T(8,128)S(1)} %collective-permute-done.refs_4_.imag_pair, ...), custom_call_target="tpu_custom_call" | custom-call | flops 8000000 | bytes 10000000 | tf_op jit(solution)/shard_map/taylor_step/pallas_call | solution.py:368
  41.0 1.9 %collective-permute-start.2 = (f32[392,128]{1,0:T(8,128)S(1)}, f32[392,128]{1,0:T(8,128)S(1)}, u32[]{:S(2)}, u32[]{:S(2)}) collective-permute-start(f32[392,128]{1,0:T(8,128)S(1)} %get-tuple-element.34.refs_3_), channel_id=1, source_target_pairs={{0,1},{1,0},{2,3},{3,2},{4,5},{5,4},{6,7},{7,6},{8,9},{9,8},{10,11... | collective-permute-start | bytes 602120 | tf_op jit(solution)/shard_map/ppermute | solution.py:328
  43.0 5.5 %collective-permute-start.3 = (f32[392,128]{1,0:T(8,128)S(1)}, f32[392,128]{1,0:T(8,128)S(1)}, u32[]{:S(2)}, u32[]{:S(2)}) collective-permute-start(f32[392,128]{1,0:T(8,128)S(1)} %get-tuple-element.34.refs_3_), channel_id=1, source_target_pairs={{1,2},{3,4},{5,6},{2,1},{4,3},{6,5},{9,10},{11,12},{13,14},{10,9},... | collective-permute-start | bytes 602120 | tf_op jit(solution)/shard_map/ppermute | solution.py:327
  48.5 0.0 collective-permute-done.8.refs_4_
  48.6 0.0 collective-permute-done.9.refs_5_
  48.6 2.4 %taylor_step.11 = (f32[392,128]{1,0:T(8,128)S(1)}, f32[384,128]{1,0:T(8,128)S(1)}) custom-call(s32[1]{0:T(128)} %bitcast.where.refs_0_, s32[8,32]{1,0:T(8,128)S(1)} %copy-done.1, s32[3,128]{1,0:T(4,128)S(1)} %copy-done.2, f32[392,128]{1,0:T(8,128)S(1)} %get-tuple-element.37.refs_3_, f32[392,128]{1,0:T(8,128)S(1)} %collective-permute-done.8.refs_4_, ...), custom_call_target="tpu_custom_call" | custom-call | flops 8000000 | bytes 10000000 | tf_op jit(solution)/shard_map/taylor_step/pallas_call | solution.py:368
  50.9 1.2 current_part.1
  52.2 3.1 %collective-permute-start.16 = (f32[6,96,128]{2,1,0:T(8,128)S(1)}, f32[6,96,128]{2,1,0:T(8,128)S(1)}, u32[]{:S(2)}, u32[]{:S(2)}) collective-permute-start(f32[6,96,128]{2,1,0:T(8,128)S(1)} %get-tuple-element.50), channel_id=1, source_target_pairs={{0,24},{8,32},{16,40},{24,0},{32,8},{40,16},{48,72},{56,80},{64,88... | collective-permute-start | bytes 884744 | tf_op jit(solution)/shard_map/ppermute | solution.py:401
  55.3 1.9 %collective-permute-start.12 = (f32[392,128]{1,0:T(8,128)S(1)}, f32[392,128]{1,0:T(8,128)S(1)}, u32[]{:S(2)}, u32[]{:S(2)}) collective-permute-start(f32[392,128]{1,0:T(8,128)S(1)} %get-tuple-element.41.refs_3_), channel_id=1, source_target_pairs={{0,1},{1,0},{2,3},{3,2},{4,5},{5,4},{6,7},{7,6},{8,9},{9,8},{10,11... | collective-permute-start | bytes 602120 | tf_op jit(solution)/shard_map/ppermute | solution.py:328
  57.2 4.5 %collective-permute-start.13 = (f32[392,128]{1,0:T(8,128)S(1)}, f32[392,128]{1,0:T(8,128)S(1)}, u32[]{:S(2)}, u32[]{:S(2)}) collective-permute-start(f32[392,128]{1,0:T(8,128)S(1)} %get-tuple-element.41.refs_3_), channel_id=1, source_target_pairs={{1,2},{3,4},{5,6},{2,1},{4,3},{6,5},{9,10},{11,12},{13,14},{10,9},... | collective-permute-start | bytes 602120 | tf_op jit(solution)/shard_map/ppermute | solution.py:327
  61.7 0.0 collective-permute-done.2.refs_4_
  61.8 0.0 collective-permute-done.3.refs_5_
  61.8 2.4 %taylor_step.10 = (f32[392,128]{1,0:T(8,128)S(1)}, f32[384,128]{1,0:T(8,128)S(1)}) custom-call(s32[1]{0:T(128)} %bitcast.where.refs_0_, s32[8,32]{1,0:T(8,128)S(1)} %copy-done.1, s32[3,128]{1,0:T(4,128)S(1)} %copy-done.2, f32[392,128]{1,0:T(8,128)S(1)} %get-tuple-element.34.refs_3_, f32[392,128]{1,0:T(8,128)S(1)} %collective-permute-done.2.refs_4_, ...), custom_call_target="tpu_custom_call" | custom-call | flops 8000000 | bytes 10000000 | tf_op jit(solution)/shard_map/taylor_step/pallas_call | solution.py:368
  64.2 1.9 %collective-permute-start.6 = (f32[392,128]{1,0:T(8,128)S(1)}, f32[392,128]{1,0:T(8,128)S(1)}, u32[]{:S(2)}, u32[]{:S(2)}) collective-permute-start(f32[392,128]{1,0:T(8,128)S(1)} %get-tuple-element.36.refs_3_), channel_id=1, source_target_pairs={{0,1},{1,0},{2,3},{3,2},{4,5},{5,4},{6,7},{7,6},{8,9},{9,8},{10,11... | collective-permute-start | bytes 602120 | tf_op jit(solution)/shard_map/ppermute | solution.py:328
  66.1 5.8 %collective-permute-start.7 = (f32[392,128]{1,0:T(8,128)S(1)}, f32[392,128]{1,0:T(8,128)S(1)}, u32[]{:S(2)}, u32[]{:S(2)}) collective-permute-start(f32[392,128]{1,0:T(8,128)S(1)} %get-tuple-element.36.refs_3_), channel_id=1, source_target_pairs={{1,2},{3,4},{5,6},{2,1},{4,3},{6,5},{9,10},{11,12},{13,14},{10,9},... | collective-permute-start | bytes 602120 | tf_op jit(solution)/shard_map/ppermute | solution.py:327
  71.9 0.0 collective-permute-done.12.refs_4_
  71.9 0.0 collective-permute-done.13.refs_5_
  71.9 2.4 %taylor_step.13 = (f32[392,128]{1,0:T(8,128)S(1)}, f32[384,128]{1,0:T(8,128)S(1)}) custom-call(s32[1]{0:T(128)} %bitcast.where.refs_0_, s32[8,32]{1,0:T(8,128)S(1)} %copy-done.1, s32[3,128]{1,0:T(4,128)S(1)} %copy-done.2, f32[392,128]{1,0:T(8,128)S(1)} %get-tuple-element.41.refs_3_, f32[392,128]{1,0:T(8,128)S(1)} %collective-permute-done.12.refs_4_, ...), custom_call_target="tpu_custom_call" | custom-call | flops 8000000 | bytes 10000000 | tf_op jit(solution)/shard_map/taylor_step/pallas_call | solution.py:368
  74.3 1.9 %collective-permute-start.14 = (f32[392,128]{1,0:T(8,128)S(1)}, f32[392,128]{1,0:T(8,128)S(1)}, u32[]{:S(2)}, u32[]{:S(2)}) collective-permute-start(f32[392,128]{1,0:T(8,128)S(1)} %get-tuple-element.44.refs_3_), channel_id=1, source_target_pairs={{0,1},{1,0},{2,3},{3,2},{4,5},{5,4},{6,7},{7,6},{8,9},{9,8},{10,11... | collective-permute-start | bytes 602120 | tf_op jit(solution)/shard_map/ppermute | solution.py:328
  76.3 3.7 %collective-permute-start.15 = (f32[392,128]{1,0:T(8,128)S(1)}, f32[392,128]{1,0:T(8,128)S(1)}, u32[]{:S(2)}, u32[]{:S(2)}) collective-permute-start(f32[392,128]{1,0:T(8,128)S(1)} %get-tuple-element.44.refs_3_), channel_id=1, source_target_pairs={{1,2},{3,4},{5,6},{2,1},{4,3},{6,5},{9,10},{11,12},{13,14},{10,9},... | collective-permute-start | bytes 602120 | tf_op jit(solution)/shard_map/ppermute | solution.py:327
  79.9 0.0 collective-permute-done.6.refs_4_
  79.9 0.0 collective-permute-done.7.refs_5_
  79.9 2.4 %taylor_step.12 = (f32[392,128]{1,0:T(8,128)S(1)}, f32[384,128]{1,0:T(8,128)S(1)}) custom-call(s32[1]{0:T(128)} %bitcast.where.refs_0_, s32[8,32]{1,0:T(8,128)S(1)} %copy-done.1, s32[3,128]{1,0:T(4,128)S(1)} %copy-done.2, f32[392,128]{1,0:T(8,128)S(1)} %get-tuple-element.36.refs_3_, f32[392,128]{1,0:T(8,128)S(1)} %collective-permute-done.6.refs_4_, ...), custom_call_target="tpu_custom_call" | custom-call | flops 8000000 | bytes 10000000 | tf_op jit(solution)/shard_map/taylor_step/pallas_call | solution.py:368
  82.4 1.9 %collective-permute-start.10 = (f32[392,128]{1,0:T(8,128)S(1)}, f32[392,128]{1,0:T(8,128)S(1)}, u32[]{:S(2)}, u32[]{:S(2)}) collective-permute-start(f32[392,128]{1,0:T(8,128)S(1)} %get-tuple-element.40.refs_3_), channel_id=1, source_target_pairs={{0,1},{1,0},{2,3},{3,2},{4,5},{5,4},{6,7},{7,6},{8,9},{9,8},{10,11... | collective-permute-start | bytes 602120 | tf_op jit(solution)/shard_map/ppermute | solution.py:328
  84.3 6.1 %collective-permute-start.11 = (f32[392,128]{1,0:T(8,128)S(1)}, f32[392,128]{1,0:T(8,128)S(1)}, u32[]{:S(2)}, u32[]{:S(2)}) collective-permute-start(f32[392,128]{1,0:T(8,128)S(1)} %get-tuple-element.40.refs_3_), channel_id=1, source_target_pairs={{1,2},{3,4},{5,6},{2,1},{4,3},{6,5},{9,10},{11,12},{13,14},{10,9},... | collective-permute-start | bytes 602120 | tf_op jit(solution)/shard_map/ppermute | solution.py:327
  90.4 0.0 collective-permute-done.16.got
  90.4 0.1 copy.10
  90.6 4.4 %collective-permute-start.17 = (f32[3,96,128]{2,0,1:T(4,128)S(1)}, f32[3,96,128]{2,0,1:T(4,128)S(1)}, u32[]{:S(2)}, u32[]{:S(2)}) collective-permute-start(f32[3,96,128]{2,0,1:T(4,128)S(1)} %copy.10), channel_id=1, source_target_pairs={{0,48},{8,56},{16,64},{24,72},{32,80},{40,88},{48,0},{56,8},{64,16... | collective-permute-start | bytes 442376 | tf_op jit(solution)/shard_map/ppermute | solution.py:404
  94.9 0.0 collective-permute-done.14.refs_4_
  94.9 0.0 collective-permute-done.15.refs_5_
  94.9 1.8 %taylor_step.14.refs_10_ = f32[384,128]{1,0:T(8,128)S(1)} custom-call(s32[1]{0:T(128)} %bitcast.where.refs_0_, s32[8,32]{1,0:T(8,128)S(1)} %copy-done.1, s32[3,128]{1,0:T(4,128)S(1)} %copy-done.2, f32[392,128]{1,0:T(8,128)S(1)} %get-tuple-element.44.refs_3_, f32[392,128]{1,0:T(8,128)S(1)} %collective-permute-done.14.refs_4_, ...), custom_call_target="tpu_custom_call" | custom-call | flops 8000000 | bytes 10000000 | tf_op jit(solution)/shard_map/taylor_step/pallas_call | solution.py:368
  96.8 0.0 collective-permute-done.10.refs_4_
  96.8 0.0 collective-permute-done.11.refs_5_
  96.8 2.6 %taylor_step.15 = (f32[2,384,128]{2,1,0:T(8,128)}, f32[4,96,128]{2,1,0:T(8,128)S(1)}) custom-call(s32[1]{0:T(128)} %bitcast.where.refs_0_, s32[8,32]{1,0:T(8,128)S(1)} %copy-done.1, s32[3,128]{1,0:T(4,128)S(1)} %copy-done.2, f32[392,128]{1,0:T(8,128)S(1)} %get-tuple-element.40.refs_3_, f32[392,128]{1,0:T(8,128)S(1)} %collective-permute-done.10.refs_4_, ...), custom_call_target="tpu_custom_call" | custom-call | flops 8000000 | bytes 10000000 | tf_op jit(solution)/shard_map/taylor_step/pallas_call | solution.py:368
  99.4 0.1 copy.12
  99.6 0.0 collective-permute-done.17
  99.6 0.1 copy_add_fusion
  99.7 0.1 maximum_bitcast_fusion
  99.8 25.8 %all_to_all.5.got = f32[96,7,128]{2,1,0:T(8,128)S(1)} all-to-all(f32[96,7,128]{2,1,0:T(8,128)S(1)} %maximum_bitcast_fusion), channel_id=1, replica_groups=mesh['orb'=96,'dom'=8] {'orb'}, dimensions={0} | all-to-all | bytes 688128 | tf_op jit(solution)/shard_map/all_to_all | solution.py:408
  125.6 0.6 sum_over_orb.1
  (4 shorter events, 0.0 us)
Async XLA Ops:
  0.6 0.7 copy-start.1
  0.6 0.7 copy-start.2
  0.7 0.7 copy-start.5
  1.3 1.0 copy-start
  2.3 0.7 copy-start.4
  3.0 16.1 %copy-start.3 = (f32[4,96,128]{2,1,0:T(8,128)S(1)}, f32[4,96,128]{2,1,0:T(8,128)}, u32[]{:S(2)}) copy-start(f32[4,96,128]{2,1,0:T(8,128)} %potential.1) | copy-start | bytes 589828
  4.7 14.4 %copy-start.6 = (f32[3]{0:T(128)S(1)}, f32[3]{0:T(128)}, u32[]{:S(2)}) copy-start(f32[3]{0:T(128)} %laser.1) | copy-start | bytes 40
  4.8 23.6 %collective-permute-start.4 = (f32[392,128]{1,0:T(8,128)S(1)}, f32[392,128]{1,0:T(8,128)S(1)}, u32[]{:S(2)}, u32[]{:S(2)}) collective-permute-start(f32[392,128]{1,0:T(8,128)S(1)} %get-tuple-element.33.refs_9_.refs_3_.real), channel_id=1, source_target_pairs={{0,1},{1,0},{2,3},{3,2},{4,5},{5,4},{6,7},{7,6},{8,9},{9,8},{10,11... | collective-permute-start | bytes 602120 | tf_op jit(solution)/shard_map/ppermute | solution.py:328
  17.2 11.2 %collective-permute-start.5 = (f32[392,128]{1,0:T(8,128)S(1)}, f32[392,128]{1,0:T(8,128)S(1)}, u32[]{:S(2)}, u32[]{:S(2)}) collective-permute-start(f32[392,128]{1,0:T(8,128)S(1)} %get-tuple-element.33.refs_9_.refs_3_.real), channel_id=1, source_target_pairs={{1,2},{3,4},{5,6},{2,1},{4,3},{6,5},{9,10},{11,12},{13,14},{10,9},... | collective-permute-start | bytes 602120 | tf_op jit(solution)/shard_map/ppermute | solution.py:327
  20.6 18.0 %collective-permute-start = (f32[392,128]{1,0:T(8,128)S(1)}, f32[392,128]{1,0:T(8,128)S(1)}, u32[]{:S(2)}, u32[]{:S(2)}) collective-permute-start(f32[392,128]{1,0:T(8,128)S(1)} %get-tuple-element.30.refs_3_.refs_9_.imag), channel_id=1, source_target_pairs={{0,1},{1,0},{2,3},{3,2},{4,5},{5,4},{6,7},{7,6},{8,9},{9,8},{10,11... | collective-permute-start | bytes 602120 | tf_op jit(solution)/shard_map/ppermute | solution.py:328
  22.6 16.0 %collective-permute-start.1 = (f32[392,128]{1,0:T(8,128)S(1)}, f32[392,128]{1,0:T(8,128)S(1)}, u32[]{:S(2)}, u32[]{:S(2)}) collective-permute-start(f32[392,128]{1,0:T(8,128)S(1)} %get-tuple-element.30.refs_3_.refs_9_.imag), channel_id=1, source_target_pairs={{1,2},{3,4},{5,6},{2,1},{4,3},{6,5},{9,10},{11,12},{13,14},{10,9},... | collective-permute-start | bytes 602120 | tf_op jit(solution)/shard_map/ppermute | solution.py:327
  30.8 17.8 %collective-permute-start.8 = (f32[392,128]{1,0:T(8,128)S(1)}, f32[392,128]{1,0:T(8,128)S(1)}, u32[]{:S(2)}, u32[]{:S(2)}) collective-permute-start(f32[392,128]{1,0:T(8,128)S(1)} %get-tuple-element.37.refs_3_), channel_id=1, source_target_pairs={{0,1},{1,0},{2,3},{3,2},{4,5},{5,4},{6,7},{7,6},{8,9},{9,8},{10,11... | collective-permute-start | bytes 602120 | tf_op jit(solution)/shard_map/ppermute | solution.py:328
  32.7 15.9 %collective-permute-start.9 = (f32[392,128]{1,0:T(8,128)S(1)}, f32[392,128]{1,0:T(8,128)S(1)}, u32[]{:S(2)}, u32[]{:S(2)}) collective-permute-start(f32[392,128]{1,0:T(8,128)S(1)} %get-tuple-element.37.refs_3_), channel_id=1, source_target_pairs={{1,2},{3,4},{5,6},{2,1},{4,3},{6,5},{9,10},{11,12},{13,14},{10,9},... | collective-permute-start | bytes 602120 | tf_op jit(solution)/shard_map/ppermute | solution.py:327
  41.0 20.7 %collective-permute-start.2 = (f32[392,128]{1,0:T(8,128)S(1)}, f32[392,128]{1,0:T(8,128)S(1)}, u32[]{:S(2)}, u32[]{:S(2)}) collective-permute-start(f32[392,128]{1,0:T(8,128)S(1)} %get-tuple-element.34.refs_3_), channel_id=1, source_target_pairs={{0,1},{1,0},{2,3},{3,2},{4,5},{5,4},{6,7},{7,6},{8,9},{9,8},{10,11... | collective-permute-start | bytes 602120 | tf_op jit(solution)/shard_map/ppermute | solution.py:328
  43.0 18.8 %collective-permute-start.3 = (f32[392,128]{1,0:T(8,128)S(1)}, f32[392,128]{1,0:T(8,128)S(1)}, u32[]{:S(2)}, u32[]{:S(2)}) collective-permute-start(f32[392,128]{1,0:T(8,128)S(1)} %get-tuple-element.34.refs_3_), channel_id=1, source_target_pairs={{1,2},{3,4},{5,6},{2,1},{4,3},{6,5},{9,10},{11,12},{13,14},{10,9},... | collective-permute-start | bytes 602120 | tf_op jit(solution)/shard_map/ppermute | solution.py:327
  52.2 38.2 %collective-permute-start.16 = (f32[6,96,128]{2,1,0:T(8,128)S(1)}, f32[6,96,128]{2,1,0:T(8,128)S(1)}, u32[]{:S(2)}, u32[]{:S(2)}) collective-permute-start(f32[6,96,128]{2,1,0:T(8,128)S(1)} %get-tuple-element.50), channel_id=1, source_target_pairs={{0,24},{8,32},{16,40},{24,0},{32,8},{40,16},{48,72},{56,80},{64,88... | collective-permute-start | bytes 884744 | tf_op jit(solution)/shard_map/ppermute | solution.py:401
  55.3 16.6 %collective-permute-start.12 = (f32[392,128]{1,0:T(8,128)S(1)}, f32[392,128]{1,0:T(8,128)S(1)}, u32[]{:S(2)}, u32[]{:S(2)}) collective-permute-start(f32[392,128]{1,0:T(8,128)S(1)} %get-tuple-element.41.refs_3_), channel_id=1, source_target_pairs={{0,1},{1,0},{2,3},{3,2},{4,5},{5,4},{6,7},{7,6},{8,9},{9,8},{10,11... | collective-permute-start | bytes 602120 | tf_op jit(solution)/shard_map/ppermute | solution.py:328
  57.2 14.7 %collective-permute-start.13 = (f32[392,128]{1,0:T(8,128)S(1)}, f32[392,128]{1,0:T(8,128)S(1)}, u32[]{:S(2)}, u32[]{:S(2)}) collective-permute-start(f32[392,128]{1,0:T(8,128)S(1)} %get-tuple-element.41.refs_3_), channel_id=1, source_target_pairs={{1,2},{3,4},{5,6},{2,1},{4,3},{6,5},{9,10},{11,12},{13,14},{10,9},... | collective-permute-start | bytes 602120 | tf_op jit(solution)/shard_map/ppermute | solution.py:327
  64.2 15.7 %collective-permute-start.6 = (f32[392,128]{1,0:T(8,128)S(1)}, f32[392,128]{1,0:T(8,128)S(1)}, u32[]{:S(2)}, u32[]{:S(2)}) collective-permute-start(f32[392,128]{1,0:T(8,128)S(1)} %get-tuple-element.36.refs_3_), channel_id=1, source_target_pairs={{0,1},{1,0},{2,3},{3,2},{4,5},{5,4},{6,7},{7,6},{8,9},{9,8},{10,11... | collective-permute-start | bytes 602120 | tf_op jit(solution)/shard_map/ppermute | solution.py:328
  66.1 13.8 %collective-permute-start.7 = (f32[392,128]{1,0:T(8,128)S(1)}, f32[392,128]{1,0:T(8,128)S(1)}, u32[]{:S(2)}, u32[]{:S(2)}) collective-permute-start(f32[392,128]{1,0:T(8,128)S(1)} %get-tuple-element.36.refs_3_), channel_id=1, source_target_pairs={{1,2},{3,4},{5,6},{2,1},{4,3},{6,5},{9,10},{11,12},{13,14},{10,9},... | collective-permute-start | bytes 602120 | tf_op jit(solution)/shard_map/ppermute | solution.py:327
  74.3 20.6 %collective-permute-start.14 = (f32[392,128]{1,0:T(8,128)S(1)}, f32[392,128]{1,0:T(8,128)S(1)}, u32[]{:S(2)}, u32[]{:S(2)}) collective-permute-start(f32[392,128]{1,0:T(8,128)S(1)} %get-tuple-element.44.refs_3_), channel_id=1, source_target_pairs={{0,1},{1,0},{2,3},{3,2},{4,5},{5,4},{6,7},{7,6},{8,9},{9,8},{10,11... | collective-permute-start | bytes 602120 | tf_op jit(solution)/shard_map/ppermute | solution.py:328
  76.3 18.7 %collective-permute-start.15 = (f32[392,128]{1,0:T(8,128)S(1)}, f32[392,128]{1,0:T(8,128)S(1)}, u32[]{:S(2)}, u32[]{:S(2)}) collective-permute-start(f32[392,128]{1,0:T(8,128)S(1)} %get-tuple-element.44.refs_3_), channel_id=1, source_target_pairs={{1,2},{3,4},{5,6},{2,1},{4,3},{6,5},{9,10},{11,12},{13,14},{10,9},... | collective-permute-start | bytes 602120 | tf_op jit(solution)/shard_map/ppermute | solution.py:327
  82.4 14.4 %collective-permute-start.10 = (f32[392,128]{1,0:T(8,128)S(1)}, f32[392,128]{1,0:T(8,128)S(1)}, u32[]{:S(2)}, u32[]{:S(2)}) collective-permute-start(f32[392,128]{1,0:T(8,128)S(1)} %get-tuple-element.40.refs_3_), channel_id=1, source_target_pairs={{0,1},{1,0},{2,3},{3,2},{4,5},{5,4},{6,7},{7,6},{8,9},{9,8},{10,11... | collective-permute-start | bytes 602120 | tf_op jit(solution)/shard_map/ppermute | solution.py:328
  84.3 12.5 %collective-permute-start.11 = (f32[392,128]{1,0:T(8,128)S(1)}, f32[392,128]{1,0:T(8,128)S(1)}, u32[]{:S(2)}, u32[]{:S(2)}) collective-permute-start(f32[392,128]{1,0:T(8,128)S(1)} %get-tuple-element.40.refs_3_), channel_id=1, source_target_pairs={{1,2},{3,4},{5,6},{2,1},{4,3},{6,5},{9,10},{11,12},{13,14},{10,9},... | collective-permute-start | bytes 602120 | tf_op jit(solution)/shard_map/ppermute | solution.py:327
  90.6 9.0 %collective-permute-start.17 = (f32[3,96,128]{2,0,1:T(4,128)S(1)}, f32[3,96,128]{2,0,1:T(4,128)S(1)}, u32[]{:S(2)}, u32[]{:S(2)}) collective-permute-start(f32[3,96,128]{2,0,1:T(4,128)S(1)} %copy.10), channel_id=1, source_target_pairs={{0,48},{8,56},{16,64},{24,72},{32,80},{40,88},{48,0},{56,8},{64,16... | collective-permute-start | bytes 442376 | tf_op jit(solution)/shard_map/ppermute | solution.py:404

commit v4 on v3

--- a/solution.py
+++ b/solution.py
@@ -22,7 +22,7 @@
 
 VMEM = pl.BlockSpec(memory_space=pltpu.VMEM)
 SMEM = pl.BlockSpec(memory_space=pltpu.SMEM)
-ANY = pl.BlockSpec(memory_space=pl.ANY)
+FAR = pl.BlockSpec(memory_space=pltpu.HBM)
 
 
 def f32(*shape):
@@ -165,7 +165,7 @@
 
 
 def step_kernel(planes, rows, slots, factor, last, scale, *refs):
-    where, atoms, anchor, u, pair_u, other_u, v, weight, proj, evolved, *refs = refs
+    where, atoms, anchor, u, other_u, pair_u, v, weight, proj, evolved, *refs = refs
     size = planes * rows
     if last == "both":
         held, result, density, acc, padded, spread, sums = refs
@@ -240,7 +240,7 @@
 
 
 def current_kernel(
-    planes, rows, scale, where, spot, real, imag, real_pair, real_other, imag_pair, imag_other, keep, send, padded
+    planes, rows, scale, where, spot, real, imag, real_other, real_pair, imag_other, imag_pair, keep, send, padded
 ):
     halos = ((real, real_pair, real_other), (imag, imag_pair, imag_other))
     pair_w, other_w = halo_weights(lax.rem(where[0], 2) == 0, planes, slope, -1.0)
@@ -325,13 +325,13 @@
 
     def exchange(value):
         other = lax.ppermute(value, "dom", others)
-        return lax.ppermute(value, "dom", pairs), other
+        return other, lax.ppermute(value, "dom", pairs)
 
     def kernel(function, name, out, scalars, arrays, scratch, far=0):
         return pl.pallas_call(
             function,
             out_shape=out,
-            in_specs=[SMEM] * scalars + [VMEM] * arrays + [ANY] * far,
+            in_specs=[SMEM] * scalars + [VMEM] * arrays + [FAR] * far,
             out_specs=jax.tree.map(lambda _: VMEM, out),
             scratch_shapes=scratch,
             compiler_params=pltpu.CompilerParams(vmem_limit_bytes=32 * 1024 * 1024),
@@ -380,6 +380,24 @@
     totals = [first, second]
     for order in range(1, TERMS + 1):
         halos = [(term, *exchange(term)) for term in terms]
+        if order == 1:
+            first_halos = (first, second, *halos[0][1:], *halos[1][1:])
+        if order == 2:
+            halo, spot = lax.optimization_barrier((halos[0][1], spot))
+            halos[0] = (halos[0][0], halo, halos[0][2])
+            half = f32(3 * planes // 2, rows, cells)
+            keep, send = kernel(
+                functools.partial(current_kernel, planes, rows, scale),
+                "current_part", (half, half), 2, 6,
+                [pltpu.VMEM((2, planes, rows + 16, cells), jnp.float32)],
+            )(where, spot, *first_halos)
+            got = lax.ppermute(send, "orb", [(i, (i // RUN ^ 1) * RUN + i % RUN) for i in range(orbs)])
+        if order == 3:
+            halo, spot = lax.optimization_barrier((halos[0][1], spot))
+            halos[0] = (halos[0][0], halo, halos[0][2])
+            quarter = f32(3 * planes // 4, rows, cells)
+            keep, send = kernel(merge_kernel, "merge_current", (quarter, quarter), 1, 2, [])(spot, keep, got)
+            got = lax.ppermute(send, "orb", [(i, (i // RUN ^ 2) * RUN + i % RUN) for i in range(orbs)])
         for channel in (0, 1):
             to = (channel + order) % 2
             if order < TERMS:
@@ -388,20 +406,6 @@
                 (totals[to],) = step(order, channel, halos[channel], totals[to])
             else:
                 evolved, density = step(order, channel, halos[channel], totals[to], totals[1 - to])
-        if order == 1:
-            halos_in = halos
-        if order == 2:
-            _, spot = lax.optimization_barrier((terms[0], spot))
-            half = f32(3 * planes // 2, rows, cells)
-            keep, send = kernel(
-                functools.partial(current_kernel, planes, rows, scale),
-                "current_part", (half, half), 2, 6,
-                [pltpu.VMEM((2, planes, rows + 16, cells), jnp.float32)],
-            )(where, spot, first, second, *halos_in[0][1:], *halos_in[1][1:])
-            got = lax.ppermute(send, "orb", [(i, (i // RUN ^ 1) * RUN + i % RUN) for i in range(orbs)])
-            quarter = f32(3 * planes // 4, rows, cells)
-            keep, send = kernel(merge_kernel, "merge_current", (quarter, quarter), 1, 2, [])(spot, keep, got)
-            got = lax.ppermute(send, "orb", [(i, (i // RUN ^ 2) * RUN + i % RUN) for i in range(orbs)])
 
     fields = jnp.concatenate([density, keep + got], axis=0)
     fields = jnp.moveaxis(fields, 1, 0)

time: 127 us -> 125 us (0.984)
  starting transfers between devices: 72.5 us -> 67.7 us
  blocking collectives: 25.8 us -> 28.3 us
    ppermute x8, starting transfers between devices: 25.9 us -> 17.7 us  [exchange(): return (other, lax.ppermute(value, 'dom', pairs))]
    ppermute x8, starting transfers between devices: 39.2 us -> 42.5 us  [exchange(): other = lax.ppermute(value, 'dom', others)]
    all_to_all x1, blocking collectives: 25.8 us -> 28.3 us  [body(): fields = lax.all_to_all(fields, 'orb', 0, 0, tiled=True)]
  transfers between devices with their start and end apart: 18 -> 18, of which waited for: 0 -> 1; matrix products, arithmetic and copies ran while one was open for 0% -> 0% of each run, Pallas kernels for 17% -> 17%
where the time goes in v4:
time: 125 us; the launch traced here: 124 us
  starting transfers between devices  67.7 us (54%)
  blocking collectives  28.3 us (23%)
  Pallas kernels  23.9 us (19%)
  local copies, waits for them, and re-layouts  2.61 us (2%)
    ppermute x8, starting transfers between devices, exchange(): other = lax.ppermute(value, 'dom', others)  42.5 us
    all_to_all x1, blocking collectives, body(): fields = lax.all_to_all(fields, 'orb', 0, 0, tiled=True)  28.3 us
    pallas_call x8, Pallas kernels, step(): kernel(functools.partial(step_kernel, planes, rows, slots, sign * time_st...  18.8 us
    ppermute x8, starting transfers between devices, exchange(): return (other, lax.ppermute(value, 'dom', pairs))  17.7 us
    ppermute x1, starting transfers between devices, body(): lax.ppermute(send, 'orb', [(i, (i // RUN ^ 2) * RUN + i % RUN) for i in r...  4.36 us
    ppermute x1, starting transfers between devices, body(): lax.ppermute(send, 'orb', [(i, (i // RUN ^ 1) * RUN + i % RUN) for i in r...  3.12 us
  transfers between devices with their start and end apart: 18, of which 1 were waited for; matrix products, arithmetic and copies ran while one was open for 0% of the time, Pallas kernels for 17%

profile of v4, /device:TPU:1, one launch (start us, length us, event | category | flops | bytes accessed | tf_op | source)
XLA Modules:
  0.0 124.2 jit_solution(15725995544201250523)
XLA Ops:
  0.6 0.0 copy-start.1
  0.6 0.0 copy-start.2
  0.7 0.0 copy-start.5
  0.7 0.7 copy-done.1
  1.3 0.0 copy-done.2
  1.3 0.0 copy-done.5
  1.3 1.0 copy-done
  2.3 0.7 copy-done.4
  3.0 1.7 %prepare_real.1 = (f32[32,8,128]{2,1,0:T(8,128)S(1)}, f32[8,128]{1,0:T(8,128)S(1)}, f32[392,128]{1,0:T(8,128)S(1)}) custom-call(s32[1]{0:T(128)} %bitcast.where.refs_0_, s32[8,32]{1,0:T(8,128)S(1)} %copy-done.1, s32[3,128]{1,0:T(4,128)S(1)} %copy-done.2, f32[4]{0:T(128)S(1)} %copy-done.5, f32[4,512]{1,0:T(4,128)S(1)} %copy-done.4, f32[2,384,128]{2,1,0:T(8,128)S(1)} %bitcast.8), custom_call_target="tpu_custom_call" | custom-call | flops 8000000 | bytes 10000000 | tf_op jit(solution)/shard_map/prepare_real/pallas_call | solution.py:344
  4.8 0.0 copy-start.6
  4.8 9.0 %collective-permute-start.4 = (f32[392,128]{1,0:T(8,128)S(1)}, f32[392,128]{1,0:T(8,128)S(1)}, u32[]{:S(2)}, u32[]{:S(2)}) collective-permute-start(f32[392,128]{1,0:T(8,128)S(1)} %get-tuple-element.36.refs_9_.refs_3_.real), channel_id=1, source_target_pairs={{1,2},{3,4},{5,6},{2,1},{4,3},{6,5},{9,10},{11,12},{13,14},{10,9},... | collective-permute-start | bytes 602120 | tf_op jit(solution)/shard_map/ppermute | solution.py:327
  13.8 4.1 %collective-permute-start.5 = (f32[392,128]{1,0:T(8,128)S(1)}, f32[392,128]{1,0:T(8,128)S(1)}, u32[]{:S(2)}, u32[]{:S(2)}) collective-permute-start(f32[392,128]{1,0:T(8,128)S(1)} %get-tuple-element.36.refs_9_.refs_3_.real), channel_id=1, source_target_pairs={{0,1},{1,0},{2,3},{3,2},{4,5},{5,4},{6,7},{7,6},{8,9},{9,8},{10,11... | collective-permute-start | bytes 602120 | tf_op jit(solution)/shard_map/ppermute | solution.py:328
  17.9 0.0 copy-done.3
  17.9 0.0 copy-done.6
  17.9 1.5 %prepare_imag.1 = (f32[4,96,128]{2,1,0:T(8,128)S(1)}, f32[392,128]{1,0:T(8,128)S(1)}) custom-call(s32[1]{0:T(128)} %bitcast.where.refs_0_, s32[8,32]{1,0:T(8,128)S(1)} %copy-done.1, s32[3,128]{1,0:T(4,128)S(1)} %copy-done.2, f32[3]{0:T(128)S(1)} %copy-done.6, f32[4,96,128]{2,1,0:T(8,128)S(1)} %copy-done.3, f32[32,8,128]{2,1,0:T(8,128)S(1)} %get-tuple-element.32.proj.refs_8_, ...), custom_call_target="tpu_custom_call" | custom-call | flops 8000000 | bytes 10000000 | tf_op jit(solution)/shard_map/prepare_imag/pallas_call | solution.py:352
  19.4 7.0 %collective-permute-start = (f32[392,128]{1,0:T(8,128)S(1)}, f32[392,128]{1,0:T(8,128)S(1)}, u32[]{:S(2)}, u32[]{:S(2)}) collective-permute-start(f32[392,128]{1,0:T(8,128)S(1)} %get-tuple-element.33.refs_3_.refs_9_.imag), channel_id=1, source_target_pairs={{1,2},{3,4},{5,6},{2,1},{4,3},{6,5},{9,10},{11,12},{13,14},{10,9},... | collective-permute-start | bytes 602120 | tf_op jit(solution)/shard_map/ppermute | solution.py:327
  26.4 1.9 %collective-permute-start.1 = (f32[392,128]{1,0:T(8,128)S(1)}, f32[392,128]{1,0:T(8,128)S(1)}, u32[]{:S(2)}, u32[]{:S(2)}) collective-permute-start(f32[392,128]{1,0:T(8,128)S(1)} %get-tuple-element.33.refs_3_.refs_9_.imag), channel_id=1, source_target_pairs={{0,1},{1,0},{2,3},{3,2},{4,5},{5,4},{6,7},{7,6},{8,9},{9,8},{10,11... | collective-permute-start | bytes 602120 | tf_op jit(solution)/shard_map/ppermute | solution.py:328
  28.4 0.0 collective-permute-done.4.refs_4_.real_other
  28.4 0.0 collective-permute-done.5.refs_5_.real_pair
  28.4 2.4 %taylor_step.9 = (f32[392,128]{1,0:T(8,128)S(1)}, f32[384,128]{1,0:T(8,128)S(1)}) custom-call(s32[1]{0:T(128)} %bitcast.where.refs_0_, s32[8,32]{1,0:T(8,128)S(1)} %copy-done.1, s32[3,128]{1,0:T(4,128)S(1)} %copy-done.2, f32[392,128]{1,0:T(8,128)S(1)} %get-tuple-element.36.refs_9_.refs_3_.real, f32[392,128]{1,0:T(8,128)S(1)} %collective-permute-done.4.refs_4_.real_other, ...), custom_call_target="tpu_custom_call" | custom-call | flops 8000000 | bytes 10000000 | tf_op jit(solution)/shard_map/taylor_step/pallas_call | solution.py:368
  30.8 5.9 %collective-permute-start.8 = (f32[392,128]{1,0:T(8,128)S(1)}, f32[392,128]{1,0:T(8,128)S(1)}, u32[]{:S(2)}, u32[]{:S(2)}) collective-permute-start(f32[392,128]{1,0:T(8,128)S(1)} %get-tuple-element.40.refs_3_), channel_id=1, source_target_pairs={{1,2},{3,4},{5,6},{2,1},{4,3},{6,5},{9,10},{11,12},{13,14},{10,9},... | collective-permute-start | bytes 602120 | tf_op jit(solution)/shard_map/ppermute | solution.py:327
  36.7 1.9 %collective-permute-start.9 = (f32[392,128]{1,0:T(8,128)S(1)}, f32[392,128]{1,0:T(8,128)S(1)}, u32[]{:S(2)}, u32[]{:S(2)}) collective-permute-start(f32[392,128]{1,0:T(8,128)S(1)} %get-tuple-element.40.refs_3_), channel_id=1, source_target_pairs={{0,1},{1,0},{2,3},{3,2},{4,5},{5,4},{6,7},{7,6},{8,9},{9,8},{10,11... | collective-permute-start | bytes 602120 | tf_op jit(solution)/shard_map/ppermute | solution.py:328
  38.6 0.0 collective-permute-done.refs_4_.imag_other
  38.6 0.0 collective-permute-done.1.refs_5_.imag_pair
  38.6 2.4 %taylor_step.8 = (f32[392,128]{1,0:T(8,128)S(1)}, f32[384,128]{1,0:T(8,128)S(1)}) custom-call(s32[1]{0:T(128)} %bitcast.where.refs_0_, s32[8,32]{1,0:T(8,128)S(1)} %copy-done.1, s32[3,128]{1,0:T(4,128)S(1)} %copy-done.2, f32[392,128]{1,0:T(8,128)S(1)} %get-tuple-element.33.refs_3_.refs_9_.imag, f32[392,128]{1,0:T(8,128)S(1)} %collective-permute-done.refs_4_.imag_other, ...), custom_call_target="tpu_custom_call" | custom-call | flops 8000000 | bytes 10000000 | tf_op jit(solution)/shard_map/taylor_step/pallas_call | solution.py:368
  41.0 2.7 %collective-permute-start.2 = (f32[392,128]{1,0:T(8,128)S(1)}, f32[392,128]{1,0:T(8,128)S(1)}, u32[]{:S(2)}, u32[]{:S(2)}) collective-permute-start(f32[392,128]{1,0:T(8,128)S(1)} %get-tuple-element.37.refs_3_), channel_id=1, source_target_pairs={{1,2},{3,4},{5,6},{2,1},{4,3},{6,5},{9,10},{11,12},{13,14},{10,9},... | collective-permute-start | bytes 602120 | tf_op jit(solution)/shard_map/ppermute | solution.py:327
  43.7 1.9 %collective-permute-start.3 = (f32[392,128]{1,0:T(8,128)S(1)}, f32[392,128]{1,0:T(8,128)S(1)}, u32[]{:S(2)}, u32[]{:S(2)}) collective-permute-start(f32[392,128]{1,0:T(8,128)S(1)} %get-tuple-element.37.refs_3_), channel_id=1, source_target_pairs={{0,1},{1,0},{2,3},{3,2},{4,5},{5,4},{6,7},{7,6},{8,9},{9,8},{10,11... | collective-permute-start | bytes 602120 | tf_op jit(solution)/shard_map/ppermute | solution.py:328
  45.7 0.0 collective-permute-done.8.refs_4_
  45.7 1.2 current_part.1
  46.9 3.1 %collective-permute-start.16 = (f32[6,96,128]{2,1,0:T(8,128)S(1)}, f32[6,96,128]{2,1,0:T(8,128)S(1)}, u32[]{:S(2)}, u32[]{:S(2)}) collective-permute-start(f32[6,96,128]{2,1,0:T(8,128)S(1)} %get-tuple-element.56), channel_id=1, source_target_pairs={{0,24},{8,32},{16,40},{24,0},{32,8},{40,16},{48,72},{56,80},{64,88... | collective-permute-start | bytes 884744 | tf_op jit(solution)/shard_map/ppermute | solution.py:394
  50.0 0.0 collective-permute-done.9.refs_5_
  50.0 2.4 %taylor_step.11 = (f32[392,128]{1,0:T(8,128)S(1)}, f32[384,128]{1,0:T(8,128)S(1)}) custom-call(s32[1]{0:T(128)} %bitcast.where.refs_0_, s32[8,32]{1,0:T(8,128)S(1)} %copy-done.1, s32[3,128]{1,0:T(4,128)S(1)} %copy-done.2, f32[392,128]{1,0:T(8,128)S(1)} %get-tuple-element.40.refs_3_, f32[392,128]{1,0:T(8,128)S(1)} %collective-permute-done.8.refs_4_, ...), custom_call_target="tpu_custom_call" | custom-call | flops 8000000 | bytes 10000000 | tf_op jit(solution)/shard_map/taylor_step/pallas_call | solution.py:368
  52.4 6.2 %collective-permute-start.12 = (f32[392,128]{1,0:T(8,128)S(1)}, f32[392,128]{1,0:T(8,128)S(1)}, u32[]{:S(2)}, u32[]{:S(2)}) collective-permute-start(f32[392,128]{1,0:T(8,128)S(1)} %get-tuple-element.45.refs_3_), channel_id=1, source_target_pairs={{1,2},{3,4},{5,6},{2,1},{4,3},{6,5},{9,10},{11,12},{13,14},{10,9},... | collective-permute-start | bytes 602120 | tf_op jit(solution)/shard_map/ppermute | solution.py:327
  58.6 1.9 %collective-permute-start.13 = (f32[392,128]{1,0:T(8,128)S(1)}, f32[392,128]{1,0:T(8,128)S(1)}, u32[]{:S(2)}, u32[]{:S(2)}) collective-permute-start(f32[392,128]{1,0:T(8,128)S(1)} %get-tuple-element.45.refs_3_), channel_id=1, source_target_pairs={{0,1},{1,0},{2,3},{3,2},{4,5},{5,4},{6,7},{7,6},{8,9},{9,8},{10,11... | collective-permute-start | bytes 602120 | tf_op jit(solution)/shard_map/ppermute | solution.py:328
  60.6 0.0 collective-permute-done.2.refs_4_
  60.6 0.0 collective-permute-done.3.refs_5_
  60.6 2.4 %taylor_step.10 = (f32[392,128]{1,0:T(8,128)S(1)}, f32[384,128]{1,0:T(8,128)S(1)}) custom-call(s32[1]{0:T(128)} %bitcast.where.refs_0_, s32[8,32]{1,0:T(8,128)S(1)} %copy-done.1, s32[3,128]{1,0:T(4,128)S(1)} %copy-done.2, f32[392,128]{1,0:T(8,128)S(1)} %get-tuple-element.37.refs_3_, f32[392,128]{1,0:T(8,128)S(1)} %collective-permute-done.2.refs_4_, ...), custom_call_target="tpu_custom_call" | custom-call | flops 8000000 | bytes 10000000 | tf_op jit(solution)/shard_map/taylor_step/pallas_call | solution.py:368
  63.0 3.1 %collective-permute-start.6 = (f32[392,128]{1,0:T(8,128)S(1)}, f32[392,128]{1,0:T(8,128)S(1)}, u32[]{:S(2)}, u32[]{:S(2)}) collective-permute-start(f32[392,128]{1,0:T(8,128)S(1)} %get-tuple-element.39.refs_3_), channel_id=1, source_target_pairs={{1,2},{3,4},{5,6},{2,1},{4,3},{6,5},{9,10},{11,12},{13,14},{10,9},... | collective-permute-start | bytes 602120 | tf_op jit(solution)/shard_map/ppermute | solution.py:327
  66.2 2.1 %collective-permute-start.7 = (f32[392,128]{1,0:T(8,128)S(1)}, f32[392,128]{1,0:T(8,128)S(1)}, u32[]{:S(2)}, u32[]{:S(2)}) collective-permute-start(f32[392,128]{1,0:T(8,128)S(1)} %get-tuple-element.39.refs_3_), channel_id=1, source_target_pairs={{0,1},{1,0},{2,3},{3,2},{4,5},{5,4},{6,7},{7,6},{8,9},{9,8},{10,11... | collective-permute-start | bytes 602120 | tf_op jit(solution)/shard_map/ppermute | solution.py:328
  68.3 0.0 collective-permute-done.12.refs_4_
  68.3 0.0 collective-permute-done.13.refs_5_
  68.3 2.4 %taylor_step.13 = (f32[392,128]{1,0:T(8,128)S(1)}, f32[384,128]{1,0:T(8,128)S(1)}) custom-call(s32[1]{0:T(128)} %bitcast.where.refs_0_, s32[8,32]{1,0:T(8,128)S(1)} %copy-done.1, s32[3,128]{1,0:T(4,128)S(1)} %copy-done.2, f32[392,128]{1,0:T(8,128)S(1)} %get-tuple-element.45.refs_3_, f32[392,128]{1,0:T(8,128)S(1)} %collective-permute-done.12.refs_4_, ...), custom_call_target="tpu_custom_call" | custom-call | flops 8000000 | bytes 10000000 | tf_op jit(solution)/shard_map/taylor_step/pallas_call | solution.py:368
  70.7 5.9 %collective-permute-start.14 = (f32[392,128]{1,0:T(8,128)S(1)}, f32[392,128]{1,0:T(8,128)S(1)}, u32[]{:S(2)}, u32[]{:S(2)}) collective-permute-start(f32[392,128]{1,0:T(8,128)S(1)} %get-tuple-element.50.refs_3_), channel_id=1, source_target_pairs={{1,2},{3,4},{5,6},{2,1},{4,3},{6,5},{9,10},{11,12},{13,14},{10,9},... | collective-permute-start | bytes 602120 | tf_op jit(solution)/shard_map/ppermute | solution.py:327
  76.6 1.9 %collective-permute-start.15 = (f32[392,128]{1,0:T(8,128)S(1)}, f32[392,128]{1,0:T(8,128)S(1)}, u32[]{:S(2)}, u32[]{:S(2)}) collective-permute-start(f32[392,128]{1,0:T(8,128)S(1)} %get-tuple-element.50.refs_3_), channel_id=1, source_target_pairs={{0,1},{1,0},{2,3},{3,2},{4,5},{5,4},{6,7},{7,6},{8,9},{9,8},{10,11... | collective-permute-start | bytes 602120 | tf_op jit(solution)/shard_map/ppermute | solution.py:328
  78.5 0.0 collective-permute-done.6.refs_4_
  78.5 0.0 collective-permute-done.7.refs_5_
  78.5 2.4 %taylor_step.12 = (f32[392,128]{1,0:T(8,128)S(1)}, f32[384,128]{1,0:T(8,128)S(1)}) custom-call(s32[1]{0:T(128)} %bitcast.where.refs_0_, s32[8,32]{1,0:T(8,128)S(1)} %copy-done.1, s32[3,128]{1,0:T(4,128)S(1)} %copy-done.2, f32[392,128]{1,0:T(8,128)S(1)} %get-tuple-element.39.refs_3_, f32[392,128]{1,0:T(8,128)S(1)} %collective-permute-done.6.refs_4_, ...), custom_call_target="tpu_custom_call" | custom-call | flops 8000000 | bytes 10000000 | tf_op jit(solution)/shard_map/taylor_step/pallas_call | solution.py:368
  81.0 2.7 %collective-permute-start.10 = (f32[392,128]{1,0:T(8,128)S(1)}, f32[392,128]{1,0:T(8,128)S(1)}, u32[]{:S(2)}, u32[]{:S(2)}) collective-permute-start(f32[392,128]{1,0:T(8,128)S(1)} %get-tuple-element.44.refs_3_), channel_id=1, source_target_pairs={{1,2},{3,4},{5,6},{2,1},{4,3},{6,5},{9,10},{11,12},{13,14},{10,9},... | collective-permute-start | bytes 602120 | tf_op jit(solution)/shard_map/ppermute | solution.py:327
  83.6 1.9 %collective-permute-start.11 = (f32[392,128]{1,0:T(8,128)S(1)}, f32[392,128]{1,0:T(8,128)S(1)}, u32[]{:S(2)}, u32[]{:S(2)}) collective-permute-start(f32[392,128]{1,0:T(8,128)S(1)} %get-tuple-element.44.refs_3_), channel_id=1, source_target_pairs={{0,1},{1,0},{2,3},{3,2},{4,5},{5,4},{6,7},{7,6},{8,9},{9,8},{10,11... | collective-permute-start | bytes 602120 | tf_op jit(solution)/shard_map/ppermute | solution.py:328
  85.6 0.0 collective-permute-done.16.got
  85.6 0.1 copy.10
  85.7 4.4 %collective-permute-start.17 = (f32[3,96,128]{2,0,1:T(4,128)S(1)}, f32[3,96,128]{2,0,1:T(4,128)S(1)}, u32[]{:S(2)}, u32[]{:S(2)}) collective-permute-start(f32[3,96,128]{2,0,1:T(4,128)S(1)} %copy.10), channel_id=1, source_target_pairs={{0,48},{8,56},{16,64},{24,72},{32,80},{40,88},{48,0},{56,8},{64,16... | collective-permute-start | bytes 442376 | tf_op jit(solution)/shard_map/ppermute | solution.py:400
  90.1 0.0 collective-permute-done.14.refs_4_
  90.1 0.0 collective-permute-done.15.refs_5_
  90.1 1.8 %taylor_step.14.refs_10_ = f32[384,128]{1,0:T(8,128)S(1)} custom-call(s32[1]{0:T(128)} %bitcast.where.refs_0_, s32[8,32]{1,0:T(8,128)S(1)} %copy-done.1, s32[3,128]{1,0:T(4,128)S(1)} %copy-done.2, f32[392,128]{1,0:T(8,128)S(1)} %get-tuple-element.50.refs_3_, f32[392,128]{1,0:T(8,128)S(1)} %collective-permute-done.14.refs_4_, ...), custom_call_target="tpu_custom_call" | custom-call | flops 8000000 | bytes 10000000 | tf_op jit(solution)/shard_map/taylor_step/pallas_call | solution.py:368
  91.9 0.0 collective-permute-done.10.refs_4_
  91.9 0.0 collective-permute-done.11.refs_5_
  92.0 2.6 %taylor_step.15 = (f32[2,384,128]{2,1,0:T(8,128)}, f32[4,96,128]{2,1,0:T(8,128)S(1)}) custom-call(s32[1]{0:T(128)} %bitcast.where.refs_0_, s32[8,32]{1,0:T(8,128)S(1)} %copy-done.1, s32[3,128]{1,0:T(4,128)S(1)} %copy-done.2, f32[392,128]{1,0:T(8,128)S(1)} %get-tuple-element.44.refs_3_, f32[392,128]{1,0:T(8,128)S(1)} %collective-permute-done.10.refs_4_, ...), custom_call_target="tpu_custom_call" | custom-call | flops 8000000 | bytes 10000000 | tf_op jit(solution)/shard_map/taylor_step/pallas_call | solution.py:368
  94.6 0.1 copy.12
  94.7 0.4 collective-permute-done.17
  95.1 0.1 copy_add_fusion
  95.2 0.1 maximum_bitcast_fusion
  95.3 28.3 %all_to_all.5.got = f32[96,7,128]{2,1,0:T(8,128)S(1)} all-to-all(f32[96,7,128]{2,1,0:T(8,128)S(1)} %maximum_bitcast_fusion), channel_id=1, replica_groups=mesh['orb'=96,'dom'=8] {'orb'}, dimensions={0} | all-to-all | bytes 688128 | tf_op jit(solution)/shard_map/all_to_all | solution.py:412
  123.6 0.6 sum_over_orb.1
  (4 shorter events, 0.0 us)
Async XLA Ops:
  0.6 0.7 copy-start.1
  0.6 0.7 copy-start.2
  0.7 0.7 copy-start.5
  1.3 1.0 copy-start
  2.3 0.7 copy-start.4
  3.0 14.9 %copy-start.3 = (f32[4,96,128]{2,1,0:T(8,128)S(1)}, f32[4,96,128]{2,1,0:T(8,128)}, u32[]{:S(2)}) copy-start(f32[4,96,128]{2,1,0:T(8,128)} %potential.1) | copy-start | bytes 589828
  4.8 13.1 %copy-start.6 = (f32[3]{0:T(128)S(1)}, f32[3]{0:T(128)}, u32[]{:S(2)}) copy-start(f32[3]{0:T(128)} %laser.1) | copy-start | bytes 40
  4.8 23.6 %collective-permute-start.4 = (f32[392,128]{1,0:T(8,128)S(1)}, f32[392,128]{1,0:T(8,128)S(1)}, u32[]{:S(2)}, u32[]{:S(2)}) collective-permute-start(f32[392,128]{1,0:T(8,128)S(1)} %get-tuple-element.36.refs_9_.refs_3_.real), channel_id=1, source_target_pairs={{1,2},{3,4},{5,6},{2,1},{4,3},{6,5},{9,10},{11,12},{13,14},{10,9},... | collective-permute-start | bytes 602120 | tf_op jit(solution)/shard_map/ppermute | solution.py:327
  13.8 14.6 %collective-permute-start.5 = (f32[392,128]{1,0:T(8,128)S(1)}, f32[392,128]{1,0:T(8,128)S(1)}, u32[]{:S(2)}, u32[]{:S(2)}) collective-permute-start(f32[392,128]{1,0:T(8,128)S(1)} %get-tuple-element.36.refs_9_.refs_3_.real), channel_id=1, source_target_pairs={{0,1},{1,0},{2,3},{3,2},{4,5},{5,4},{6,7},{7,6},{8,9},{9,8},{10,11... | collective-permute-start | bytes 602120 | tf_op jit(solution)/shard_map/ppermute | solution.py:328
  19.4 19.2 %collective-permute-start = (f32[392,128]{1,0:T(8,128)S(1)}, f32[392,128]{1,0:T(8,128)S(1)}, u32[]{:S(2)}, u32[]{:S(2)}) collective-permute-start(f32[392,128]{1,0:T(8,128)S(1)} %get-tuple-element.33.refs_3_.refs_9_.imag), channel_id=1, source_target_pairs={{1,2},{3,4},{5,6},{2,1},{4,3},{6,5},{9,10},{11,12},{13,14},{10,9},... | collective-permute-start | bytes 602120 | tf_op jit(solution)/shard_map/ppermute | solution.py:327
  26.4 12.2 %collective-permute-start.1 = (f32[392,128]{1,0:T(8,128)S(1)}, f32[392,128]{1,0:T(8,128)S(1)}, u32[]{:S(2)}, u32[]{:S(2)}) collective-permute-start(f32[392,128]{1,0:T(8,128)S(1)} %get-tuple-element.33.refs_3_.refs_9_.imag), channel_id=1, source_target_pairs={{0,1},{1,0},{2,3},{3,2},{4,5},{5,4},{6,7},{7,6},{8,9},{9,8},{10,11... | collective-permute-start | bytes 602120 | tf_op jit(solution)/shard_map/ppermute | solution.py:328
  30.8 14.9 %collective-permute-start.8 = (f32[392,128]{1,0:T(8,128)S(1)}, f32[392,128]{1,0:T(8,128)S(1)}, u32[]{:S(2)}, u32[]{:S(2)}) collective-permute-start(f32[392,128]{1,0:T(8,128)S(1)} %get-tuple-element.40.refs_3_), channel_id=1, source_target_pairs={{1,2},{3,4},{5,6},{2,1},{4,3},{6,5},{9,10},{11,12},{13,14},{10,9},... | collective-permute-start | bytes 602120 | tf_op jit(solution)/shard_map/ppermute | solution.py:327
  36.7 13.3 %collective-permute-start.9 = (f32[392,128]{1,0:T(8,128)S(1)}, f32[392,128]{1,0:T(8,128)S(1)}, u32[]{:S(2)}, u32[]{:S(2)}) collective-permute-start(f32[392,128]{1,0:T(8,128)S(1)} %get-tuple-element.40.refs_3_), channel_id=1, source_target_pairs={{0,1},{1,0},{2,3},{3,2},{4,5},{5,4},{6,7},{7,6},{8,9},{9,8},{10,11... | collective-permute-start | bytes 602120 | tf_op jit(solution)/shard_map/ppermute | solution.py:328
  41.0 19.5 %collective-permute-start.2 = (f32[392,128]{1,0:T(8,128)S(1)}, f32[392,128]{1,0:T(8,128)S(1)}, u32[]{:S(2)}, u32[]{:S(2)}) collective-permute-start(f32[392,128]{1,0:T(8,128)S(1)} %get-tuple-element.37.refs_3_), channel_id=1, source_target_pairs={{1,2},{3,4},{5,6},{2,1},{4,3},{6,5},{9,10},{11,12},{13,14},{10,9},... | collective-permute-start | bytes 602120 | tf_op jit(solution)/shard_map/ppermute | solution.py:327
  43.7 16.9 %collective-permute-start.3 = (f32[392,128]{1,0:T(8,128)S(1)}, f32[392,128]{1,0:T(8,128)S(1)}, u32[]{:S(2)}, u32[]{:S(2)}) collective-permute-start(f32[392,128]{1,0:T(8,128)S(1)} %get-tuple-element.37.refs_3_), channel_id=1, source_target_pairs={{0,1},{1,0},{2,3},{3,2},{4,5},{5,4},{6,7},{7,6},{8,9},{9,8},{10,11... | collective-permute-start | bytes 602120 | tf_op jit(solution)/shard_map/ppermute | solution.py:328
  46.9 38.7 %collective-permute-start.16 = (f32[6,96,128]{2,1,0:T(8,128)S(1)}, f32[6,96,128]{2,1,0:T(8,128)S(1)}, u32[]{:S(2)}, u32[]{:S(2)}) collective-permute-start(f32[6,96,128]{2,1,0:T(8,128)S(1)} %get-tuple-element.56), channel_id=1, source_target_pairs={{0,24},{8,32},{16,40},{24,0},{32,8},{40,16},{48,72},{56,80},{64,88... | collective-permute-start | bytes 884744 | tf_op jit(solution)/shard_map/ppermute | solution.py:394
  52.4 15.8 %collective-permute-start.12 = (f32[392,128]{1,0:T(8,128)S(1)}, f32[392,128]{1,0:T(8,128)S(1)}, u32[]{:S(2)}, u32[]{:S(2)}) collective-permute-start(f32[392,128]{1,0:T(8,128)S(1)} %get-tuple-element.45.refs_3_), channel_id=1, source_target_pairs={{1,2},{3,4},{5,6},{2,1},{4,3},{6,5},{9,10},{11,12},{13,14},{10,9},... | collective-permute-start | bytes 602120 | tf_op jit(solution)/shard_map/ppermute | solution.py:327
  58.6 9.6 %collective-permute-start.13 = (f32[392,128]{1,0:T(8,128)S(1)}, f32[392,128]{1,0:T(8,128)S(1)}, u32[]{:S(2)}, u32[]{:S(2)}) collective-permute-start(f32[392,128]{1,0:T(8,128)S(1)} %get-tuple-element.45.refs_3_), channel_id=1, source_target_pairs={{0,1},{1,0},{2,3},{3,2},{4,5},{5,4},{6,7},{7,6},{8,9},{9,8},{10,11... | collective-permute-start | bytes 602120 | tf_op jit(solution)/shard_map/ppermute | solution.py:328
  63.0 15.5 %collective-permute-start.6 = (f32[392,128]{1,0:T(8,128)S(1)}, f32[392,128]{1,0:T(8,128)S(1)}, u32[]{:S(2)}, u32[]{:S(2)}) collective-permute-start(f32[392,128]{1,0:T(8,128)S(1)} %get-tuple-element.39.refs_3_), channel_id=1, source_target_pairs={{1,2},{3,4},{5,6},{2,1},{4,3},{6,5},{9,10},{11,12},{13,14},{10,9},... | collective-permute-start | bytes 602120 | tf_op jit(solution)/shard_map/ppermute | solution.py:327
  66.2 12.4 %collective-permute-start.7 = (f32[392,128]{1,0:T(8,128)S(1)}, f32[392,128]{1,0:T(8,128)S(1)}, u32[]{:S(2)}, u32[]{:S(2)}) collective-permute-start(f32[392,128]{1,0:T(8,128)S(1)} %get-tuple-element.39.refs_3_), channel_id=1, source_target_pairs={{0,1},{1,0},{2,3},{3,2},{4,5},{5,4},{6,7},{7,6},{8,9},{9,8},{10,11... | collective-permute-start | bytes 602120 | tf_op jit(solution)/shard_map/ppermute | solution.py:328
  70.7 19.4 %collective-permute-start.14 = (f32[392,128]{1,0:T(8,128)S(1)}, f32[392,128]{1,0:T(8,128)S(1)}, u32[]{:S(2)}, u32[]{:S(2)}) collective-permute-start(f32[392,128]{1,0:T(8,128)S(1)} %get-tuple-element.50.refs_3_), channel_id=1, source_target_pairs={{1,2},{3,4},{5,6},{2,1},{4,3},{6,5},{9,10},{11,12},{13,14},{10,9},... | collective-permute-start | bytes 602120 | tf_op jit(solution)/shard_map/ppermute | solution.py:327
  76.6 13.5 %collective-permute-start.15 = (f32[392,128]{1,0:T(8,128)S(1)}, f32[392,128]{1,0:T(8,128)S(1)}, u32[]{:S(2)}, u32[]{:S(2)}) collective-permute-start(f32[392,128]{1,0:T(8,128)S(1)} %get-tuple-element.50.refs_3_), channel_id=1, source_target_pairs={{0,1},{1,0},{2,3},{3,2},{4,5},{5,4},{6,7},{7,6},{8,9},{9,8},{10,11... | collective-permute-start | bytes 602120 | tf_op jit(solution)/shard_map/ppermute | solution.py:328
  81.0 11.0 %collective-permute-start.10 = (f32[392,128]{1,0:T(8,128)S(1)}, f32[392,128]{1,0:T(8,128)S(1)}, u32[]{:S(2)}, u32[]{:S(2)}) collective-permute-start(f32[392,128]{1,0:T(8,128)S(1)} %get-tuple-element.44.refs_3_), channel_id=1, source_target_pairs={{1,2},{3,4},{5,6},{2,1},{4,3},{6,5},{9,10},{11,12},{13,14},{10,9},... | collective-permute-start | bytes 602120 | tf_op jit(solution)/shard_map/ppermute | solution.py:327
  83.6 8.3 %collective-permute-start.11 = (f32[392,128]{1,0:T(8,128)S(1)}, f32[392,128]{1,0:T(8,128)S(1)}, u32[]{:S(2)}, u32[]{:S(2)}) collective-permute-start(f32[392,128]{1,0:T(8,128)S(1)} %get-tuple-element.44.refs_3_), channel_id=1, source_target_pairs={{0,1},{1,0},{2,3},{3,2},{4,5},{5,4},{6,7},{7,6},{8,9},{9,8},{10,11... | collective-permute-start | bytes 602120 | tf_op jit(solution)/shard_map/ppermute | solution.py:328
  85.7 9.4 %collective-permute-start.17 = (f32[3,96,128]{2,0,1:T(4,128)S(1)}, f32[3,96,128]{2,0,1:T(4,128)S(1)}, u32[]{:S(2)}, u32[]{:S(2)}) collective-permute-start(f32[3,96,128]{2,0,1:T(4,128)S(1)} %copy.10), channel_id=1, source_target_pairs={{0,48},{8,56},{16,64},{24,72},{32,80},{40,88},{48,0},{56,8},{64,16... | collective-permute-start | bytes 442376 | tf_op jit(solution)/shard_map/ppermute | solution.py:400

commit v5 on v4

--- a/solution.py
+++ b/solution.py
@@ -22,7 +22,6 @@
 
 VMEM = pl.BlockSpec(memory_space=pltpu.VMEM)
 SMEM = pl.BlockSpec(memory_space=pltpu.SMEM)
-FAR = pl.BlockSpec(memory_space=pltpu.HBM)
 
 
 def f32(*shape):
@@ -108,15 +107,11 @@
 
 
 def prepare_kernel(
-    planes, rows, slots, where, atoms, anchor, strength, projector_far, u,
-    proj, weight, message, sums, projector, sems,
+    planes, rows, slots, where, atoms, anchor, strength, projector, u,
+    proj, weight, message, sums,
 ):
     cells = u.shape[-1]
     size = planes * rows
-    fetch = pltpu.make_async_copy(u.at[0], message.at[0:size], sems.at[0])
-    fetch_projector = pltpu.make_async_copy(projector_far, projector, sems.at[1])
-    fetch.start()
-    fetch_projector.start()
     me = where[0]
     behind = jnp.maximum(me - 1, 0)
     lane = lax.broadcasted_iota(jnp.int32, (8, cells), 1)
@@ -132,7 +127,6 @@
         strengths = jnp.where((lane % PROJ) == p, strength[p], strengths)
     weight[...] = listed * strengths
 
-    fetch_projector.wait()
     for chunk in range(BOX**3 // cells):
         block = projector[:, chunk * cells : (chunk + 1) * cells]
         for part in range(cells // BOX):
@@ -142,26 +136,24 @@
             for p in range(PROJ):
                 proj[p * BOX + i, j : j + 1, :] = moved[p : p + 1]
 
-    fetch.wait()
-    message[size : size + 8, :] = partial_sums(planes, rows, slots, me, atoms, anchor, message, proj, sums)
+    message[0:size, :] = u[0]
+    message[size : size + 8, :] = partial_sums(planes, rows, slots, me, atoms, anchor, u.at[0], proj, sums)
 
 
 def second_kernel(
-    planes, rows, slots, domains, where, atoms, anchor, laser, potential, proj, u, v, message, sums, sem
+    planes, rows, slots, domains, where, atoms, anchor, laser, potential, proj, u, v, message, sums
 ):
     cells = u.shape[-1]
     size = planes * rows
     me = where[0]
-    fetch = pltpu.make_async_copy(u.at[1], message.at[0:size], sem)
-    fetch.start()
     y = lax.broadcasted_iota(jnp.int32, (rows, cells), 0).astype(jnp.float32)
     z = lax.broadcasted_iota(jnp.int32, (rows, cells), 1).astype(jnp.float32)
     along = laser[1] * ((y - (rows - 1) / 2.0) * spacing) + laser[2] * ((z - (cells - 1) / 2.0) * spacing)
     for i in range(planes):
         x = ((me * planes + i).astype(jnp.float32) - (domains * planes - 1) / 2.0) * spacing
         v[i] = potential[i] + laser[0] * x + along + 3.0 * kinetic[0]
-    fetch.wait()
-    message[size : size + 8, :] = partial_sums(planes, rows, slots, me, atoms, anchor, message, proj, sums)
+    message[0:size, :] = u[1]
+    message[size : size + 8, :] = partial_sums(planes, rows, slots, me, atoms, anchor, u.at[1], proj, sums)
 
 
 def step_kernel(planes, rows, slots, factor, last, scale, *refs):
@@ -282,30 +274,18 @@
                 send[at] = jnp.where(lower, flow, first)
 
 
-def merge_kernel(spot, held, got, keep, send):
-    lower = lax.rem(spot[0] // 2, 2) == 0
-    for c in range(3):
-        first = held[2 * c] + got[2 * c]
-        second = held[2 * c + 1] + got[2 * c + 1]
-        keep[c] = jnp.where(lower, first, second)
-        send[c] = jnp.where(lower, second, first)
-
-
-def plane_kept(source):
-    x = source // RUN
-    return 2 * (x % 2) + x // 2 % 2
-
-
 def gather_kernel(planes, got, density, current):
-    totals = [None] * planes
+    half = planes // 2
+    totals = [None, None]
     for source in range(got.shape[0]):
-        p = plane_kept(source)
-        totals[p] = got[source] if totals[p] is None else totals[p] + got[source]
-    everywhere = totals[0] + totals[1] + totals[2] + totals[3]
+        kept = source // RUN % 2
+        totals[kept] = got[source] if totals[kept] is None else totals[kept] + got[source]
+    everywhere = totals[0] + totals[1]
     for i in range(planes):
         density[i] = everywhere[i : i + 1]
         for c in range(3):
-            current[c, i] = totals[i][planes + c : planes + c + 1]
+            at = planes + c * half + i % half
+            current[c, i] = totals[i // half][at : at + 1]
 
 
 def body(orbitals, potential, laser_field, box_anchor, domain_atoms, projector, strength):
@@ -327,11 +307,11 @@
         other = lax.ppermute(value, "dom", others)
         return other, lax.ppermute(value, "dom", pairs)
 
-    def kernel(function, name, out, scalars, arrays, scratch, far=0):
+    def kernel(function, name, out, scalars, arrays, scratch):
         return pl.pallas_call(
             function,
             out_shape=out,
-            in_specs=[SMEM] * scalars + [VMEM] * arrays + [FAR] * far,
+            in_specs=[SMEM] * scalars + [VMEM] * arrays,
             out_specs=jax.tree.map(lambda _: VMEM, out),
             scratch_shapes=scratch,
             compiler_params=pltpu.CompilerParams(vmem_limit_bytes=32 * 1024 * 1024),
@@ -345,15 +325,13 @@
         functools.partial(prepare_kernel, planes, rows, slots),
         "prepare_real",
         (f32(PROJ * BOX, BOX, cells), f32(8, cells), f32(size + 8, cells)),
-        4, 0,
-        [sums, pltpu.VMEM((PROJ, BOX**3), jnp.float32), pltpu.SemaphoreType.DMA((2,))],
-        2,
+        4, 2, [sums],
     )(*places, strength, projector, u)
     v, second = kernel(
         functools.partial(second_kernel, planes, rows, slots, domains),
         "prepare_imag",
         (f32(planes, rows, cells), f32(size + 8, cells)),
-        4, 2, [sums, pltpu.SemaphoreType.DMA], 1,
+        4, 3, [sums],
     )(*places, laser_field, potential, proj, u)
 
     def step(order, channel, halos, evolved, held=None):
@@ -380,11 +358,7 @@
     totals = [first, second]
     for order in range(1, TERMS + 1):
         halos = [(term, *exchange(term)) for term in terms]
-        if order == 1:
-            first_halos = (first, second, *halos[0][1:], *halos[1][1:])
-        if order == 2:
-            halo, spot = lax.optimization_barrier((halos[0][1], spot))
-            halos[0] = (halos[0][0], halo, halos[0][2])
+        if order == TERMS:
             half = f32(3 * planes // 2, rows, cells)
             keep, send = kernel(
                 functools.partial(current_kernel, planes, rows, scale),
@@ -392,12 +366,6 @@
                 [pltpu.VMEM((2, planes, rows + 16, cells), jnp.float32)],
             )(where, spot, *first_halos)
             got = lax.ppermute(send, "orb", [(i, (i // RUN ^ 1) * RUN + i % RUN) for i in range(orbs)])
-        if order == 3:
-            halo, spot = lax.optimization_barrier((halos[0][1], spot))
-            halos[0] = (halos[0][0], halo, halos[0][2])
-            quarter = f32(3 * planes // 4, rows, cells)
-            keep, send = kernel(merge_kernel, "merge_current", (quarter, quarter), 1, 2, [])(spot, keep, got)
-            got = lax.ppermute(send, "orb", [(i, (i // RUN ^ 2) * RUN + i % RUN) for i in range(orbs)])
         for channel in (0, 1):
             to = (channel + order) % 2
             if order < TERMS:
@@ -406,6 +374,8 @@
                 (totals[to],) = step(order, channel, halos[channel], totals[to])
             else:
                 evolved, density = step(order, channel, halos[channel], totals[to], totals[1 - to])
+        if order == 1:
+            first_halos = (first, second, *halos[0][1:], *halos[1][1:])
 
     fields = jnp.concatenate([density, keep + got], axis=0)
     fields = jnp.moveaxis(fields, 1, 0)

time: 125 us -> 130 us (1.040)
  blocking collectives: 28.3 us -> 36 us
  starting transfers between devices: 67.7 us -> 63.3 us
  waiting for transfers between devices: 0.44 us -> 2.18 us
    all_to_all x1, blocking collectives: 28.3 us -> 36 us  [body(): fields = lax.all_to_all(fields, 'orb', 0, 0, tiled=True)]
    ppermute x1 -> x0, starting transfers between devices: 4.36 us -> none  [body(): lax.ppermute(send, 'orb', [(i, (i // RUN ^ 2) * RUN + i % RUN) for i in r...]
    ppermute x8, waiting for transfers between devices: 0.02 us -> 2.16 us  [exchange(): other = lax.ppermute(value, 'dom', others)]
  transfers between devices with their start and end apart: 18 -> 17, of which waited for: 1 -> 1; matrix products, arithmetic and copies ran while one was open for 0% -> 0% of each run, Pallas kernels for 17% -> 15%
where the time goes in v5:
time: 130 us; the launch traced here: 129 us
  starting transfers between devices  63.3 us (49%)
  blocking collectives  36 us (28%)
  Pallas kernels  23.3 us (18%)
  local copies, waits for them, and re-layouts  2.68 us (2%)
  waiting for transfers between devices  2.18 us (2%)
    ppermute x8, starting transfers between devices, exchange(): other = lax.ppermute(value, 'dom', others)  42.5 us
    all_to_all x1, blocking collectives, body(): fields = lax.all_to_all(fields, 'orb', 0, 0, tiled=True)  36 us
    pallas_call x8, Pallas kernels, step(): kernel(functools.partial(step_kernel, planes, rows, slots, sign * time_st...  18.9 us
    ppermute x8, starting transfers between devices, exchange(): return (other, lax.ppermute(value, 'dom', pairs))  17.7 us
    ppermute x1, starting transfers between devices, body(): lax.ppermute(send, 'orb', [(i, (i // RUN ^ 1) * RUN + i % RUN) for i in r...  3.12 us
  transfers between devices with their start and end apart: 17, of which 1 were waited for; matrix products, arithmetic and copies ran while one was open for 0% of the time, Pallas kernels for 15%

profile of v5, /device:TPU:1, one launch (start us, length us, event | category | flops | bytes accessed | tf_op | source)
XLA Modules:
  0.0 128.9 jit_solution(6682286582093961137)
XLA Ops:
  0.6 0.0 copy-start.1
  0.6 0.0 copy-start.2
  0.7 0.0 copy-start.5
  0.7 0.7 copy-done.1
  1.3 0.0 copy-done.2
  1.3 0.0 copy-done.5
  1.3 0.0 copy-start
  1.3 1.0 copy-done
  2.3 0.0 copy-start.4
  2.3 0.7 copy-done.4
  3.0 0.0 copy-start.3
  3.0 1.3 %prepare_real.1 = (f32[32,8,128]{2,1,0:T(8,128)S(1)}, f32[8,128]{1,0:T(8,128)S(1)}, f32[392,128]{1,0:T(8,128)S(1)}) custom-call(s32[1]{0:T(128)} %bitcast.where.refs_0_, s32[8,32]{1,0:T(8,128)S(1)} %copy-done.1, s32[3,128]{1,0:T(4,128)S(1)} %copy-done.2, f32[4]{0:T(128)S(1)} %copy-done.5, f32[4,512]{1,0:T(4,128)S(1)} %copy-done.4, f32[2,384,128]{2,1,0:T(8,128)S(1)} %bitcast.8), custom_call_target="tpu_custom_call" | custom-call | flops 8000000 | bytes 10000000 | tf_op jit(solution)/shard_map/prepare_real/pallas_call | solution.py:324
  4.3 9.0 %collective-permute-start.4 = (f32[392,128]{1,0:T(8,128)S(1)}, f32[392,128]{1,0:T(8,128)S(1)}, u32[]{:S(2)}, u32[]{:S(2)}) collective-permute-start(f32[392,128]{1,0:T(8,128)S(1)} %get-tuple-element.30.refs_9_.refs_3_.real), channel_id=1, source_target_pairs={{1,2},{3,4},{5,6},{2,1},{4,3},{6,5},{9,10},{11,12},{13,14},{10,9},... | collective-permute-start | bytes 602120 | tf_op jit(solution)/shard_map/ppermute | solution.py:307
  13.4 4.1 %collective-permute-start.5 = (f32[392,128]{1,0:T(8,128)S(1)}, f32[392,128]{1,0:T(8,128)S(1)}, u32[]{:S(2)}, u32[]{:S(2)}) collective-permute-start(f32[392,128]{1,0:T(8,128)S(1)} %get-tuple-element.30.refs_9_.refs_3_.real), channel_id=1, source_target_pairs={{0,1},{1,0},{2,3},{3,2},{4,5},{5,4},{6,7},{7,6},{8,9},{9,8},{10,11... | collective-permute-start | bytes 602120 | tf_op jit(solution)/shard_map/ppermute | solution.py:308
  17.5 0.0 copy-done.3
  17.5 0.0 copy-done.6
  17.5 1.2 prepare_imag.1
  18.7 7.0 %collective-permute-start = (f32[392,128]{1,0:T(8,128)S(1)}, f32[392,128]{1,0:T(8,128)S(1)}, u32[]{:S(2)}, u32[]{:S(2)}) collective-permute-start(f32[392,128]{1,0:T(8,128)S(1)} %get-tuple-element.27.refs_3_.refs_9_.imag), channel_id=1, source_target_pairs={{1,2},{3,4},{5,6},{2,1},{4,3},{6,5},{9,10},{11,12},{13,14},{10,9},... | collective-permute-start | bytes 602120 | tf_op jit(solution)/shard_map/ppermute | solution.py:307
  25.8 1.9 %collective-permute-start.1 = (f32[392,128]{1,0:T(8,128)S(1)}, f32[392,128]{1,0:T(8,128)S(1)}, u32[]{:S(2)}, u32[]{:S(2)}) collective-permute-start(f32[392,128]{1,0:T(8,128)S(1)} %get-tuple-element.27.refs_3_.refs_9_.imag), channel_id=1, source_target_pairs={{0,1},{1,0},{2,3},{3,2},{4,5},{5,4},{6,7},{7,6},{8,9},{9,8},{10,11... | collective-permute-start | bytes 602120 | tf_op jit(solution)/shard_map/ppermute | solution.py:308
  27.7 0.0 collective-permute-done.4.refs_4_.real_other
  27.7 0.0 collective-permute-done.5.refs_5_.real_pair
  27.7 2.4 %taylor_step.9 = (f32[392,128]{1,0:T(8,128)S(1)}, f32[384,128]{1,0:T(8,128)S(1)}) custom-call(s32[1]{0:T(128)} %bitcast.where.refs_0_, s32[8,32]{1,0:T(8,128)S(1)} %copy-done.1, s32[3,128]{1,0:T(4,128)S(1)} %copy-done.2, f32[392,128]{1,0:T(8,128)S(1)} %get-tuple-element.30.refs_9_.refs_3_.real, f32[392,128]{1,0:T(8,128)S(1)} %collective-permute-done.4.refs_4_.real_other, ...), custom_call_target="tpu_custom_call" | custom-call | flops 8000000 | bytes 10000000 | tf_op jit(solution)/shard_map/taylor_step/pallas_call | solution.py:346
  30.1 5.9 %collective-permute-start.8 = (f32[392,128]{1,0:T(8,128)S(1)}, f32[392,128]{1,0:T(8,128)S(1)}, u32[]{:S(2)}, u32[]{:S(2)}) collective-permute-start(f32[392,128]{1,0:T(8,128)S(1)} %get-tuple-element.34.refs_3_), channel_id=1, source_target_pairs={{1,2},{3,4},{5,6},{2,1},{4,3},{6,5},{9,10},{11,12},{13,14},{10,9},... | collective-permute-start | bytes 602120 | tf_op jit(solution)/shard_map/ppermute | solution.py:307
  36.0 1.9 %collective-permute-start.9 = (f32[392,128]{1,0:T(8,128)S(1)}, f32[392,128]{1,0:T(8,128)S(1)}, u32[]{:S(2)}, u32[]{:S(2)}) collective-permute-start(f32[392,128]{1,0:T(8,128)S(1)} %get-tuple-element.34.refs_3_), channel_id=1, source_target_pairs={{0,1},{1,0},{2,3},{3,2},{4,5},{5,4},{6,7},{7,6},{8,9},{9,8},{10,11... | collective-permute-start | bytes 602120 | tf_op jit(solution)/shard_map/ppermute | solution.py:308
  37.9 0.0 collective-permute-done.refs_4_.imag_other
  37.9 0.0 collective-permute-done.1.refs_5_.imag_pair
  38.0 2.4 %taylor_step.8 = (f32[392,128]{1,0:T(8,128)S(1)}, f32[384,128]{1,0:T(8,128)S(1)}) custom-call(s32[1]{0:T(128)} %bitcast.where.refs_0_, s32[8,32]{1,0:T(8,128)S(1)} %copy-done.1, s32[3,128]{1,0:T(4,128)S(1)} %copy-done.2, f32[392,128]{1,0:T(8,128)S(1)} %get-tuple-element.27.refs_3_.refs_9_.imag, f32[392,128]{1,0:T(8,128)S(1)} %collective-permute-done.refs_4_.imag_other, ...), custom_call_target="tpu_custom_call" | custom-call | flops 8000000 | bytes 10000000 | tf_op jit(solution)/shard_map/taylor_step/pallas_call | solution.py:346
  40.4 2.7 %collective-permute-start.2 = (f32[392,128]{1,0:T(8,128)S(1)}, f32[392,128]{1,0:T(8,128)S(1)}, u32[]{:S(2)}, u32[]{:S(2)}) collective-permute-start(f32[392,128]{1,0:T(8,128)S(1)} %get-tuple-element.31.refs_3_), channel_id=1, source_target_pairs={{1,2},{3,4},{5,6},{2,1},{4,3},{6,5},{9,10},{11,12},{13,14},{10,9},... | collective-permute-start | bytes 602120 | tf_op jit(solution)/shard_map/ppermute | solution.py:307
  43.0 1.9 %collective-permute-start.3 = (f32[392,128]{1,0:T(8,128)S(1)}, f32[392,128]{1,0:T(8,128)S(1)}, u32[]{:S(2)}, u32[]{:S(2)}) collective-permute-start(f32[392,128]{1,0:T(8,128)S(1)} %get-tuple-element.31.refs_3_), channel_id=1, source_target_pairs={{0,1},{1,0},{2,3},{3,2},{4,5},{5,4},{6,7},{7,6},{8,9},{9,8},{10,11... | collective-permute-start | bytes 602120 | tf_op jit(solution)/shard_map/ppermute | solution.py:308
  45.0 1.2 current_part.1
  46.2 0.2 copy.10
  46.4 3.1 %collective-permute-start.16 = (f32[6,96,128]{2,0,1:T(8,128)S(1)}, f32[6,96,128]{2,0,1:T(8,128)S(1)}, u32[]{:S(2)}, u32[]{:S(2)}) collective-permute-start(f32[6,96,128]{2,0,1:T(8,128)S(1)} %copy.10), channel_id=1, source_target_pairs={{0,24},{8,32},{16,40},{24,0},{32,8},{40,16},{48,72},{56,80},{64,88... | collective-permute-start | bytes 884744 | tf_op jit(solution)/shard_map/ppermute | solution.py:368
  49.5 0.0 collective-permute-done.8.refs_4_
  49.5 0.0 collective-permute-done.9.refs_5_
  49.5 2.4 %taylor_step.11 = (f32[392,128]{1,0:T(8,128)S(1)}, f32[384,128]{1,0:T(8,128)S(1)}) custom-call(s32[1]{0:T(128)} %bitcast.where.refs_0_, s32[8,32]{1,0:T(8,128)S(1)} %copy-done.1, s32[3,128]{1,0:T(4,128)S(1)} %copy-done.2, f32[392,128]{1,0:T(8,128)S(1)} %get-tuple-element.34.refs_3_, f32[392,128]{1,0:T(8,128)S(1)} %collective-permute-done.8.refs_4_, ...), custom_call_target="tpu_custom_call" | custom-call | flops 8000000 | bytes 10000000 | tf_op jit(solution)/shard_map/taylor_step/pallas_call | solution.py:346
  52.0 6.2 %collective-permute-start.12 = (f32[392,128]{1,0:T(8,128)S(1)}, f32[392,128]{1,0:T(8,128)S(1)}, u32[]{:S(2)}, u32[]{:S(2)}) collective-permute-start(f32[392,128]{1,0:T(8,128)S(1)} %get-tuple-element.38.refs_3_), channel_id=1, source_target_pairs={{1,2},{3,4},{5,6},{2,1},{4,3},{6,5},{9,10},{11,12},{13,14},{10,9},... | collective-permute-start | bytes 602120 | tf_op jit(solution)/shard_map/ppermute | solution.py:307
  58.2 1.9 %collective-permute-start.13 = (f32[392,128]{1,0:T(8,128)S(1)}, f32[392,128]{1,0:T(8,128)S(1)}, u32[]{:S(2)}, u32[]{:S(2)}) collective-permute-start(f32[392,128]{1,0:T(8,128)S(1)} %get-tuple-element.38.refs_3_), channel_id=1, source_target_pairs={{0,1},{1,0},{2,3},{3,2},{4,5},{5,4},{6,7},{7,6},{8,9},{9,8},{10,11... | collective-permute-start | bytes 602120 | tf_op jit(solution)/shard_map/ppermute | solution.py:308
  60.1 0.0 collective-permute-done.2.refs_4_
  60.1 0.0 collective-permute-done.3.refs_5_
  60.1 2.4 %taylor_step.10 = (f32[392,128]{1,0:T(8,128)S(1)}, f32[384,128]{1,0:T(8,128)S(1)}) custom-call(s32[1]{0:T(128)} %bitcast.where.refs_0_, s32[8,32]{1,0:T(8,128)S(1)} %copy-done.1, s32[3,128]{1,0:T(4,128)S(1)} %copy-done.2, f32[392,128]{1,0:T(8,128)S(1)} %get-tuple-element.31.refs_3_, f32[392,128]{1,0:T(8,128)S(1)} %collective-permute-done.2.refs_4_, ...), custom_call_target="tpu_custom_call" | custom-call | flops 8000000 | bytes 10000000 | tf_op jit(solution)/shard_map/taylor_step/pallas_call | solution.py:346
  62.5 3.2 %collective-permute-start.6 = (f32[392,128]{1,0:T(8,128)S(1)}, f32[392,128]{1,0:T(8,128)S(1)}, u32[]{:S(2)}, u32[]{:S(2)}) collective-permute-start(f32[392,128]{1,0:T(8,128)S(1)} %get-tuple-element.33.refs_3_), channel_id=1, source_target_pairs={{1,2},{3,4},{5,6},{2,1},{4,3},{6,5},{9,10},{11,12},{13,14},{10,9},... | collective-permute-start | bytes 602120 | tf_op jit(solution)/shard_map/ppermute | solution.py:307
  65.7 2.1 %collective-permute-start.7 = (f32[392,128]{1,0:T(8,128)S(1)}, f32[392,128]{1,0:T(8,128)S(1)}, u32[]{:S(2)}, u32[]{:S(2)}) collective-permute-start(f32[392,128]{1,0:T(8,128)S(1)} %get-tuple-element.33.refs_3_), channel_id=1, source_target_pairs={{0,1},{1,0},{2,3},{3,2},{4,5},{5,4},{6,7},{7,6},{8,9},{9,8},{10,11... | collective-permute-start | bytes 602120 | tf_op jit(solution)/shard_map/ppermute | solution.py:308
  67.8 0.0 collective-permute-done.12.refs_4_
  67.8 0.0 collective-permute-done.13.refs_5_
  67.8 2.4 %taylor_step.13 = (f32[392,128]{1,0:T(8,128)S(1)}, f32[384,128]{1,0:T(8,128)S(1)}) custom-call(s32[1]{0:T(128)} %bitcast.where.refs_0_, s32[8,32]{1,0:T(8,128)S(1)} %copy-done.1, s32[3,128]{1,0:T(4,128)S(1)} %copy-done.2, f32[392,128]{1,0:T(8,128)S(1)} %get-tuple-element.38.refs_3_, f32[392,128]{1,0:T(8,128)S(1)} %collective-permute-done.12.refs_4_, ...), custom_call_target="tpu_custom_call" | custom-call | flops 8000000 | bytes 10000000 | tf_op jit(solution)/shard_map/taylor_step/pallas_call | solution.py:346
  70.2 5.9 %collective-permute-start.14 = (f32[392,128]{1,0:T(8,128)S(1)}, f32[392,128]{1,0:T(8,128)S(1)}, u32[]{:S(2)}, u32[]{:S(2)}) collective-permute-start(f32[392,128]{1,0:T(8,128)S(1)} %get-tuple-element.41.refs_3_), channel_id=1, source_target_pairs={{1,2},{3,4},{5,6},{2,1},{4,3},{6,5},{9,10},{11,12},{13,14},{10,9},... | collective-permute-start | bytes 602120 | tf_op jit(solution)/shard_map/ppermute | solution.py:307
  76.1 1.9 %collective-permute-start.15 = (f32[392,128]{1,0:T(8,128)S(1)}, f32[392,128]{1,0:T(8,128)S(1)}, u32[]{:S(2)}, u32[]{:S(2)}) collective-permute-start(f32[392,128]{1,0:T(8,128)S(1)} %get-tuple-element.41.refs_3_), channel_id=1, source_target_pairs={{0,1},{1,0},{2,3},{3,2},{4,5},{5,4},{6,7},{7,6},{8,9},{9,8},{10,11... | collective-permute-start | bytes 602120 | tf_op jit(solution)/shard_map/ppermute | solution.py:308
  78.0 0.0 collective-permute-done.6.refs_4_
  78.1 0.0 collective-permute-done.7.refs_5_
  78.1 2.4 %taylor_step.12 = (f32[392,128]{1,0:T(8,128)S(1)}, f32[384,128]{1,0:T(8,128)S(1)}) custom-call(s32[1]{0:T(128)} %bitcast.where.refs_0_, s32[8,32]{1,0:T(8,128)S(1)} %copy-done.1, s32[3,128]{1,0:T(4,128)S(1)} %copy-done.2, f32[392,128]{1,0:T(8,128)S(1)} %get-tuple-element.33.refs_3_, f32[392,128]{1,0:T(8,128)S(1)} %collective-permute-done.6.refs_4_, ...), custom_call_target="tpu_custom_call" | custom-call | flops 8000000 | bytes 10000000 | tf_op jit(solution)/shard_map/taylor_step/pallas_call | solution.py:346
  80.5 2.7 %collective-permute-start.10 = (f32[392,128]{1,0:T(8,128)S(1)}, f32[392,128]{1,0:T(8,128)S(1)}, u32[]{:S(2)}, u32[]{:S(2)}) collective-permute-start(f32[392,128]{1,0:T(8,128)S(1)} %get-tuple-element.37.refs_3_), channel_id=1, source_target_pairs={{1,2},{3,4},{5,6},{2,1},{4,3},{6,5},{9,10},{11,12},{13,14},{10,9},... | collective-permute-start | bytes 602120 | tf_op jit(solution)/shard_map/ppermute | solution.py:307
  83.2 1.9 %collective-permute-start.11 = (f32[392,128]{1,0:T(8,128)S(1)}, f32[392,128]{1,0:T(8,128)S(1)}, u32[]{:S(2)}, u32[]{:S(2)}) collective-permute-start(f32[392,128]{1,0:T(8,128)S(1)} %get-tuple-element.37.refs_3_), channel_id=1, source_target_pairs={{0,1},{1,0},{2,3},{3,2},{4,5},{5,4},{6,7},{7,6},{8,9},{9,8},{10,11... | collective-permute-start | bytes 602120 | tf_op jit(solution)/shard_map/ppermute | solution.py:308
  85.1 0.0 collective-permute-done.16
  85.1 0.2 copy_add_fusion
  85.3 0.0 collective-permute-done.14.refs_4_
  85.3 0.0 collective-permute-done.15.refs_5_
  85.3 1.8 %taylor_step.14.refs_10_ = f32[384,128]{1,0:T(8,128)S(1)} custom-call(s32[1]{0:T(128)} %bitcast.where.refs_0_, s32[8,32]{1,0:T(8,128)S(1)} %copy-done.1, s32[3,128]{1,0:T(4,128)S(1)} %copy-done.2, f32[392,128]{1,0:T(8,128)S(1)} %get-tuple-element.41.refs_3_, f32[392,128]{1,0:T(8,128)S(1)} %collective-permute-done.14.refs_4_, ...), custom_call_target="tpu_custom_call" | custom-call | flops 8000000 | bytes 10000000 | tf_op jit(solution)/shard_map/taylor_step/pallas_call | solution.py:346
  87.2 2.1 %collective-permute-done.10.refs_4_ = f32[392,128]{1,0:T(8,128)S(1)} collective-permute-done((f32[392,128]{1,0:T(8,128)S(1)}, f32[392,128]{1,0:T(8,128)S(1)}, u32[]{:S(2)}, u32[]{:S(2)}) %collective-permute-start.10) | collective-permute-done | bytes 200736 | tf_op jit(solution)/shard_map/ppermute | solution.py:307
  89.3 0.0 collective-permute-done.11.refs_5_
  89.3 2.6 %taylor_step.15 = (f32[2,384,128]{2,1,0:T(8,128)}, f32[4,96,128]{2,1,0:T(8,128)S(1)}) custom-call(s32[1]{0:T(128)} %bitcast.where.refs_0_, s32[8,32]{1,0:T(8,128)S(1)} %copy-done.1, s32[3,128]{1,0:T(4,128)S(1)} %copy-done.2, f32[392,128]{1,0:T(8,128)S(1)} %get-tuple-element.37.refs_3_, f32[392,128]{1,0:T(8,128)S(1)} %collective-permute-done.10.refs_4_, ...), custom_call_target="tpu_custom_call" | custom-call | flops 8000000 | bytes 10000000 | tf_op jit(solution)/shard_map/taylor_step/pallas_call | solution.py:346
  91.9 0.1 copy.12
  92.1 0.1 maximum_bitcast_fusion
  92.2 36.0 %all_to_all.5.got = f32[96,10,128]{2,1,0:T(8,128)S(1)} all-to-all(f32[96,10,128]{2,1,0:T(8,128)S(1)} %maximum_bitcast_fusion), channel_id=1, replica_groups=mesh['orb'=96,'dom'=8] {'orb'}, dimensions={0} | all-to-all | bytes 983040 | tf_op jit(solution)/shard_map/all_to_all | solution.py:382
  128.2 0.7 sum_over_orb.1
  (1 shorter events, 0.0 us)
Async XLA Ops:
  0.6 0.7 copy-start.1
  0.6 0.7 copy-start.2
  0.7 0.7 copy-start.5
  1.3 1.0 copy-start
  2.3 0.7 copy-start.4
  3.0 14.4 %copy-start.3 = (f32[4,96,128]{2,1,0:T(8,128)S(1)}, f32[4,96,128]{2,1,0:T(8,128)}, u32[]{:S(2)}) copy-start(f32[4,96,128]{2,1,0:T(8,128)} %potential.1) | copy-start | bytes 589828
  4.3 13.1 %copy-start.6 = (f32[3]{0:T(128)S(1)}, f32[3]{0:T(128)}, u32[]{:S(2)}) copy-start(f32[3]{0:T(128)} %laser.1) | copy-start | bytes 40
  4.3 23.3 %collective-permute-start.4 = (f32[392,128]{1,0:T(8,128)S(1)}, f32[392,128]{1,0:T(8,128)S(1)}, u32[]{:S(2)}, u32[]{:S(2)}) collective-permute-start(f32[392,128]{1,0:T(8,128)S(1)} %get-tuple-element.30.refs_9_.refs_3_.real), channel_id=1, source_target_pairs={{1,2},{3,4},{5,6},{2,1},{4,3},{6,5},{9,10},{11,12},{13,14},{10,9},... | collective-permute-start | bytes 602120 | tf_op jit(solution)/shard_map/ppermute | solution.py:307
  13.4 14.3 %collective-permute-start.5 = (f32[392,128]{1,0:T(8,128)S(1)}, f32[392,128]{1,0:T(8,128)S(1)}, u32[]{:S(2)}, u32[]{:S(2)}) collective-permute-start(f32[392,128]{1,0:T(8,128)S(1)} %get-tuple-element.30.refs_9_.refs_3_.real), channel_id=1, source_target_pairs={{0,1},{1,0},{2,3},{3,2},{4,5},{5,4},{6,7},{7,6},{8,9},{9,8},{10,11... | collective-permute-start | bytes 602120 | tf_op jit(solution)/shard_map/ppermute | solution.py:308
  18.7 19.2 %collective-permute-start = (f32[392,128]{1,0:T(8,128)S(1)}, f32[392,128]{1,0:T(8,128)S(1)}, u32[]{:S(2)}, u32[]{:S(2)}) collective-permute-start(f32[392,128]{1,0:T(8,128)S(1)} %get-tuple-element.27.refs_3_.refs_9_.imag), channel_id=1, source_target_pairs={{1,2},{3,4},{5,6},{2,1},{4,3},{6,5},{9,10},{11,12},{13,14},{10,9},... | collective-permute-start | bytes 602120 | tf_op jit(solution)/shard_map/ppermute | solution.py:307
  25.8 12.2 %collective-permute-start.1 = (f32[392,128]{1,0:T(8,128)S(1)}, f32[392,128]{1,0:T(8,128)S(1)}, u32[]{:S(2)}, u32[]{:S(2)}) collective-permute-start(f32[392,128]{1,0:T(8,128)S(1)} %get-tuple-element.27.refs_3_.refs_9_.imag), channel_id=1, source_target_pairs={{0,1},{1,0},{2,3},{3,2},{4,5},{5,4},{6,7},{7,6},{8,9},{9,8},{10,11... | collective-permute-start | bytes 602120 | tf_op jit(solution)/shard_map/ppermute | solution.py:308
  30.1 19.4 %collective-permute-start.8 = (f32[392,128]{1,0:T(8,128)S(1)}, f32[392,128]{1,0:T(8,128)S(1)}, u32[]{:S(2)}, u32[]{:S(2)}) collective-permute-start(f32[392,128]{1,0:T(8,128)S(1)} %get-tuple-element.34.refs_3_), channel_id=1, source_target_pairs={{1,2},{3,4},{5,6},{2,1},{4,3},{6,5},{9,10},{11,12},{13,14},{10,9},... | collective-permute-start | bytes 602120 | tf_op jit(solution)/shard_map/ppermute | solution.py:307
  36.0 13.5 %collective-permute-start.9 = (f32[392,128]{1,0:T(8,128)S(1)}, f32[392,128]{1,0:T(8,128)S(1)}, u32[]{:S(2)}, u32[]{:S(2)}) collective-permute-start(f32[392,128]{1,0:T(8,128)S(1)} %get-tuple-element.34.refs_3_), channel_id=1, source_target_pairs={{0,1},{1,0},{2,3},{3,2},{4,5},{5,4},{6,7},{7,6},{8,9},{9,8},{10,11... | collective-permute-start | bytes 602120 | tf_op jit(solution)/shard_map/ppermute | solution.py:308
  40.4 19.7 %collective-permute-start.2 = (f32[392,128]{1,0:T(8,128)S(1)}, f32[392,128]{1,0:T(8,128)S(1)}, u32[]{:S(2)}, u32[]{:S(2)}) collective-permute-start(f32[392,128]{1,0:T(8,128)S(1)} %get-tuple-element.31.refs_3_), channel_id=1, source_target_pairs={{1,2},{3,4},{5,6},{2,1},{4,3},{6,5},{9,10},{11,12},{13,14},{10,9},... | collective-permute-start | bytes 602120 | tf_op jit(solution)/shard_map/ppermute | solution.py:307
  43.0 17.1 %collective-permute-start.3 = (f32[392,128]{1,0:T(8,128)S(1)}, f32[392,128]{1,0:T(8,128)S(1)}, u32[]{:S(2)}, u32[]{:S(2)}) collective-permute-start(f32[392,128]{1,0:T(8,128)S(1)} %get-tuple-element.31.refs_3_), channel_id=1, source_target_pairs={{0,1},{1,0},{2,3},{3,2},{4,5},{5,4},{6,7},{7,6},{8,9},{9,8},{10,11... | collective-permute-start | bytes 602120 | tf_op jit(solution)/shard_map/ppermute | solution.py:308
  46.4 38.7 %collective-permute-start.16 = (f32[6,96,128]{2,0,1:T(8,128)S(1)}, f32[6,96,128]{2,0,1:T(8,128)S(1)}, u32[]{:S(2)}, u32[]{:S(2)}) collective-permute-start(f32[6,96,128]{2,0,1:T(8,128)S(1)} %copy.10), channel_id=1, source_target_pairs={{0,24},{8,32},{16,40},{24,0},{32,8},{40,16},{48,72},{56,80},{64,88... | collective-permute-start | bytes 884744 | tf_op jit(solution)/shard_map/ppermute | solution.py:368
  52.0 15.8 %collective-permute-start.12 = (f32[392,128]{1,0:T(8,128)S(1)}, f32[392,128]{1,0:T(8,128)S(1)}, u32[]{:S(2)}, u32[]{:S(2)}) collective-permute-start(f32[392,128]{1,0:T(8,128)S(1)} %get-tuple-element.38.refs_3_), channel_id=1, source_target_pairs={{1,2},{3,4},{5,6},{2,1},{4,3},{6,5},{9,10},{11,12},{13,14},{10,9},... | collective-permute-start | bytes 602120 | tf_op jit(solution)/shard_map/ppermute | solution.py:307
  58.2 9.7 %collective-permute-start.13 = (f32[392,128]{1,0:T(8,128)S(1)}, f32[392,128]{1,0:T(8,128)S(1)}, u32[]{:S(2)}, u32[]{:S(2)}) collective-permute-start(f32[392,128]{1,0:T(8,128)S(1)} %get-tuple-element.38.refs_3_), channel_id=1, source_target_pairs={{0,1},{1,0},{2,3},{3,2},{4,5},{5,4},{6,7},{7,6},{8,9},{9,8},{10,11... | collective-permute-start | bytes 602120 | tf_op jit(solution)/shard_map/ppermute | solution.py:308
  62.5 15.5 %collective-permute-start.6 = (f32[392,128]{1,0:T(8,128)S(1)}, f32[392,128]{1,0:T(8,128)S(1)}, u32[]{:S(2)}, u32[]{:S(2)}) collective-permute-start(f32[392,128]{1,0:T(8,128)S(1)} %get-tuple-element.33.refs_3_), channel_id=1, source_target_pairs={{1,2},{3,4},{5,6},{2,1},{4,3},{6,5},{9,10},{11,12},{13,14},{10,9},... | collective-permute-start | bytes 602120 | tf_op jit(solution)/shard_map/ppermute | solution.py:307
  65.7 12.4 %collective-permute-start.7 = (f32[392,128]{1,0:T(8,128)S(1)}, f32[392,128]{1,0:T(8,128)S(1)}, u32[]{:S(2)}, u32[]{:S(2)}) collective-permute-start(f32[392,128]{1,0:T(8,128)S(1)} %get-tuple-element.33.refs_3_), channel_id=1, source_target_pairs={{0,1},{1,0},{2,3},{3,2},{4,5},{5,4},{6,7},{7,6},{8,9},{9,8},{10,11... | collective-permute-start | bytes 602120 | tf_op jit(solution)/shard_map/ppermute | solution.py:308
  70.2 15.1 %collective-permute-start.14 = (f32[392,128]{1,0:T(8,128)S(1)}, f32[392,128]{1,0:T(8,128)S(1)}, u32[]{:S(2)}, u32[]{:S(2)}) collective-permute-start(f32[392,128]{1,0:T(8,128)S(1)} %get-tuple-element.41.refs_3_), channel_id=1, source_target_pairs={{1,2},{3,4},{5,6},{2,1},{4,3},{6,5},{9,10},{11,12},{13,14},{10,9},... | collective-permute-start | bytes 602120 | tf_op jit(solution)/shard_map/ppermute | solution.py:307
  76.1 9.2 %collective-permute-start.15 = (f32[392,128]{1,0:T(8,128)S(1)}, f32[392,128]{1,0:T(8,128)S(1)}, u32[]{:S(2)}, u32[]{:S(2)}) collective-permute-start(f32[392,128]{1,0:T(8,128)S(1)} %get-tuple-element.41.refs_3_), channel_id=1, source_target_pairs={{0,1},{1,0},{2,3},{3,2},{4,5},{5,4},{6,7},{7,6},{8,9},{9,8},{10,11... | collective-permute-start | bytes 602120 | tf_op jit(solution)/shard_map/ppermute | solution.py:308
  80.5 8.8 %collective-permute-start.10 = (f32[392,128]{1,0:T(8,128)S(1)}, f32[392,128]{1,0:T(8,128)S(1)}, u32[]{:S(2)}, u32[]{:S(2)}) collective-permute-start(f32[392,128]{1,0:T(8,128)S(1)} %get-tuple-element.37.refs_3_), channel_id=1, source_target_pairs={{1,2},{3,4},{5,6},{2,1},{4,3},{6,5},{9,10},{11,12},{13,14},{10,9},... | collective-permute-start | bytes 602120 | tf_op jit(solution)/shard_map/ppermute | solution.py:307
  83.2 6.1 %collective-permute-start.11 = (f32[392,128]{1,0:T(8,128)S(1)}, f32[392,128]{1,0:T(8,128)S(1)}, u32[]{:S(2)}, u32[]{:S(2)}) collective-permute-start(f32[392,128]{1,0:T(8,128)S(1)} %get-tuple-element.37.refs_3_), channel_id=1, source_target_pairs={{0,1},{1,0},{2,3},{3,2},{4,5},{5,4},{6,7},{7,6},{8,9},{9,8},{10,11... | collective-permute-start | bytes 602120 | tf_op jit(solution)/shard_map/ppermute | solution.py:308

commit v6 on v4

--- a/solution.py
+++ b/solution.py
@@ -22,7 +22,6 @@
 
 VMEM = pl.BlockSpec(memory_space=pltpu.VMEM)
 SMEM = pl.BlockSpec(memory_space=pltpu.SMEM)
-FAR = pl.BlockSpec(memory_space=pltpu.HBM)
 
 
 def f32(*shape):
@@ -108,15 +107,11 @@
 
 
 def prepare_kernel(
-    planes, rows, slots, where, atoms, anchor, strength, projector_far, u,
-    proj, weight, message, sums, projector, sems,
+    planes, rows, slots, where, atoms, anchor, strength, projector, u,
+    proj, weight, message, sums,
 ):
     cells = u.shape[-1]
     size = planes * rows
-    fetch = pltpu.make_async_copy(u.at[0], message.at[0:size], sems.at[0])
-    fetch_projector = pltpu.make_async_copy(projector_far, projector, sems.at[1])
-    fetch.start()
-    fetch_projector.start()
     me = where[0]
     behind = jnp.maximum(me - 1, 0)
     lane = lax.broadcasted_iota(jnp.int32, (8, cells), 1)
@@ -132,7 +127,6 @@
         strengths = jnp.where((lane % PROJ) == p, strength[p], strengths)
     weight[...] = listed * strengths
 
-    fetch_projector.wait()
     for chunk in range(BOX**3 // cells):
         block = projector[:, chunk * cells : (chunk + 1) * cells]
         for part in range(cells // BOX):
@@ -142,33 +136,54 @@
             for p in range(PROJ):
                 proj[p * BOX + i, j : j + 1, :] = moved[p : p + 1]
 
-    fetch.wait()
-    message[size : size + 8, :] = partial_sums(planes, rows, slots, me, atoms, anchor, message, proj, sums)
+    message[0:size, :] = u[0]
+    message[size : size + 8, :] = partial_sums(planes, rows, slots, me, atoms, anchor, u.at[0], proj, sums)
 
 
 def second_kernel(
-    planes, rows, slots, domains, where, atoms, anchor, laser, potential, proj, u, v, message, sums, sem
+    planes, rows, slots, domains, where, atoms, anchor, laser, potential, proj, u, v, message, sums
 ):
     cells = u.shape[-1]
     size = planes * rows
     me = where[0]
-    fetch = pltpu.make_async_copy(u.at[1], message.at[0:size], sem)
-    fetch.start()
     y = lax.broadcasted_iota(jnp.int32, (rows, cells), 0).astype(jnp.float32)
     z = lax.broadcasted_iota(jnp.int32, (rows, cells), 1).astype(jnp.float32)
     along = laser[1] * ((y - (rows - 1) / 2.0) * spacing) + laser[2] * ((z - (cells - 1) / 2.0) * spacing)
     for i in range(planes):
         x = ((me * planes + i).astype(jnp.float32) - (domains * planes - 1) / 2.0) * spacing
         v[i] = potential[i] + laser[0] * x + along + 3.0 * kinetic[0]
-    fetch.wait()
-    message[size : size + 8, :] = partial_sums(planes, rows, slots, me, atoms, anchor, message, proj, sums)
+    message[0:size, :] = u[1]
+    message[size : size + 8, :] = partial_sums(planes, rows, slots, me, atoms, anchor, u.at[1], proj, sums)
+
+
+def local_part(planes, rows, i, u, v, padded):
+    def plane_of(j):
+        return u[j * rows : (j + 1) * rows, :]
+
+    centre = plane_of(i)
+    total = v[i] * centre
+    for m in (1, 2, 3, 4):
+        near = padded[i, 8 + m : 8 + m + rows, :] + padded[i, 8 - m : 8 - m + rows, :]
+        near = near + shifted(centre, m) + shifted(centre, -m)
+        if i + m < planes:
+            near = near + plane_of(i + m)
+        if i >= m:
+            near = near + plane_of(i - m)
+        total = total + kinetic[m] * near
+    return total
+
+
+def local_kernel(planes, rows, u, v, local, padded):
+    fill_padded(padded, planes, rows, lambda i: u[i * rows : (i + 1) * rows, :])
+    for i in range(planes):
+        local[i * rows : (i + 1) * rows, :] = local_part(planes, rows, i, u, v, padded)
 
 
 def step_kernel(planes, rows, slots, factor, last, scale, *refs):
     where, atoms, anchor, u, other_u, pair_u, v, weight, proj, evolved, *refs = refs
     size = planes * rows
     if last == "both":
-        held, result, density, acc, padded, spread, sums = refs
+        held, local, result, density, acc, padded, spread, sums = refs
     elif last:
         result, acc, padded, spread, sums = refs
     else:
@@ -182,18 +197,10 @@
     def plane_of(ref, i):
         return ref[i * rows : (i + 1) * rows, :]
 
-    fill_padded(padded, planes, rows, lambda i: plane_of(u, i))
-    for i in range(planes):
-        centre = plane_of(u, i)
-        total = v[i] * centre
-        for m in (1, 2, 3, 4):
-            near = padded[i, 8 + m : 8 + m + rows, :] + padded[i, 8 - m : 8 - m + rows, :]
-            near = near + shifted(centre, m) + shifted(centre, -m)
-            if i + m < planes:
-                near = near + plane_of(u, i + m)
-            if i >= m:
-                near = near + plane_of(u, i - m)
-            total = total + kinetic[m] * near
+    if last != "both":
+        fill_padded(padded, planes, rows, lambda i: plane_of(u, i))
+    for i in range(planes):
+        total = plane_of(local, i) if last == "both" else local_part(planes, rows, i, u, v, padded)
         for j in range(planes):
             total = total + pair_w[i, j] * plane_of(pair_u, j) + other_w[i, j] * plane_of(other_u, j)
         acc[i * rows : (i + 1) * rows, :] = total
@@ -327,11 +334,11 @@
         other = lax.ppermute(value, "dom", others)
         return other, lax.ppermute(value, "dom", pairs)
 
-    def kernel(function, name, out, scalars, arrays, scratch, far=0):
+    def kernel(function, name, out, scalars, arrays, scratch):
         return pl.pallas_call(
             function,
             out_shape=out,
-            in_specs=[SMEM] * scalars + [VMEM] * arrays + [FAR] * far,
+            in_specs=[SMEM] * scalars + [VMEM] * arrays,
             out_specs=jax.tree.map(lambda _: VMEM, out),
             scratch_shapes=scratch,
             compiler_params=pltpu.CompilerParams(vmem_limit_bytes=32 * 1024 * 1024),
@@ -345,15 +352,13 @@
         functools.partial(prepare_kernel, planes, rows, slots),
         "prepare_real",
         (f32(PROJ * BOX, BOX, cells), f32(8, cells), f32(size + 8, cells)),
-        4, 0,
-        [sums, pltpu.VMEM((PROJ, BOX**3), jnp.float32), pltpu.SemaphoreType.DMA((2,))],
-        2,
+        4, 2, [sums],
     )(*places, strength, projector, u)
     v, second = kernel(
         functools.partial(second_kernel, planes, rows, slots, domains),
         "prepare_imag",
         (f32(planes, rows, cells), f32(size + 8, cells)),
-        4, 2, [sums, pltpu.SemaphoreType.DMA], 1,
+        4, 3, [sums],
     )(*places, laser_field, potential, proj, u)
 
     def step(order, channel, halos, evolved, held=None):
@@ -364,13 +369,19 @@
             out = (f32(size + 8, cells),) + out
         if last == "both":
             out = (f32(2, size, cells), f32(planes, rows, cells))
-        extra = () if held is None else (held,)
+        padded = pltpu.VMEM((planes, rows + 16, cells), jnp.float32)
+        extra = ()
+        if held is not None:
+            local = kernel(
+                functools.partial(local_kernel, planes, rows), "local_part", f32(size, cells), 0, 2, [padded]
+            )(halos[0], v)
+            extra = (held, local)
         return kernel(
             functools.partial(step_kernel, planes, rows, slots, sign * time_step / order, last, scale),
             "taylor_step", out, 3, 7 + len(extra),
             [
                 pltpu.VMEM((size, cells), jnp.float32),
-                pltpu.VMEM((planes, rows + 16, cells), jnp.float32),
+                padded,
                 pltpu.VMEM((2 * slots * PROJ, cells), jnp.float32),
                 sums,
             ],

time: 125 us -> 124 us (level); the launches traced: 124 us -> 122 us
  blocking collectives: 28.3 us -> 26.7 us
    all_to_all x1, blocking collectives: 28.3 us -> 26.7 us  [body(): fields = lax.all_to_all(fields, 'orb', 0, 0, tiled=True)]
where the time goes in v6:
time: 124 us; the launch traced here: 122 us
  starting transfers between devices  67.8 us (55%)
  blocking collectives  26.7 us (22%)
  Pallas kernels  23.2 us (19%)
  local copies, waits for them, and re-layouts  2.61 us (2%)
    ppermute x8, starting transfers between devices, exchange(): other = lax.ppermute(value, 'dom', others)  42.7 us
    all_to_all x1, blocking collectives, body(): fields = lax.all_to_all(fields, 'orb', 0, 0, tiled=True)  26.7 us
    pallas_call x8, Pallas kernels, step(): kernel(functools.partial(step_kernel, planes, rows, slots, sign * time_st...  18.3 us
    ppermute x8, starting transfers between devices, exchange(): return (other, lax.ppermute(value, 'dom', pairs))  17.5 us
    ppermute x1, starting transfers between devices, body(): lax.ppermute(send, 'orb', [(i, (i // RUN ^ 2) * RUN + i % RUN) for i in r...  4.36 us
    ppermute x1, starting transfers between devices, body(): lax.ppermute(send, 'orb', [(i, (i // RUN ^ 1) * RUN + i % RUN) for i in r...  3.12 us
  transfers between devices with their start and end apart: 18, of which 1 were waited for; matrix products, arithmetic and copies ran while one was open for 0% of the time, Pallas kernels for 17%

profile of v6, /device:TPU:1, one launch (start us, length us, event | category | flops | bytes accessed | tf_op | source)
XLA Modules:
  0.0 121.9 jit_solution(16199129922917403968)
XLA Ops:
  0.6 0.0 copy-start.1
  0.6 0.0 copy-start.2
  0.7 0.0 copy-start.5
  0.7 0.7 copy-done.1
  1.3 0.0 copy-done.2
  1.3 0.0 copy-done.5
  1.3 1.0 copy-done
  2.3 0.7 copy-done.4
  3.0 1.3 %prepare_real.1 = (f32[32,8,128]{2,1,0:T(8,128)S(1)}, f32[8,128]{1,0:T(8,128)S(1)}, f32[392,128]{1,0:T(8,128)S(1)}) custom-call(s32[1]{0:T(128)} %bitcast.where.refs_0_, s32[8,32]{1,0:T(8,128)S(1)} %copy-done.1, s32[3,128]{1,0:T(4,128)S(1)} %copy-done.2, f32[4]{0:T(128)S(1)} %copy-done.5, f32[4,512]{1,0:T(4,128)S(1)} %copy-done.4, f32[2,384,128]{2,1,0:T(8,128)S(1)} %bitcast.8), custom_call_target="tpu_custom_call" | custom-call | flops 8000000 | bytes 10000000 | tf_op jit(solution)/shard_map/prepare_real/pallas_call | solution.py:351
  4.3 9.0 %collective-permute-start.4 = (f32[392,128]{1,0:T(8,128)S(1)}, f32[392,128]{1,0:T(8,128)S(1)}, u32[]{:S(2)}, u32[]{:S(2)}) collective-permute-start(f32[392,128]{1,0:T(8,128)S(1)} %get-tuple-element.36.refs_9_.refs_3_.real), channel_id=1, source_target_pairs={{1,2},{3,4},{5,6},{2,1},{4,3},{6,5},{9,10},{11,12},{13,14},{10,9},... | collective-permute-start | bytes 602120 | tf_op jit(solution)/shard_map/ppermute | solution.py:334
  13.4 4.1 %collective-permute-start.5 = (f32[392,128]{1,0:T(8,128)S(1)}, f32[392,128]{1,0:T(8,128)S(1)}, u32[]{:S(2)}, u32[]{:S(2)}) collective-permute-start(f32[392,128]{1,0:T(8,128)S(1)} %get-tuple-element.36.refs_9_.refs_3_.real), channel_id=1, source_target_pairs={{0,1},{1,0},{2,3},{3,2},{4,5},{5,4},{6,7},{7,6},{8,9},{9,8},{10,11... | collective-permute-start | bytes 602120 | tf_op jit(solution)/shard_map/ppermute | solution.py:335
  17.5 0.0 copy-done.3
  17.5 0.0 copy-done.6
  17.5 1.2 %prepare_imag.1 = (f32[4,96,128]{2,1,0:T(8,128)S(1)}, f32[392,128]{1,0:T(8,128)S(1)}) custom-call(s32[1]{0:T(128)} %bitcast.where.refs_0_, s32[8,32]{1,0:T(8,128)S(1)} %copy-done.1, s32[3,128]{1,0:T(4,128)S(1)} %copy-done.2, f32[3]{0:T(128)S(1)} %copy-done.6, f32[4,96,128]{2,1,0:T(8,128)S(1)} %copy-done.3, f32[32,8,128]{2,1,0:T(8,128)S(1)} %get-tuple-element.32.proj.refs_8_, ...), custom_call_target="tpu_custom_call" | custom-call | flops 8000000 | bytes 10000000 | tf_op jit(solution)/shard_map/prepare_imag/pallas_call | solution.py:357
  18.7 7.0 %collective-permute-start = (f32[392,128]{1,0:T(8,128)S(1)}, f32[392,128]{1,0:T(8,128)S(1)}, u32[]{:S(2)}, u32[]{:S(2)}) collective-permute-start(f32[392,128]{1,0:T(8,128)S(1)} %get-tuple-element.33.refs_3_.refs_9_.imag), channel_id=1, source_target_pairs={{1,2},{3,4},{5,6},{2,1},{4,3},{6,5},{9,10},{11,12},{13,14},{10,9},... | collective-permute-start | bytes 602120 | tf_op jit(solution)/shard_map/ppermute | solution.py:334
  25.8 1.9 %collective-permute-start.1 = (f32[392,128]{1,0:T(8,128)S(1)}, f32[392,128]{1,0:T(8,128)S(1)}, u32[]{:S(2)}, u32[]{:S(2)}) collective-permute-start(f32[392,128]{1,0:T(8,128)S(1)} %get-tuple-element.33.refs_3_.refs_9_.imag), channel_id=1, source_target_pairs={{0,1},{1,0},{2,3},{3,2},{4,5},{5,4},{6,7},{7,6},{8,9},{9,8},{10,11... | collective-permute-start | bytes 602120 | tf_op jit(solution)/shard_map/ppermute | solution.py:335
  27.7 0.0 collective-permute-done.4.refs_4_.real_other
  27.7 0.0 collective-permute-done.5.refs_5_.real_pair
  27.7 2.4 %taylor_step.9 = (f32[392,128]{1,0:T(8,128)S(1)}, f32[384,128]{1,0:T(8,128)S(1)}) custom-call(s32[1]{0:T(128)} %bitcast.where.refs_0_, s32[8,32]{1,0:T(8,128)S(1)} %copy-done.1, s32[3,128]{1,0:T(4,128)S(1)} %copy-done.2, f32[392,128]{1,0:T(8,128)S(1)} %get-tuple-element.36.refs_9_.refs_3_.real, f32[392,128]{1,0:T(8,128)S(1)} %collective-permute-done.4.refs_4_.real_other, ...), custom_call_target="tpu_custom_call" | custom-call | flops 8000000 | bytes 10000000 | tf_op jit(solution)/shard_map/taylor_step/pallas_call | solution.py:379
  30.1 5.9 %collective-permute-start.8 = (f32[392,128]{1,0:T(8,128)S(1)}, f32[392,128]{1,0:T(8,128)S(1)}, u32[]{:S(2)}, u32[]{:S(2)}) collective-permute-start(f32[392,128]{1,0:T(8,128)S(1)} %get-tuple-element.40.refs_3_), channel_id=1, source_target_pairs={{1,2},{3,4},{5,6},{2,1},{4,3},{6,5},{9,10},{11,12},{13,14},{10,9},... | collective-permute-start | bytes 602120 | tf_op jit(solution)/shard_map/ppermute | solution.py:334
  36.0 1.9 %collective-permute-start.9 = (f32[392,128]{1,0:T(8,128)S(1)}, f32[392,128]{1,0:T(8,128)S(1)}, u32[]{:S(2)}, u32[]{:S(2)}) collective-permute-start(f32[392,128]{1,0:T(8,128)S(1)} %get-tuple-element.40.refs_3_), channel_id=1, source_target_pairs={{0,1},{1,0},{2,3},{3,2},{4,5},{5,4},{6,7},{7,6},{8,9},{9,8},{10,11... | collective-permute-start | bytes 602120 | tf_op jit(solution)/shard_map/ppermute | solution.py:335
  37.9 0.0 collective-permute-done.refs_4_.imag_other
  37.9 0.0 collective-permute-done.1.refs_5_.imag_pair
  37.9 2.4 %taylor_step.8 = (f32[392,128]{1,0:T(8,128)S(1)}, f32[384,128]{1,0:T(8,128)S(1)}) custom-call(s32[1]{0:T(128)} %bitcast.where.refs_0_, s32[8,32]{1,0:T(8,128)S(1)} %copy-done.1, s32[3,128]{1,0:T(4,128)S(1)} %copy-done.2, f32[392,128]{1,0:T(8,128)S(1)} %get-tuple-element.33.refs_3_.refs_9_.imag, f32[392,128]{1,0:T(8,128)S(1)} %collective-permute-done.refs_4_.imag_other, ...), custom_call_target="tpu_custom_call" | custom-call | flops 8000000 | bytes 10000000 | tf_op jit(solution)/shard_map/taylor_step/pallas_call | solution.py:379
  40.3 2.7 %collective-permute-start.2 = (f32[392,128]{1,0:T(8,128)S(1)}, f32[392,128]{1,0:T(8,128)S(1)}, u32[]{:S(2)}, u32[]{:S(2)}) collective-permute-start(f32[392,128]{1,0:T(8,128)S(1)} %get-tuple-element.37.refs_3_), channel_id=1, source_target_pairs={{1,2},{3,4},{5,6},{2,1},{4,3},{6,5},{9,10},{11,12},{13,14},{10,9},... | collective-permute-start | bytes 602120 | tf_op jit(solution)/shard_map/ppermute | solution.py:334
  43.0 1.9 %collective-permute-start.3 = (f32[392,128]{1,0:T(8,128)S(1)}, f32[392,128]{1,0:T(8,128)S(1)}, u32[]{:S(2)}, u32[]{:S(2)}) collective-permute-start(f32[392,128]{1,0:T(8,128)S(1)} %get-tuple-element.37.refs_3_), channel_id=1, source_target_pairs={{0,1},{1,0},{2,3},{3,2},{4,5},{5,4},{6,7},{7,6},{8,9},{9,8},{10,11... | collective-permute-start | bytes 602120 | tf_op jit(solution)/shard_map/ppermute | solution.py:335
  45.0 0.0 collective-permute-done.8.refs_4_
  45.0 1.2 current_part.1
  46.2 3.1 %collective-permute-start.16 = (f32[6,96,128]{2,1,0:T(8,128)S(1)}, f32[6,96,128]{2,1,0:T(8,128)S(1)}, u32[]{:S(2)}, u32[]{:S(2)}) collective-permute-start(f32[6,96,128]{2,1,0:T(8,128)S(1)} %get-tuple-element.56), channel_id=1, source_target_pairs={{0,24},{8,32},{16,40},{24,0},{32,8},{40,16},{48,72},{56,80},{64,88... | collective-permute-start | bytes 884744 | tf_op jit(solution)/shard_map/ppermute | solution.py:405
  49.3 0.0 collective-permute-done.9.refs_5_
  49.3 2.4 %taylor_step.11 = (f32[392,128]{1,0:T(8,128)S(1)}, f32[384,128]{1,0:T(8,128)S(1)}) custom-call(s32[1]{0:T(128)} %bitcast.where.refs_0_, s32[8,32]{1,0:T(8,128)S(1)} %copy-done.1, s32[3,128]{1,0:T(4,128)S(1)} %copy-done.2, f32[392,128]{1,0:T(8,128)S(1)} %get-tuple-element.40.refs_3_, f32[392,128]{1,0:T(8,128)S(1)} %collective-permute-done.8.refs_4_, ...), custom_call_target="tpu_custom_call" | custom-call | flops 8000000 | bytes 10000000 | tf_op jit(solution)/shard_map/taylor_step/pallas_call | solution.py:379
  51.8 6.2 %collective-permute-start.12 = (f32[392,128]{1,0:T(8,128)S(1)}, f32[392,128]{1,0:T(8,128)S(1)}, u32[]{:S(2)}, u32[]{:S(2)}) collective-permute-start(f32[392,128]{1,0:T(8,128)S(1)} %get-tuple-element.45.refs_3_), channel_id=1, source_target_pairs={{1,2},{3,4},{5,6},{2,1},{4,3},{6,5},{9,10},{11,12},{13,14},{10,9},... | collective-permute-start | bytes 602120 | tf_op jit(solution)/shard_map/ppermute | solution.py:334
  58.0 1.9 %collective-permute-start.13 = (f32[392,128]{1,0:T(8,128)S(1)}, f32[392,128]{1,0:T(8,128)S(1)}, u32[]{:S(2)}, u32[]{:S(2)}) collective-permute-start(f32[392,128]{1,0:T(8,128)S(1)} %get-tuple-element.45.refs_3_), channel_id=1, source_target_pairs={{0,1},{1,0},{2,3},{3,2},{4,5},{5,4},{6,7},{7,6},{8,9},{9,8},{10,11... | collective-permute-start | bytes 602120 | tf_op jit(solution)/shard_map/ppermute | solution.py:335
  59.9 0.0 collective-permute-done.2.refs_4_
  59.9 0.0 collective-permute-done.3.refs_5_
  59.9 2.4 %taylor_step.10 = (f32[392,128]{1,0:T(8,128)S(1)}, f32[384,128]{1,0:T(8,128)S(1)}) custom-call(s32[1]{0:T(128)} %bitcast.where.refs_0_, s32[8,32]{1,0:T(8,128)S(1)} %copy-done.1, s32[3,128]{1,0:T(4,128)S(1)} %copy-done.2, f32[392,128]{1,0:T(8,128)S(1)} %get-tuple-element.37.refs_3_, f32[392,128]{1,0:T(8,128)S(1)} %collective-permute-done.2.refs_4_, ...), custom_call_target="tpu_custom_call" | custom-call | flops 8000000 | bytes 10000000 | tf_op jit(solution)/shard_map/taylor_step/pallas_call | solution.py:379
  62.3 3.2 %collective-permute-start.6 = (f32[392,128]{1,0:T(8,128)S(1)}, f32[392,128]{1,0:T(8,128)S(1)}, u32[]{:S(2)}, u32[]{:S(2)}) collective-permute-start(f32[392,128]{1,0:T(8,128)S(1)} %get-tuple-element.39.refs_3_), channel_id=1, source_target_pairs={{1,2},{3,4},{5,6},{2,1},{4,3},{6,5},{9,10},{11,12},{13,14},{10,9},... | collective-permute-start | bytes 602120 | tf_op jit(solution)/shard_map/ppermute | solution.py:334
  65.5 1.9 %collective-permute-start.7 = (f32[392,128]{1,0:T(8,128)S(1)}, f32[392,128]{1,0:T(8,128)S(1)}, u32[]{:S(2)}, u32[]{:S(2)}) collective-permute-start(f32[392,128]{1,0:T(8,128)S(1)} %get-tuple-element.39.refs_3_), channel_id=1, source_target_pairs={{0,1},{1,0},{2,3},{3,2},{4,5},{5,4},{6,7},{7,6},{8,9},{9,8},{10,11... | collective-permute-start | bytes 602120 | tf_op jit(solution)/shard_map/ppermute | solution.py:335
  67.4 0.0 collective-permute-done.12.refs_4_
  67.4 0.0 collective-permute-done.13.refs_5_
  67.4 2.4 %taylor_step.13 = (f32[392,128]{1,0:T(8,128)S(1)}, f32[384,128]{1,0:T(8,128)S(1)}) custom-call(s32[1]{0:T(128)} %bitcast.where.refs_0_, s32[8,32]{1,0:T(8,128)S(1)} %copy-done.1, s32[3,128]{1,0:T(4,128)S(1)} %copy-done.2, f32[392,128]{1,0:T(8,128)S(1)} %get-tuple-element.45.refs_3_, f32[392,128]{1,0:T(8,128)S(1)} %collective-permute-done.12.refs_4_, ...), custom_call_target="tpu_custom_call" | custom-call | flops 8000000 | bytes 10000000 | tf_op jit(solution)/shard_map/taylor_step/pallas_call | solution.py:379
  69.8 6.1 %collective-permute-start.14 = (f32[392,128]{1,0:T(8,128)S(1)}, f32[392,128]{1,0:T(8,128)S(1)}, u32[]{:S(2)}, u32[]{:S(2)}) collective-permute-start(f32[392,128]{1,0:T(8,128)S(1)} %get-tuple-element.50.refs_3_), channel_id=1, source_target_pairs={{1,2},{3,4},{5,6},{2,1},{4,3},{6,5},{9,10},{11,12},{13,14},{10,9},... | collective-permute-start | bytes 602120 | tf_op jit(solution)/shard_map/ppermute | solution.py:334
  75.9 1.9 %collective-permute-start.15 = (f32[392,128]{1,0:T(8,128)S(1)}, f32[392,128]{1,0:T(8,128)S(1)}, u32[]{:S(2)}, u32[]{:S(2)}) collective-permute-start(f32[392,128]{1,0:T(8,128)S(1)} %get-tuple-element.50.refs_3_), channel_id=1, source_target_pairs={{0,1},{1,0},{2,3},{3,2},{4,5},{5,4},{6,7},{7,6},{8,9},{9,8},{10,11... | collective-permute-start | bytes 602120 | tf_op jit(solution)/shard_map/ppermute | solution.py:335
  77.8 0.0 collective-permute-done.6.refs_4_
  77.8 0.0 collective-permute-done.7.refs_5_
  77.8 2.4 %taylor_step.12 = (f32[392,128]{1,0:T(8,128)S(1)}, f32[384,128]{1,0:T(8,128)S(1)}) custom-call(s32[1]{0:T(128)} %bitcast.where.refs_0_, s32[8,32]{1,0:T(8,128)S(1)} %copy-done.1, s32[3,128]{1,0:T(4,128)S(1)} %copy-done.2, f32[392,128]{1,0:T(8,128)S(1)} %get-tuple-element.39.refs_3_, f32[392,128]{1,0:T(8,128)S(1)} %collective-permute-done.6.refs_4_, ...), custom_call_target="tpu_custom_call" | custom-call | flops 8000000 | bytes 10000000 | tf_op jit(solution)/shard_map/taylor_step/pallas_call | solution.py:379
  80.2 2.7 %collective-permute-start.10 = (f32[392,128]{1,0:T(8,128)S(1)}, f32[392,128]{1,0:T(8,128)S(1)}, u32[]{:S(2)}, u32[]{:S(2)}) collective-permute-start(f32[392,128]{1,0:T(8,128)S(1)} %get-tuple-element.44.u.refs_3_), channel_id=1, source_target_pairs={{1,2},{3,4},{5,6},{2,1},{4,3},{6,5},{9,10},{11,12},{13,14},{10,9},... | collective-permute-start | bytes 602120 | tf_op jit(solution)/shard_map/ppermute | solution.py:334
  82.9 1.9 %collective-permute-start.11 = (f32[392,128]{1,0:T(8,128)S(1)}, f32[392,128]{1,0:T(8,128)S(1)}, u32[]{:S(2)}, u32[]{:S(2)}) collective-permute-start(f32[392,128]{1,0:T(8,128)S(1)} %get-tuple-element.44.u.refs_3_), channel_id=1, source_target_pairs={{0,1},{1,0},{2,3},{3,2},{4,5},{5,4},{6,7},{7,6},{8,9},{9,8},{10,11... | collective-permute-start | bytes 602120 | tf_op jit(solution)/shard_map/ppermute | solution.py:335
  84.9 0.0 collective-permute-done.16.got
  84.9 0.1 copy.10
  85.0 4.4 %collective-permute-start.17 = (f32[3,96,128]{2,0,1:T(4,128)S(1)}, f32[3,96,128]{2,0,1:T(4,128)S(1)}, u32[]{:S(2)}, u32[]{:S(2)}) collective-permute-start(f32[3,96,128]{2,0,1:T(4,128)S(1)} %copy.10), channel_id=1, source_target_pairs={{0,48},{8,56},{16,64},{24,72},{32,80},{40,88},{48,0},{56,8},{64,16... | collective-permute-start | bytes 442376 | tf_op jit(solution)/shard_map/ppermute | solution.py:411
  89.4 0.5 local_part.1.refs_11_
  89.9 0.0 collective-permute-done.14.refs_4_
  89.9 0.0 collective-permute-done.15.refs_5_
  89.9 1.8 %taylor_step.14.refs_10_ = f32[384,128]{1,0:T(8,128)S(1)} custom-call(s32[1]{0:T(128)} %bitcast.where.refs_0_, s32[8,32]{1,0:T(8,128)S(1)} %copy-done.1, s32[3,128]{1,0:T(4,128)S(1)} %copy-done.2, f32[392,128]{1,0:T(8,128)S(1)} %get-tuple-element.50.refs_3_, f32[392,128]{1,0:T(8,128)S(1)} %collective-permute-done.14.refs_4_, ...), custom_call_target="tpu_custom_call" | custom-call | flops 8000000 | bytes 10000000 | tf_op jit(solution)/shard_map/taylor_step/pallas_call | solution.py:379
  91.8 0.0 collective-permute-done.10.refs_4_
  91.8 0.0 collective-permute-done.11.refs_5_
  91.8 2.1 %taylor_step.15 = (f32[2,384,128]{2,1,0:T(8,128)}, f32[4,96,128]{2,1,0:T(8,128)S(1)}) custom-call(s32[1]{0:T(128)} %bitcast.where.refs_0_, s32[8,32]{1,0:T(8,128)S(1)} %copy-done.1, s32[3,128]{1,0:T(4,128)S(1)} %copy-done.2, f32[392,128]{1,0:T(8,128)S(1)} %get-tuple-element.44.u.refs_3_, f32[392,128]{1,0:T(8,128)S(1)} %collective-permute-done.10.refs_4_, ...), custom_call_target="tpu_custom_call" | custom-call | flops 8000000 | bytes 10000000 | tf_op jit(solution)/shard_map/taylor_step/pallas_call | solution.py:379
  93.9 0.1 copy.12
  94.1 0.3 collective-permute-done.17
  94.4 0.1 copy_add_fusion
  94.5 0.1 maximum_bitcast_fusion
  94.6 26.7 %all_to_all.5.got = f32[96,7,128]{2,1,0:T(8,128)S(1)} all-to-all(f32[96,7,128]{2,1,0:T(8,128)S(1)} %maximum_bitcast_fusion), channel_id=1, replica_groups=mesh['orb'=96,'dom'=8] {'orb'}, dimensions={0} | all-to-all | bytes 688128 | tf_op jit(solution)/shard_map/all_to_all | solution.py:423
  121.3 0.6 sum_over_orb.1
  (5 shorter events, 0.0 us)
Async XLA Ops:
  0.6 0.7 copy-start.1
  0.6 0.7 copy-start.2
  0.7 0.7 copy-start.5
  1.3 1.0 copy-start
  2.3 0.7 copy-start.4
  3.0 14.4 %copy-start.3 = (f32[4,96,128]{2,1,0:T(8,128)S(1)}, f32[4,96,128]{2,1,0:T(8,128)}, u32[]{:S(2)}) copy-start(f32[4,96,128]{2,1,0:T(8,128)} %potential.1) | copy-start | bytes 589828
  4.3 13.1 %copy-start.6 = (f32[3]{0:T(128)S(1)}, f32[3]{0:T(128)}, u32[]{:S(2)}) copy-start(f32[3]{0:T(128)} %laser.1) | copy-start | bytes 40
  4.3 23.4 %collective-permute-start.4 = (f32[392,128]{1,0:T(8,128)S(1)}, f32[392,128]{1,0:T(8,128)S(1)}, u32[]{:S(2)}, u32[]{:S(2)}) collective-permute-start(f32[392,128]{1,0:T(8,128)S(1)} %get-tuple-element.36.refs_9_.refs_3_.real), channel_id=1, source_target_pairs={{1,2},{3,4},{5,6},{2,1},{4,3},{6,5},{9,10},{11,12},{13,14},{10,9},... | collective-permute-start | bytes 602120 | tf_op jit(solution)/shard_map/ppermute | solution.py:334
  13.4 14.3 %collective-permute-start.5 = (f32[392,128]{1,0:T(8,128)S(1)}, f32[392,128]{1,0:T(8,128)S(1)}, u32[]{:S(2)}, u32[]{:S(2)}) collective-permute-start(f32[392,128]{1,0:T(8,128)S(1)} %get-tuple-element.36.refs_9_.refs_3_.real), channel_id=1, source_target_pairs={{0,1},{1,0},{2,3},{3,2},{4,5},{5,4},{6,7},{7,6},{8,9},{9,8},{10,11... | collective-permute-start | bytes 602120 | tf_op jit(solution)/shard_map/ppermute | solution.py:335
  18.7 19.2 %collective-permute-start = (f32[392,128]{1,0:T(8,128)S(1)}, f32[392,128]{1,0:T(8,128)S(1)}, u32[]{:S(2)}, u32[]{:S(2)}) collective-permute-start(f32[392,128]{1,0:T(8,128)S(1)} %get-tuple-element.33.refs_3_.refs_9_.imag), channel_id=1, source_target_pairs={{1,2},{3,4},{5,6},{2,1},{4,3},{6,5},{9,10},{11,12},{13,14},{10,9},... | collective-permute-start | bytes 602120 | tf_op jit(solution)/shard_map/ppermute | solution.py:334
  25.8 12.2 %collective-permute-start.1 = (f32[392,128]{1,0:T(8,128)S(1)}, f32[392,128]{1,0:T(8,128)S(1)}, u32[]{:S(2)}, u32[]{:S(2)}) collective-permute-start(f32[392,128]{1,0:T(8,128)S(1)} %get-tuple-element.33.refs_3_.refs_9_.imag), channel_id=1, source_target_pairs={{0,1},{1,0},{2,3},{3,2},{4,5},{5,4},{6,7},{7,6},{8,9},{9,8},{10,11... | collective-permute-start | bytes 602120 | tf_op jit(solution)/shard_map/ppermute | solution.py:335
  30.1 14.9 %collective-permute-start.8 = (f32[392,128]{1,0:T(8,128)S(1)}, f32[392,128]{1,0:T(8,128)S(1)}, u32[]{:S(2)}, u32[]{:S(2)}) collective-permute-start(f32[392,128]{1,0:T(8,128)S(1)} %get-tuple-element.40.refs_3_), channel_id=1, source_target_pairs={{1,2},{3,4},{5,6},{2,1},{4,3},{6,5},{9,10},{11,12},{13,14},{10,9},... | collective-permute-start | bytes 602120 | tf_op jit(solution)/shard_map/ppermute | solution.py:334
  36.0 13.3 %collective-permute-start.9 = (f32[392,128]{1,0:T(8,128)S(1)}, f32[392,128]{1,0:T(8,128)S(1)}, u32[]{:S(2)}, u32[]{:S(2)}) collective-permute-start(f32[392,128]{1,0:T(8,128)S(1)} %get-tuple-element.40.refs_3_), channel_id=1, source_target_pairs={{0,1},{1,0},{2,3},{3,2},{4,5},{5,4},{6,7},{7,6},{8,9},{9,8},{10,11... | collective-permute-start | bytes 602120 | tf_op jit(solution)/shard_map/ppermute | solution.py:335
  40.3 19.5 %collective-permute-start.2 = (f32[392,128]{1,0:T(8,128)S(1)}, f32[392,128]{1,0:T(8,128)S(1)}, u32[]{:S(2)}, u32[]{:S(2)}) collective-permute-start(f32[392,128]{1,0:T(8,128)S(1)} %get-tuple-element.37.refs_3_), channel_id=1, source_target_pairs={{1,2},{3,4},{5,6},{2,1},{4,3},{6,5},{9,10},{11,12},{13,14},{10,9},... | collective-permute-start | bytes 602120 | tf_op jit(solution)/shard_map/ppermute | solution.py:334
  43.0 16.9 %collective-permute-start.3 = (f32[392,128]{1,0:T(8,128)S(1)}, f32[392,128]{1,0:T(8,128)S(1)}, u32[]{:S(2)}, u32[]{:S(2)}) collective-permute-start(f32[392,128]{1,0:T(8,128)S(1)} %get-tuple-element.37.refs_3_), channel_id=1, source_target_pairs={{0,1},{1,0},{2,3},{3,2},{4,5},{5,4},{6,7},{7,6},{8,9},{9,8},{10,11... | collective-permute-start | bytes 602120 | tf_op jit(solution)/shard_map/ppermute | solution.py:335
  46.2 38.7 %collective-permute-start.16 = (f32[6,96,128]{2,1,0:T(8,128)S(1)}, f32[6,96,128]{2,1,0:T(8,128)S(1)}, u32[]{:S(2)}, u32[]{:S(2)}) collective-permute-start(f32[6,96,128]{2,1,0:T(8,128)S(1)} %get-tuple-element.56), channel_id=1, source_target_pairs={{0,24},{8,32},{16,40},{24,0},{32,8},{40,16},{48,72},{56,80},{64,88... | collective-permute-start | bytes 884744 | tf_op jit(solution)/shard_map/ppermute | solution.py:405
  51.8 15.7 %collective-permute-start.12 = (f32[392,128]{1,0:T(8,128)S(1)}, f32[392,128]{1,0:T(8,128)S(1)}, u32[]{:S(2)}, u32[]{:S(2)}) collective-permute-start(f32[392,128]{1,0:T(8,128)S(1)} %get-tuple-element.45.refs_3_), channel_id=1, source_target_pairs={{1,2},{3,4},{5,6},{2,1},{4,3},{6,5},{9,10},{11,12},{13,14},{10,9},... | collective-permute-start | bytes 602120 | tf_op jit(solution)/shard_map/ppermute | solution.py:334
  58.0 9.5 %collective-permute-start.13 = (f32[392,128]{1,0:T(8,128)S(1)}, f32[392,128]{1,0:T(8,128)S(1)}, u32[]{:S(2)}, u32[]{:S(2)}) collective-permute-start(f32[392,128]{1,0:T(8,128)S(1)} %get-tuple-element.45.refs_3_), channel_id=1, source_target_pairs={{0,1},{1,0},{2,3},{3,2},{4,5},{5,4},{6,7},{7,6},{8,9},{9,8},{10,11... | collective-permute-start | bytes 602120 | tf_op jit(solution)/shard_map/ppermute | solution.py:335
  62.3 15.5 %collective-permute-start.6 = (f32[392,128]{1,0:T(8,128)S(1)}, f32[392,128]{1,0:T(8,128)S(1)}, u32[]{:S(2)}, u32[]{:S(2)}) collective-permute-start(f32[392,128]{1,0:T(8,128)S(1)} %get-tuple-element.39.refs_3_), channel_id=1, source_target_pairs={{1,2},{3,4},{5,6},{2,1},{4,3},{6,5},{9,10},{11,12},{13,14},{10,9},... | collective-permute-start | bytes 602120 | tf_op jit(solution)/shard_map/ppermute | solution.py:334
  65.5 12.3 %collective-permute-start.7 = (f32[392,128]{1,0:T(8,128)S(1)}, f32[392,128]{1,0:T(8,128)S(1)}, u32[]{:S(2)}, u32[]{:S(2)}) collective-permute-start(f32[392,128]{1,0:T(8,128)S(1)} %get-tuple-element.39.refs_3_), channel_id=1, source_target_pairs={{0,1},{1,0},{2,3},{3,2},{4,5},{5,4},{6,7},{7,6},{8,9},{9,8},{10,11... | collective-permute-start | bytes 602120 | tf_op jit(solution)/shard_map/ppermute | solution.py:335
  69.8 20.1 %collective-permute-start.14 = (f32[392,128]{1,0:T(8,128)S(1)}, f32[392,128]{1,0:T(8,128)S(1)}, u32[]{:S(2)}, u32[]{:S(2)}) collective-permute-start(f32[392,128]{1,0:T(8,128)S(1)} %get-tuple-element.50.refs_3_), channel_id=1, source_target_pairs={{1,2},{3,4},{5,6},{2,1},{4,3},{6,5},{9,10},{11,12},{13,14},{10,9},... | collective-permute-start | bytes 602120 | tf_op jit(solution)/shard_map/ppermute | solution.py:334
  75.9 14.0 %collective-permute-start.15 = (f32[392,128]{1,0:T(8,128)S(1)}, f32[392,128]{1,0:T(8,128)S(1)}, u32[]{:S(2)}, u32[]{:S(2)}) collective-permute-start(f32[392,128]{1,0:T(8,128)S(1)} %get-tuple-element.50.refs_3_), channel_id=1, source_target_pairs={{0,1},{1,0},{2,3},{3,2},{4,5},{5,4},{6,7},{7,6},{8,9},{9,8},{10,11... | collective-permute-start | bytes 602120 | tf_op jit(solution)/shard_map/ppermute | solution.py:335
  80.2 11.5 %collective-permute-start.10 = (f32[392,128]{1,0:T(8,128)S(1)}, f32[392,128]{1,0:T(8,128)S(1)}, u32[]{:S(2)}, u32[]{:S(2)}) collective-permute-start(f32[392,128]{1,0:T(8,128)S(1)} %get-tuple-element.44.u.refs_3_), channel_id=1, source_target_pairs={{1,2},{3,4},{5,6},{2,1},{4,3},{6,5},{9,10},{11,12},{13,14},{10,9},... | collective-permute-start | bytes 602120 | tf_op jit(solution)/shard_map/ppermute | solution.py:334
  82.9 8.9 %collective-permute-start.11 = (f32[392,128]{1,0:T(8,128)S(1)}, f32[392,128]{1,0:T(8,128)S(1)}, u32[]{:S(2)}, u32[]{:S(2)}) collective-permute-start(f32[392,128]{1,0:T(8,128)S(1)} %get-tuple-element.44.u.refs_3_), channel_id=1, source_target_pairs={{0,1},{1,0},{2,3},{3,2},{4,5},{5,4},{6,7},{7,6},{8,9},{9,8},{10,11... | collective-permute-start | bytes 602120 | tf_op jit(solution)/shard_map/ppermute | solution.py:335
  85.0 9.4 %collective-permute-start.17 = (f32[3,96,128]{2,0,1:T(4,128)S(1)}, f32[3,96,128]{2,0,1:T(4,128)S(1)}, u32[]{:S(2)}, u32[]{:S(2)}) collective-permute-start(f32[3,96,128]{2,0,1:T(4,128)S(1)} %copy.10), channel_id=1, source_target_pairs={{0,48},{8,56},{16,64},{24,72},{32,80},{40,88},{48,0},{56,8},{64,16... | collective-permute-start | bytes 442376 | tf_op jit(solution)/shard_map/ppermute | solution.py:411
